TPU v7x, 256 devices: a whole 4x4x8 slice. The times are simulated.
256 devices in a mesh: ctx: 32 (over y, z), tp: 8 (over x, core).
Axes of the slice: x: 4, y: 4, z: 8, core: 2. Of those that a mesh axis runs over, the one named last changes fastest.
Arguments:
- hidden_in: bfloat16 [4096, 5120], P('ctx', 'tp'), may hold values from -60 to 60
- norm_gain: bfloat16 [5120], P('tp'), may hold values from 0.099609375 to 1.8984375
- out_grad: bfloat16 [4096, 5120], P('ctx', 'tp'), may hold values from -6 to 6
- router_score: bfloat16 [4096], P('ctx'), may hold values from 0.19921875 to 1.5
- expert_ids: int32 [4096, 1], P('ctx'), may hold values from 0 to 7; in each aligned block of 128 rows (0 to 127, 128 to 255, ...) at most 24 rows name the same one
- gate_saved: bfloat16 [32, 2048, 768], P('ctx', 'tp'), may hold values from -6 to 6
- up_saved: bfloat16 [32, 2048, 768], P('ctx', 'tp'), may hold values from -6 to 6
- w_gate: bfloat16 [32, 5120, 2048], P('ctx', 'tp'), may hold values from -0.078125 to 0.078125
- w_up: bfloat16 [32, 5120, 2048], P('ctx', 'tp'), may hold values from -0.078125 to 0.078125
- w_down: bfloat16 [32, 2048, 5120], P('ctx', None, 'tp'), may hold values from -0.0625 to 0.0625
- w_out: bfloat16 [5120, 5120], P('tp', 'ctx'), may hold values from -0.078125 to 0.078125
- queries: bfloat16 [4096, 5120], P('ctx', 'tp'), may hold values from -18 to 18
- keys: bfloat16 [4096, 1024], P('ctx', 'tp'), may hold values from -18 to 18
- values: bfloat16 [4096, 1024], P('ctx', 'tp'), may hold values from -6 to 6
Outputs:
- d_hidden: bfloat16 [4096, 5120], P('ctx', 'tp')
- router_grad: float32 [4096], P('ctx')
- query_grad: bfloat16 [4096, 5120], P('ctx', 'tp')
- key_grad: bfloat16 [4096, 1024], P('ctx', 'tp')
- value_grad: bfloat16 [4096, 1024], P('ctx', 'tp')
Inputs may be any that keep to these rules, and one draw needn't show every extreme that they name: `expert_ids`: in the 128 tokens of one device no expert is named more than 24 times.
All inputs are finite; a program needn't handle non-finite values.
Results may differ from a plain program's by a relative error of at most 0.035.
Values may be sent and summed in bfloat16 or wider, within the bound.
A program may use at most 128 MiB of HBM per device.

v0:
```python
import jax
import jax.numpy as jnp
from jax import lax
from jax.sharding import PartitionSpec as P

D = 5120
QH = 40
KVH = 8
HD = 128
EXPERTS = 8


EPSILON = 1e-05
MASKED = -1e30


def silu_parts(gate_pre):
    sigmoid_val = jax.nn.sigmoid(gate_pre)
    return (gate_pre * sigmoid_val, sigmoid_val * (1.0 + gate_pre * (1.0 - sigmoid_val)))


def contract_last(left_mat, right_mat):
    return lax.dot_general(
        left_mat, right_mat, (((1,), (1,)), ((), ())), preferred_element_type=jnp.float32
    )


def contract_first(left_mat, right_mat):
    return lax.dot_general(
        left_mat, right_mat, (((0,), (1,)), ((), ())), preferred_element_type=jnp.float32
    )


def block_scores(query_grid, key_block, row_pos, key_pos, softmax_scale):
    scores = (
        jnp.einsum("rkgd,jkd->kgrj", query_grid, key_block, preferred_element_type=jnp.float32)
        * softmax_scale
    )
    allowed = key_pos[None, :] <= row_pos[:, None]
    return jnp.where(allowed[None, None, :, :], scores, MASKED)


def attend_group(
    query_grid, dout_grid, row_first, keys_all, values_all, key_accum, value_accum, block_len
):
    num_rows, kv_local, group_q, head_dim = query_grid.shape
    softmax_scale = head_dim ** (-0.5)
    row_pos = row_first + jnp.arange(num_rows, dtype=jnp.int32)
    num_blocks = (row_first + num_rows - 1) // block_len + 1

    def key_positions(block_index):
        return block_index * block_len + jnp.arange(block_len, dtype=jnp.int32)

    def fetch(source, block_index):
        return lax.dynamic_slice_in_dim(source, block_index * block_len, block_len, 0)

    def stats_step(block_index, state_now):
        row_max, row_sum = state_now
        scores = block_scores(
            query_grid,
            fetch(keys_all, block_index),
            row_pos,
            key_positions(block_index),
            softmax_scale,
        )
        new_max = jnp.maximum(row_max, jnp.max(scores, axis=3))
        row_sum = row_sum * jnp.exp(row_max - new_max) + jnp.sum(
            jnp.exp(scores - new_max[..., None]), axis=3
        )
        return (new_max, row_sum)

    stat_shape = (kv_local, group_q, num_rows)
    start_stats = (jnp.full(stat_shape, MASKED, jnp.float32), jnp.zeros(stat_shape, jnp.float32))
    row_max, row_sum = lax.fori_loop(0, num_blocks, stats_step, start_stats)
    log_total = row_max + jnp.log(row_sum)

    def probabilities(block_index):
        scores = block_scores(
            query_grid,
            fetch(keys_all, block_index),
            row_pos,
            key_positions(block_index),
            softmax_scale,
        )
        prob_full = jnp.exp(scores - log_total[..., None])
        dprob = jnp.einsum(
            "rkgd,jkd->kgrj",
            dout_grid,
            fetch(values_all, block_index),
            preferred_element_type=jnp.float32,
        )
        return (prob_full, dprob)

    def delta_step(block_index, delta_now):
        prob_full, dprob = probabilities(block_index)
        return delta_now + jnp.sum(prob_full * dprob, axis=3)

    delta_all = lax.fori_loop(0, num_blocks, delta_step, jnp.zeros(stat_shape, jnp.float32))

    def grad_step(block_index, state_now):
        query_acc, key_now, value_now = state_now
        prob_full, dprob = probabilities(block_index)
        dscore = (prob_full * (dprob - delta_all[..., None])).astype(jnp.bfloat16)
        key_block = fetch(keys_all, block_index)
        query_acc = query_acc + jnp.einsum(
            "kgrj,jkd->rkgd", dscore, key_block, preferred_element_type=jnp.float32
        )
        key_part = (
            jnp.einsum("kgrj,rkgd->jkd", dscore, query_grid, preferred_element_type=jnp.float32)
            * softmax_scale
        )
        value_part = jnp.einsum(
            "kgrj,rkgd->jkd",
            prob_full.astype(jnp.bfloat16),
            dout_grid,
            preferred_element_type=jnp.float32,
        )
        key_now = lax.dynamic_update_slice_in_dim(
            key_now, fetch(key_now, block_index) + key_part, block_index * block_len, 0
        )
        value_now = lax.dynamic_update_slice_in_dim(
            value_now, fetch(value_now, block_index) + value_part, block_index * block_len, 0
        )
        return (query_acc, key_now, value_now)

    start_grads = (jnp.zeros(query_grid.shape, jnp.float32), key_accum, value_accum)
    query_acc, key_accum, value_accum = lax.fori_loop(0, num_blocks, grad_step, start_grads)
    return (query_acc * softmax_scale, key_accum, value_accum)


def body(
    hidden_in,
    norm_gain,
    out_grad,
    router_score,
    expert_ids,
    gate_saved,
    up_saved,
    w_gate,
    w_up,
    w_down,
    w_out,
    queries,
    keys,
    values,
):
    devices = lax.axis_size("ctx")
    sharing = devices // EXPERTS
    tok_rows, feature_cols = out_grad.shape
    capacity = gate_saved.shape[2] // devices
    chosen = expert_ids[:, 0]
    onehot = (chosen[:, None] == jnp.arange(EXPERTS, dtype=jnp.int32)[None, :]).astype(jnp.int32)
    ranked = jnp.sum((jnp.cumsum(onehot, axis=0) - onehot) * onehot, axis=1)
    slot_index = chosen * capacity + ranked
    placing = (
        jnp.arange(EXPERTS * capacity, dtype=jnp.int32)[:, None] == slot_index[None, :]
    ).astype(jnp.bfloat16)
    grad_slots = jnp.dot(placing, out_grad, preferred_element_type=jnp.float32).astype(jnp.bfloat16)
    score_slots = jnp.dot(
        placing, router_score[:, None], preferred_element_type=jnp.float32
    ).astype(jnp.bfloat16)
    sent_grad = jnp.repeat(grad_slots.reshape(EXPERTS, capacity, feature_cols), sharing, axis=0)
    sent_score = jnp.repeat(score_slots.reshape(EXPERTS, capacity), sharing, axis=0)
    arrived, arrived_score = (
        lax.all_to_all(sent_grad, "ctx", split_axis=0, concat_axis=0, tiled=True),
        lax.all_to_all(sent_score, "ctx", split_axis=0, concat_axis=0, tiled=True),
    )
    slot_grad = arrived.reshape(devices * capacity, feature_cols)
    slot_score = arrived_score.reshape(devices * capacity).astype(jnp.float32)
    down_local = w_down[0]
    hidden_grad = lax.psum_scatter(
        contract_last(down_local, slot_grad).astype(jnp.bfloat16),
        "tp",
        scatter_dimension=0,
        tiled=True,
    ).astype(jnp.float32)
    gate_val = gate_saved[0].astype(jnp.float32)
    up_val = up_saved[0].astype(jnp.float32)
    activation, slope = silu_parts(gate_val)
    scaled = hidden_grad * slot_score[None, :]
    grad_gate = (scaled * up_val * slope).astype(jnp.bfloat16)
    grad_up = (scaled * activation).astype(jnp.bfloat16)
    router_part = jnp.sum(activation * up_val * hidden_grad, axis=0).astype(jnp.bfloat16)
    gate_local = w_gate[0]
    up_local = w_up[0]
    running = contract_first(lax.all_gather(grad_gate, "tp", axis=0, tiled=True), gate_local)
    back = running + contract_first(lax.all_gather(grad_up, "tp", axis=0, tiled=True), up_local)
    back_parts = back.astype(jnp.bfloat16).reshape(devices, capacity, feature_cols)
    returned, returned_router = (
        lax.all_to_all(back_parts, "ctx", split_axis=0, concat_axis=0, tiled=True),
        lax.all_to_all(
            router_part.reshape(devices, capacity), "ctx", split_axis=0, concat_axis=0, tiled=True
        ),
    )
    summed = jnp.sum(
        returned.astype(jnp.float32).reshape(EXPERTS, sharing, capacity, feature_cols), axis=1
    ).reshape(EXPERTS * capacity, feature_cols)
    router_sum = jnp.sum(
        returned_router.astype(jnp.float32).reshape(EXPERTS, sharing, capacity), axis=1
    ).reshape(EXPERTS * capacity)
    norm_grad = jnp.take(summed, slot_index, axis=0)
    router_tok = jnp.take(router_sum, slot_index, axis=0)
    hidden_val = hidden_in.astype(jnp.float32)
    gain_val = norm_gain.astype(jnp.float32)[None, :]
    squares_part = jnp.sum(hidden_val * hidden_val, axis=1)
    cross_part = jnp.sum(hidden_val * gain_val * norm_grad, axis=1)
    router_grad, sum_squares, cross_sum = lax.psum((router_tok, squares_part, cross_part), "tp")
    inverse_rms = lax.rsqrt(sum_squares / D + EPSILON)[:, None]
    d_hidden = (
        out_grad.astype(jnp.float32)
        + inverse_rms * gain_val * norm_grad
        - hidden_val * inverse_rms * inverse_rms * inverse_rms * cross_sum[:, None] / D
    ).astype(jnp.bfloat16)
    full_grad = lax.all_gather(d_hidden, "tp", axis=1, tiled=True)
    attn_grad = contract_last(full_grad, lax.all_gather(w_out, "ctx", axis=1, tiled=True))
    dout = attn_grad.astype(jnp.bfloat16)
    kv_local = keys.shape[1] // HD
    group_q = QH // KVH
    query_grid = queries.reshape(tok_rows, kv_local, group_q, HD)
    dout_grid = dout.reshape(tok_rows, kv_local, group_q, HD)
    keys_all, values_all = (
        lax.all_gather(keys, "ctx", axis=0, tiled=True),
        lax.all_gather(values, "ctx", axis=0, tiled=True),
    )
    total_rows = keys_all.shape[0]
    keys_all = keys_all.reshape(total_rows, kv_local, HD)
    values_all = values_all.reshape(total_rows, kv_local, HD)
    block_len = min(512, total_rows)
    key_accum = jnp.zeros((total_rows, kv_local, HD), jnp.float32)
    value_accum = jnp.zeros((total_rows, kv_local, HD), jnp.float32)
    position = lax.axis_index("ctx")
    query_acc, key_accum, value_accum = attend_group(
        query_grid,
        dout_grid,
        position * tok_rows,
        keys_all,
        values_all,
        key_accum,
        value_accum,
        block_len,
    )
    query_out = query_acc.astype(jnp.bfloat16)
    key_grad, value_grad = (
        lax.psum_scatter(
            key_accum.astype(jnp.bfloat16), "ctx", scatter_dimension=0, tiled=True
        ).astype(jnp.float32),
        lax.psum_scatter(
            value_accum.astype(jnp.bfloat16), "ctx", scatter_dimension=0, tiled=True
        ).astype(jnp.float32),
    )
    return (
        d_hidden,
        router_grad,
        query_out.reshape(tok_rows, kv_local * group_q * HD),
        key_grad.astype(jnp.bfloat16).reshape(tok_rows, kv_local * HD),
        value_grad.astype(jnp.bfloat16).reshape(tok_rows, kv_local * HD),
    )


def solution(mesh):
    in_specs = (
        P("ctx", "tp"),
        P("tp"),
        P("ctx", "tp"),
        P("ctx"),
        P("ctx", None),
        P("ctx", "tp", None),
        P("ctx", "tp", None),
        P("ctx", "tp", None),
        P("ctx", "tp", None),
        P("ctx", None, "tp"),
        P("tp", "ctx"),
        P("ctx", "tp"),
        P("ctx", "tp"),
        P("ctx", "tp"),
    )
    out_specs = (P("ctx", "tp"), P("ctx"), P("ctx", "tp"), P("ctx", "tp"), P("ctx", "tp"))
    return jax.shard_map(body, mesh=mesh, in_specs=in_specs, out_specs=out_specs, check_vma=False)
```

profile of v0, /device:TPU:88, one launch (start us, length us, event | category | flops | bytes accessed | tf_op | source)
XLA Modules:
  0.0 961.7 jit_solution(6375433308347410947)
XLA Ops:
  11.0 35.2 %all_to_all.25 = bf16[32,24,640]{2,1,0:T(8,128)(2,1)S(1)} all-to-all(bf16[32,24,640]{2,1,0:T(8,128)(2,1)S(1)} %bitcast.267), channel_id=1, replica_groups=mesh['ctx'=32,'tp'=8] {'ctx'}, dimensions={0} | all-to-all | bytes 1966080 | tf_op jit(solution)/shard_map/all_to_all | solution.py:165
  46.2 4.0 fusion.50
  51.8 7.5 all-to-all-start.1
  60.8 4.7 all-to-all-done.1
  65.6 21.9 %reduce-scatter.4.cloned.1.call-done = bf16[256,768]{0,1:T(8,128)(2,1)} async-done(((bf16[2048,768]{0,1:T(8,128)(2,1)}), bf16[256,768]{0,1:T(8,128)(2,1)}) %reduce-scatter.4.cloned.1.call-update) | async-done | bytes 393232 | tf_op jit(solution)/shard_map/reduce_scatter | solution.py:171
  92.6 10.1 %all-to-all-start.3 = ((bf16[32,1,24]{2,1,0:T(2,128)(2,1)}), bf16[32,1,24]{2,1,0:T(2,128)(2,1)S(1)}, u32[]{:S(2)}, u32[]{:S(2)}) async-start(bf16[32,1,24]{2,1,0:T(2,128)(2,1)} %convert_element_type.144), calls=%async_computation.4 | async-start | bytes 32768 | tf_op jit(solution)/shard_map/all_to_all | solution.py:191
  102.7 20.6 %all-gather.9.cloned.1.call-done = bf16[2048,768]{0,1:T(8,128)(2,1)} async-done(((bf16[256,768]{0,1:T(8,128)(2,1)}), bf16[2048,768]{0,1:T(8,128)(2,1)}) %all-gather.9.cloned.1.call-update) | async-done | bytes 3145744 | tf_op jit(solution)/shard_map/all_gather | solution.py:187
  123.3 6.6 fusion.51
  129.9 30.4 %all-gather.7.cloned.1.call-done = bf16[2048,768]{0,1:T(8,128)(2,1)} async-done(((bf16[256,768]{0,1:T(8,128)(2,1)}), bf16[2048,768]{0,1:T(8,128)(2,1)}) %all-gather.7.cloned.1.call-update) | async-done | bytes 3145744 | tf_op jit(solution)/shard_map/all_gather | solution.py:186
  160.4 6.8 add_convert_fusion
  167.2 10.2 %all-to-all-start.2 = ((bf16[32,24,640]{2,1,0:T(8,128)(2,1)}), bf16[32,24,640]{2,1,0:T(8,128)(2,1)}, u32[]{:S(2)}, u32[]{:S(2)}) async-start(bf16[32,24,640]{2,1,0:T(8,128)(2,1)} %bitcast.271), calls=%async_computation.3 | async-start | bytes 1966080 | tf_op jit(solution)/shard_map/all_to_all | solution.py:190
  178.9 24.8 %all-to-all-done.2 = bf16[32,24,640]{2,1,0:T(8,128)(2,1)} async-done(((bf16[32,24,640]{2,1,0:T(8,128)(2,1)}), bf16[32,24,640]{2,1,0:T(8,128)(2,1)}, u32[]{:S(2)}, u32[]{:S(2)}) %all-to-all-start.2) | async-done | bytes 983072 | tf_op jit(solution)/shard_map/all_to_all | solution.py:190
  207.1 13.3 %all-reduce = (f32[128]{0:T(128)S(1)}, f32[128]{0:T(128)S(1)}, f32[128]{0:T(128)}) all-reduce(f32[128]{0:T(128)S(1)} %get-tuple-element.352, f32[128]{0:T(128)S(1)} %get-tuple-element.351, f32[128]{0:T(128)S(1)} %broadcast_select_fusion), channel_id=1, replica_groups=mesh['ctx'=32,'tp'=8] {'tp'}, use_global_device_ids=true, to_apply=%region_7.8 | all-reduce | flops 384 | bytes 3072 | tf_op jit(solution)/shard_map/psum | solution.py:207
  224.4 15.4 %all-gather.11.cloned.1.call-done = bf16[4096,128]{1,0:T(8,128)(2,1)} async-done(((bf16[128,128]{1,0:T(8,128)(2,1)}), bf16[4096,128]{1,0:T(8,128)(2,1)}) %all-gather.11.cloned.1.call-update) | async-done | bytes 1048592 | tf_op jit(solution)/shard_map/all_gather | solution.py:222
  239.8 12.0 %while.39 = (s32[]{:T(128)}, f32[1,5,128]{2,1,0:T(8,128)S(1)}, f32[1,5,128]{2,1,0:T(8,128)S(1)}, s32[]{:T(128)}, bf16[4096,1,128]{2,0,1:T(8,128)(2,1)}, /*index=...) while((s32[]{:T(128)}, f32[1,5,128]{2,1,0:T(8,128)S(1)}, ...), condition=%wide.region_14.15_spmd.clone, body=%wide.region_11.14_spmd.clone.sunk | while | flops 85591944 | bytes 3085991 | solution.py:74
  251.9 77.2 %all-gather.17.cloned.1.call-done = bf16[640,5120]{0,1:T(8,128)(2,1)} async-done(((bf16[640,160]{0,1:T(8,128)(2,1)}), bf16[640,5120]{0,1:T(8,128)(2,1)}) %all-gather.17.cloned.1.call-update) | async-done | bytes 6553616 | tf_op jit(solution)/shard_map/all_gather | solution.py:215
  329.1 28.6 %all-gather.15.cloned.1.call-done = bf16[128,5120]{1,0:T(8,128)(2,1)} async-done(((bf16[128,640]{1,0:T(8,128)(2,1)}), bf16[128,5120]{1,0:T(8,128)(2,1)}) %all-gather.15.cloned.1.call-update) | async-done | bytes 1310736 | tf_op jit(solution)/shard_map/all_gather | solution.py:214
  357.7 4.5 convolution_convert_fusion.2
  362.5 71.8 %all-gather.13.cloned.1.call-done = bf16[4096,128]{1,0:T(8,128)(2,1)} async-done(((bf16[128,128]{1,0:T(8,128)(2,1)}), bf16[4096,128]{1,0:T(8,128)(2,1)}) %all-gather.13.cloned.1.call-update) | async-done | bytes 1048592 | tf_op jit(solution)/shard_map/all_gather | solution.py:223
  434.3 19.4 %while.40 = (s32[]{:T(128)}, f32[1,5,128]{2,1,0:T(8,128)S(1)}, s32[]{:T(128)}, bf16[4096,1,128]{2,0,1:T(8,128)(2,1)}, bf16[128,1,5,128]{3,0,2,1:T(8,128)(2,1)S(1...) while((s32[]{:T(128)}, f32[1,5,128]{2,1,0:T(8,128)S(1)}, ...), condition=%wide.region_17.18_spmd.clone, body=%wide.region_15.17_spmd.clone.sunk | while | flops 169476736 | bytes 3360443 | solution.py:98
  456.6 56.1 %while.41 = (s32[]{:T(128)}, f32[128,1,5,128]{0,3,2,1:T(8,128)S(1)}, f32[4096,1,128]{2,0,1:T(8,128)}, f32[4096,1,128]{2,0,1:T(8,128)}, s32[]{:T(128)}, /*index=5...) while((s32[]{:T(128)}, ...), condition=%wide.region_19.20_spmd.clone, body=%wide.region_18.19_spmd.clone.sunk | while | flops 422068864 | bytes 8792287 | solution.py:127
  515.4 2.7 convert_element_type.137
  519.0 219.2 %reduce-scatter.6.cloned.1.call-done = bf16[128,1,128]{2,0,1:T(8,128)(2,1)} async-done(((bf16[4096,1,128]{2,0,1:T(8,128)(2,1)}), bf16[128,1,128]{2,0,1:T(8,128)(2,1)}) %reduce-scatter.6.cloned.1.call-update) | async-done | bytes 32784 | tf_op jit(solution)/shard_map/reduce_scatter | solution.py:244
  738.1 217.0 %reduce-scatter.8.cloned.1.call-done = bf16[128,1,128]{2,0,1:T(8,128)(2,1)} async-done(((bf16[4096,1,128]{2,0,1:T(8,128)(2,1)}), bf16[128,1,128]{2,0,1:T(8,128)(2,1)}) %reduce-scatter.8.cloned.1.call-update) | async-done | bytes 32784 | tf_op jit(solution)/shard_map/reduce_scatter | solution.py:247
  (227 shorter events, 113.3 us)
Async XLA Ops:
  7.2 39.1 %copy-start = (bf16[1,2048,640]{2,1,0:T(8,128)(2,1)S(1)}, bf16[1,2048,640]{2,1,0:T(8,128)(2,1)}, u32[]{:S(2)}) copy-start(bf16[1,2048,640]{2,1,0:T(8,128)(2,1)} %param.29) | copy-start | bytes 7864324
  7.2 80.3 %reduce-scatter.4.cloned.1.call-start = ((), (), s32[]{:S(2)}) async-start(), calls=%async_computation.7 | async-start | bytes 3538944 | tf_op jit(solution)/shard_map/reduce_scatter | solution.py:171
  50.3 0.7 copy-start.4
  50.3 9.1 copy-start.1
  51.8 13.6 %all-to-all-start.1 = ((bf16[32,1,24]{2,1,0:T(2,128)(2,1)}), bf16[32,1,24]{2,1,0:T(2,128)(2,1)S(1)}, u32[]{:S(2)}, u32[]{:S(2)}) async-start(bf16[32,1,24]{2,1,0:T(2,128)(2,1)} %copy.53), calls=%async_computation.2 | async-start | bytes 32768 | tf_op jit(solution)/shard_map/all_to_all | solution.py:166
  59.3 64.0 %all-gather.9.cloned.1.call-start = ((), (), s32[]{:S(2)}) async-start(), calls=%async_computation.9 | async-start | bytes 3538944 | tf_op jit(solution)/shard_map/all_gather | solution.py:187
  90.0 70.4 %all-gather.7.cloned.1.call-start = ((), (), s32[]{:S(2)}) async-start(), calls=%async_computation.8 | async-start | bytes 3538944 | tf_op jit(solution)/shard_map/all_gather | solution.py:186
  90.7 149.1 %all-gather.11.cloned.1.call-start = ((), (), s32[]{:S(2)}) async-start(), calls=%async_computation.10 | async-start | bytes 1081344 | tf_op jit(solution)/shard_map/all_gather | solution.py:222
  91.3 237.8 %all-gather.17.cloned.1.call-start = ((), (), s32[]{:S(2)}) async-start(), calls=%async_computation.13 | async-start | bytes 6758400 | tf_op jit(solution)/shard_map/all_gather | solution.py:215
  92.6 74.6 %all-to-all-start.3 = ((bf16[32,1,24]{2,1,0:T(2,128)(2,1)}), bf16[32,1,24]{2,1,0:T(2,128)(2,1)S(1)}, u32[]{:S(2)}, u32[]{:S(2)}) async-start(bf16[32,1,24]{2,1,0:T(2,128)(2,1)} %convert_element_type.144), calls=%async_computation.4 | async-start | bytes 32768 | tf_op jit(solution)/shard_map/all_to_all | solution.py:191
  167.2 10.2 %copy-start.3 = (bf16[640]{0:T(1024)(128)(2,1)S(1)}, bf16[640]{0:T(1024)(128)(2,1)}, u32[]{:S(2)}) copy-start(bf16[640]{0:T(1024)(128)(2,1)} %param.21) | copy-start | bytes 3844
  167.2 10.3 %copy-start.2 = (s32[128,1]{0,1:T(1,128)S(1)}, s32[128,1]{0,1:T(1,128)}, u32[]{:S(2)}) copy-start(s32[128,1]{0,1:T(1,128)} %param.24) | copy-start | bytes 1540
  167.2 36.6 %all-to-all-start.2 = ((bf16[32,24,640]{2,1,0:T(8,128)(2,1)}), bf16[32,24,640]{2,1,0:T(8,128)(2,1)}, u32[]{:S(2)}, u32[]{:S(2)}) async-start(bf16[32,24,640]{2,1,0:T(8,128)(2,1)} %bitcast.271), calls=%async_computation.3 | async-start | bytes 1966080 | tf_op jit(solution)/shard_map/all_to_all | solution.py:190
  177.4 180.3 %all-gather.15.cloned.1.call-start = ((), (), s32[]{:S(2)}) async-start(), calls=%async_computation.12 | async-start | bytes 1474560 | tf_op jit(solution)/shard_map/all_gather | solution.py:214
  222.4 211.9 %all-gather.13.cloned.1.call-start = ((), (), s32[]{:S(2)}) async-start(), calls=%async_computation.11 | async-start | bytes 1081344 | tf_op jit(solution)/shard_map/all_gather | solution.py:223
  223.1 515.0 %reduce-scatter.6.cloned.1.call-start = ((), (), s32[]{:S(2)}) async-start(), calls=%async_computation.14 | async-start | bytes 1081344 | tf_op jit(solution)/shard_map/reduce_scatter | solution.py:244
  515.4 439.8 %reduce-scatter.8.cloned.1.call-start = ((), (), s32[]{:S(2)}) async-start(), calls=%async_computation.15 | async-start | bytes 1081344 | tf_op jit(solution)/shard_map/reduce_scatter | solution.py:247
Sparse Core Ops, SparseCore 0:
  50.4 37.0 reduce-scatter.3
  90.1 33.1 all-gather.8
  125.1 35.1 all-gather.6
  162.8 76.9 all-gather.10
  242.3 86.7 all-gather.16
  331.3 26.2 all-gather.14
  360.3 73.9 all-gather.12
  515.5 222.5 reduce-scatter.5
  742.5 212.5 reduce-scatter.7
where the time goes:
time: 967 us; the launch traced here: 962 us
  waiting for transfers between devices  734 us (76%)
  matrix products  105 us (11%)
  blocking collectives  48.6 us (5%)
  starting transfers between devices  28.1 us (3%)
  other arithmetic  19.4 us (2%)
  between operations  14.1 us (1%)
  local copies, waits for them, and re-layouts  11.1 us (1%)
    reduce_scatter x1, waiting for transfers between devices, body(): lax.psum_scatter(key_accum.astype(jnp.bfloat16), 'ctx', scatter_dimension...  219 us
    reduce_scatter x1, waiting for transfers between devices, body(): lax.psum_scatter(value_accum.astype(jnp.bfloat16), 'ctx', scatter_dimensi...  217 us
    all_gather x1, waiting for transfers between devices, body(): lax.all_gather(w_out, 'ctx', axis=1, tiled=True)  77.2 us
    all_gather x1, waiting for transfers between devices, body(): lax.all_gather(values, 'ctx', axis=0, tiled=True)  71.8 us
    all_to_all x1, blocking collectives, body(): lax.all_to_all(sent_grad, 'ctx', split_axis=0, concat_axis=0, tiled=True)  35.2 us
    all_gather x1, waiting for transfers between devices, body(): lax.all_gather(grad_gate, 'tp', axis=0, tiled=True)  30.4 us
    all_gather x1, waiting for transfers between devices, body(): full_grad = lax.all_gather(d_hidden, 'tp', axis=1, tiled=True)  28.6 us
    dot_general x21, matrix products, block_scores(): jnp.einsum('rkgd,jkd->kgrj', query_grid, key_block, preferred_element_typ...  26.9 us
  transfers between devices with their start and end apart: 12, of which 11 were waited for; matrix products, arithmetic and copies ran while one was open for 5% of the time, Pallas kernels for 0%

commit v1 on v0

v1 whole, which is shorter than its diff:
```python
import jax
import jax.numpy as jnp
from jax import lax
from jax.experimental import pallas as pl
from jax.experimental.pallas import tpu as pltpu
from jax.sharding import PartitionSpec as P

D = 5120
QH = 40
KVH = 8
HD = 128
EXPERTS = 8
GROUP_Q = QH // KVH
N_CTX = 32
BLOCK = 128
PAIR = 2 * BLOCK
ROWS_Q = GROUP_Q * BLOCK
W_ROWS = 160
MESH = pl.DeviceIdType.MESH
EPSILON = 1e-05
NEG = -1e30
LOG2E = 1.4426950408889634


def silu_parts(gate_pre):
    sigmoid_val = jax.nn.sigmoid(gate_pre)
    return (gate_pre * sigmoid_val, sigmoid_val * (1.0 + gate_pre * (1.0 - sigmoid_val)))


def contract_last(left_mat, right_mat):
    return lax.dot_general(
        left_mat, right_mat, (((1,), (1,)), ((), ())), preferred_element_type=jnp.float32
    )


def contract_first(left_mat, right_mat):
    return lax.dot_general(
        left_mat, right_mat, (((0,), (1,)), ((), ())), preferred_element_type=jnp.float32
    )


def mm(a, b):
    return jnp.dot(a, b, preferred_element_type=jnp.float32)


def attention_kernel(
    full_ref, q_ref, gathered_ref, dq_ref, dk_ref, dv_ref,
    w_buf, k_buf, v_buf, kt_buf, qt_buf, q5_buf, dt_buf, d5_buf,
    s_buf, dp_buf, p16_buf, ds16_buf, m_buf, l_buf, r_buf, dqt_buf,
    send_buf, recv_buf, w_sem, kv_sem, send_sem, recv_sem,
):
    me = lax.axis_index("ctx")
    tp = lax.axis_index("tp")
    scale = HD ** -0.5

    barrier = pltpu.get_barrier_semaphore()

    def greet(j, carry):
        pl.semaphore_signal(barrier, inc=1, device_id=(j, tp), device_id_type=MESH)
        return carry

    lax.fori_loop(me + 1, N_CTX, greet, 0)

    w_copy = pltpu.make_async_copy(gathered_ref.at[:, pl.ds(0, ROWS_Q)], w_buf, w_sem)

    def kv_copies(j):
        rows = pl.ds(pl.multiple_of(j * W_ROWS, 32), BLOCK)
        own = pl.ds(pl.multiple_of(j * BLOCK, BLOCK), BLOCK)
        return (
            pltpu.make_async_copy(
                gathered_ref.at[rows, pl.ds(ROWS_Q, HD)], k_buf.at[own], kv_sem.at[0, j]
            ),
            pltpu.make_async_copy(
                gathered_ref.at[rows, pl.ds(ROWS_Q + HD, HD)], v_buf.at[own], kv_sem.at[1, j]
            ),
        )

    def kv_start(j, carry):
        for copy in kv_copies(j):
            copy.start()
        return carry

    lax.fori_loop(0, N_CTX, kv_start, 0)
    w_copy.start()

    for h in range(GROUP_Q):
        cols = slice(h * BLOCK, (h + 1) * BLOCK)
        head = q_ref[:, cols]
        q5_buf[cols, :] = head
        qt_buf[:, cols] = head.astype(jnp.float32).T.astype(jnp.bfloat16)

    def kv_wait(j, carry):
        for copy in kv_copies(j):
            copy.wait()
        return carry

    lax.fori_loop(0, N_CTX, kv_wait, 0)

    last = me // 2
    m_buf[...] = jnp.full(m_buf.shape, NEG, jnp.float32)
    l_buf[...] = jnp.zeros_like(l_buf)
    r_buf[...] = jnp.zeros_like(r_buf)
    dqt_buf[...] = jnp.zeros_like(dqt_buf)

    def pair_rows(p):
        return pl.ds(pl.multiple_of(p * PAIR, PAIR), PAIR)

    def fold(x, op):
        total = x[0:8]
        for i in range(1, x.shape[0] // 8):
            total = op(total, x[8 * i : 8 * i + 8])
        return total

    def score_pass(p, masked):
        keys = k_buf[pair_rows(p), :]
        kt_buf[p] = keys.astype(jnp.float32).T.astype(jnp.bfloat16)
        for n in range(GROUP_Q):
            cols = slice(n * BLOCK, (n + 1) * BLOCK)
            part = mm(keys, qt_buf[:, cols])
            if masked:
                key_pos = lax.broadcasted_iota(jnp.int32, (PAIR, BLOCK), 0)
                row_pos = lax.broadcasted_iota(jnp.int32, (PAIR, BLOCK), 1)
                part = jnp.where(key_pos <= row_pos + (me % 2) * BLOCK, part, NEG)
            s_buf[p, :, cols] = part
            m_buf[:, cols] = jnp.maximum(m_buf[:, cols], fold(part, jnp.maximum))

    def score_step(p, carry):
        score_pass(p, False)
        return carry

    lax.fori_loop(0, last, score_step, 0)
    score_pass(last, True)
    row_max = jnp.max(m_buf[...], axis=0, keepdims=True)
    m_buf[...] = jnp.broadcast_to(row_max, m_buf.shape)

    w_copy.wait()
    dout = mm(full_ref[...], w_buf[...]).astype(jnp.bfloat16)
    for h in range(GROUP_Q):
        cols = slice(h * BLOCK, (h + 1) * BLOCK)
        head = dout[:, cols]
        d5_buf[cols, :] = head
        dt_buf[:, cols] = head.astype(jnp.float32).T.astype(jnp.bfloat16)

    step_rows = 32

    def prob_step(p, carry):
        vals = v_buf[pair_rows(p), :]
        dp_buf[p] = mm(vals, dt_buf[...])
        top = m_buf[0:1, :]
        l_now = l_buf[...]
        r_now = r_buf[...]
        for i in range(PAIR // step_rows):
            rows = slice(i * step_rows, (i + 1) * step_rows)
            e = jnp.exp2((s_buf[p, rows, :] - top) * (scale * LOG2E))
            s_buf[p, rows, :] = e
            l_now = l_now + fold(e, jnp.add)
            r_now = r_now + fold(e * dp_buf[p, rows, :], jnp.add)
        l_buf[...] = l_now
        r_buf[...] = r_now
        return carry

    lax.fori_loop(0, last + 1, prob_step, 0)
    row_sum = jnp.sum(l_buf[...], axis=0, keepdims=True)
    inverse = 1.0 / row_sum
    delta = jnp.sum(r_buf[...], axis=0, keepdims=True) * inverse

    @pl.when(me > 0)
    def _():
        pl.semaphore_wait(barrier, me)

    def sent(j):
        return pltpu.make_async_remote_copy(
            src_ref=send_buf.at[j],
            dst_ref=recv_buf.at[me],
            send_sem=send_sem.at[j],
            recv_sem=recv_sem.at[me],
            device_id=(j, tp),
            device_id_type=MESH,
        )

    def grad_step(p, carry):
        for i in range(PAIR // step_rows):
            rows = slice(i * step_rows, (i + 1) * step_rows)
            prob = s_buf[p, rows, :] * inverse
            p16_buf[rows, :] = prob.astype(jnp.bfloat16)
            ds16_buf[rows, :] = (prob * (dp_buf[p, rows, :] - delta)).astype(jnp.bfloat16)
        ds16 = ds16_buf[...]
        dk = (mm(ds16, q5_buf[...]) * scale).astype(jnp.bfloat16)
        dv = mm(p16_buf[...], d5_buf[...]).astype(jnp.bfloat16)
        dqt_buf[...] += mm(kt_buf[p], ds16)
        for half in range(2):
            j = 2 * p + half
            rows = slice(half * BLOCK, (half + 1) * BLOCK)
            send_buf[j, 0:BLOCK, :] = dk[rows]
            send_buf[j, BLOCK:PAIR, :] = dv[rows]

            @pl.when(j < me)
            def _():
                sent(j).start()

        return carry

    lax.fori_loop(0, last + 1, grad_step, 0)

    for h in range(GROUP_Q):
        cols = slice(h * BLOCK, (h + 1) * BLOCK)
        dq_ref[:, cols] = (dqt_buf[:, cols].T * scale).astype(jnp.bfloat16)

    dk_ref[...] = send_buf[me, 0:BLOCK, :].astype(jnp.float32)
    dv_ref[...] = send_buf[me, BLOCK:PAIR, :].astype(jnp.float32)

    def take(j, carry):
        pltpu.make_async_remote_copy(
            src_ref=send_buf.at[j],
            dst_ref=recv_buf.at[j],
            send_sem=send_sem.at[j],
            recv_sem=recv_sem.at[j],
            device_id=(j, tp),
            device_id_type=MESH,
        ).wait_recv()
        dk_ref[...] += recv_buf[j, 0:BLOCK, :].astype(jnp.float32)
        dv_ref[...] += recv_buf[j, BLOCK:PAIR, :].astype(jnp.float32)
        return carry

    lax.fori_loop(me + 1, N_CTX, take, 0)

    def drain(j, carry):
        sent(j).wait_send()
        return carry

    lax.fori_loop(0, me, drain, 0)


def attention(full_grad, queries, gathered):
    pairs = N_CTX // 2
    bf, f32 = jnp.bfloat16, jnp.float32
    vmem = pl.BlockSpec(memory_space=pltpu.VMEM)
    return pl.pallas_call(
        attention_kernel,
        name="attention_grads",
        out_shape=[
            jax.ShapeDtypeStruct((BLOCK, ROWS_Q), bf),
            jax.ShapeDtypeStruct((BLOCK, HD), f32),
            jax.ShapeDtypeStruct((BLOCK, HD), f32),
        ],
        in_specs=[vmem, vmem, pl.BlockSpec(memory_space=pl.ANY)],
        out_specs=[vmem, vmem, vmem],
        scratch_shapes=[
            pltpu.VMEM((D, ROWS_Q), bf),
            pltpu.VMEM((N_CTX * BLOCK, HD), bf),
            pltpu.VMEM((N_CTX * BLOCK, HD), bf),
            pltpu.VMEM((pairs, HD, PAIR), bf),
            pltpu.VMEM((HD, ROWS_Q), bf),
            pltpu.VMEM((ROWS_Q, HD), bf),
            pltpu.VMEM((HD, ROWS_Q), bf),
            pltpu.VMEM((ROWS_Q, HD), bf),
            pltpu.VMEM((pairs, PAIR, ROWS_Q), f32),
            pltpu.VMEM((pairs, PAIR, ROWS_Q), f32),
            pltpu.VMEM((PAIR, ROWS_Q), bf),
            pltpu.VMEM((PAIR, ROWS_Q), bf),
            pltpu.VMEM((8, ROWS_Q), f32),
            pltpu.VMEM((8, ROWS_Q), f32),
            pltpu.VMEM((8, ROWS_Q), f32),
            pltpu.VMEM((HD, ROWS_Q), f32),
            pltpu.VMEM((N_CTX, PAIR, HD), bf),
            pltpu.VMEM((N_CTX, PAIR, HD), bf),
            pltpu.SemaphoreType.DMA,
            pltpu.SemaphoreType.DMA((2, N_CTX)),
            pltpu.SemaphoreType.DMA((N_CTX,)),
            pltpu.SemaphoreType.DMA((N_CTX,)),
        ],
        cost_estimate=pl.CostEstimate(
            flops=6_000_000_000, bytes_accessed=12_000_000, transcendentals=3_000_000
        ),
        compiler_params=pltpu.CompilerParams(
            collective_id=4, has_side_effects=True, vmem_limit_bytes=56 * 2**20
        ),
    )(full_grad, queries, gathered)


def body(
    hidden_in,
    norm_gain,
    out_grad,
    router_score,
    expert_ids,
    gate_saved,
    up_saved,
    w_gate,
    w_up,
    w_down,
    w_out,
    queries,
    keys,
    values,
):
    devices = lax.axis_size("ctx")
    sharing = devices // EXPERTS
    tok_rows, feature_cols = out_grad.shape
    capacity = gate_saved.shape[2] // devices

    pad = W_ROWS - tok_rows
    shared_part = jnp.concatenate(
        [w_out.T, jnp.pad(keys, ((0, pad), (0, 0))), jnp.pad(values, ((0, pad), (0, 0)))], axis=1
    )
    gathered = lax.all_gather(shared_part, "ctx", axis=0, tiled=True)

    chosen = expert_ids[:, 0]
    onehot = (chosen[:, None] == jnp.arange(EXPERTS, dtype=jnp.int32)[None, :]).astype(jnp.int32)
    ranked = jnp.sum((jnp.cumsum(onehot, axis=0) - onehot) * onehot, axis=1)
    slot_index = chosen * capacity + ranked
    placing = (
        jnp.arange(EXPERTS * capacity, dtype=jnp.int32)[:, None] == slot_index[None, :]
    ).astype(jnp.bfloat16)
    grad_slots = jnp.dot(placing, out_grad, preferred_element_type=jnp.float32).astype(jnp.bfloat16)
    score_slots = jnp.dot(
        placing, router_score[:, None], preferred_element_type=jnp.float32
    ).astype(jnp.bfloat16)
    sent_grad = jnp.repeat(grad_slots.reshape(EXPERTS, capacity, feature_cols), sharing, axis=0)
    sent_score = jnp.repeat(score_slots.reshape(EXPERTS, capacity), sharing, axis=0)
    arrived, arrived_score = (
        lax.all_to_all(sent_grad, "ctx", split_axis=0, concat_axis=0, tiled=True),
        lax.all_to_all(sent_score, "ctx", split_axis=0, concat_axis=0, tiled=True),
    )
    slot_grad = arrived.reshape(devices * capacity, feature_cols)
    slot_score = arrived_score.reshape(devices * capacity).astype(jnp.float32)
    down_local = w_down[0]
    hidden_grad = lax.psum_scatter(
        contract_last(down_local, slot_grad).astype(jnp.bfloat16),
        "tp",
        scatter_dimension=0,
        tiled=True,
    ).astype(jnp.float32)
    gate_val = gate_saved[0].astype(jnp.float32)
    up_val = up_saved[0].astype(jnp.float32)
    activation, slope = silu_parts(gate_val)
    scaled = hidden_grad * slot_score[None, :]
    grad_gate = (scaled * up_val * slope).astype(jnp.bfloat16)
    grad_up = (scaled * activation).astype(jnp.bfloat16)
    router_part = jnp.sum(activation * up_val * hidden_grad, axis=0).astype(jnp.bfloat16)
    gate_local = w_gate[0]
    up_local = w_up[0]
    running = contract_first(lax.all_gather(grad_gate, "tp", axis=0, tiled=True), gate_local)
    back = running + contract_first(lax.all_gather(grad_up, "tp", axis=0, tiled=True), up_local)
    back_parts = back.astype(jnp.bfloat16).reshape(devices, capacity, feature_cols)
    returned, returned_router = (
        lax.all_to_all(back_parts, "ctx", split_axis=0, concat_axis=0, tiled=True),
        lax.all_to_all(
            router_part.reshape(devices, capacity), "ctx", split_axis=0, concat_axis=0, tiled=True
        ),
    )
    summed = jnp.sum(
        returned.astype(jnp.float32).reshape(EXPERTS, sharing, capacity, feature_cols), axis=1
    ).reshape(EXPERTS * capacity, feature_cols)
    router_sum = jnp.sum(
        returned_router.astype(jnp.float32).reshape(EXPERTS, sharing, capacity), axis=1
    ).reshape(EXPERTS * capacity)
    norm_grad = jnp.take(summed, slot_index, axis=0)
    router_tok = jnp.take(router_sum, slot_index, axis=0)
    hidden_val = hidden_in.astype(jnp.float32)
    gain_val = norm_gain.astype(jnp.float32)[None, :]
    squares_part = jnp.sum(hidden_val * hidden_val, axis=1)
    cross_part = jnp.sum(hidden_val * gain_val * norm_grad, axis=1)
    router_grad, sum_squares, cross_sum = lax.psum((router_tok, squares_part, cross_part), "tp")
    inverse_rms = lax.rsqrt(sum_squares / D + EPSILON)[:, None]
    d_hidden = (
        out_grad.astype(jnp.float32)
        + inverse_rms * gain_val * norm_grad
        - hidden_val * inverse_rms * inverse_rms * inverse_rms * cross_sum[:, None] / D
    ).astype(jnp.bfloat16)
    full_grad = lax.all_gather(d_hidden, "tp", axis=1, tiled=True)
    query_grad, key_grad, value_grad = attention(full_grad, queries, gathered)
    return (
        d_hidden,
        router_grad,
        query_grad,
        key_grad.astype(jnp.bfloat16),
        value_grad.astype(jnp.bfloat16),
    )


def solution(mesh):
    in_specs = (
        P("ctx", "tp"),
        P("tp"),
        P("ctx", "tp"),
        P("ctx"),
        P("ctx", None),
        P("ctx", "tp", None),
        P("ctx", "tp", None),
        P("ctx", "tp", None),
        P("ctx", "tp", None),
        P("ctx", None, "tp"),
        P("tp", "ctx"),
        P("ctx", "tp"),
        P("ctx", "tp"),
        P("ctx", "tp"),
    )
    out_specs = (P("ctx", "tp"), P("ctx"), P("ctx", "tp"), P("ctx", "tp"), P("ctx", "tp"))
    return jax.shard_map(body, mesh=mesh, in_specs=in_specs, out_specs=out_specs, check_vma=False)
```

time: 967 us -> 385 us (0.40)
  waiting for transfers between devices: 734 us -> 184 us
  matrix products: 105 us -> 18.8 us
  Pallas kernels: 0 us -> 69.8 us
    reduce_scatter x2 -> x0, waiting for transfers between devices: 436 us -> none  [the longest x1 219 us: body(): lax.psum_scatter(key_accum.astype(jnp.bfloat16), 'ctx', scatter_dimension...]
    all_gather x3 -> x1, waiting for transfers between devices: 164 us -> 45 us  [body(): gathered = lax.all_gather(shared_part, 'ctx', axis=0, tiled=True)]
    dot_general x56 -> x0, matrix products: 81.3 us -> none  [the longest x21 26.9 us: block_scores(): jnp.einsum('rkgd,jkd->kgrj', query_grid, key_block, preferred_element_typ...]
    pallas_call x0 -> x1, Pallas kernels: none -> 69.8 us  [attention(): pl.pallas_call(attention_kernel, name='attention_grads', out_shape=[jax.S...]
  transfers between devices with their start and end apart: 12 -> 8, of which waited for: 11 -> 7; matrix products, arithmetic and copies ran while one was open for 5% -> 6% of each run, Pallas kernels for 0% -> 0%
where the time goes in v1:
time: 385 us; the launch traced here: 384 us
  waiting for transfers between devices  184 us (48%)
  Pallas kernels  69.8 us (18%)
  blocking collectives  48.6 us (13%)
  starting transfers between devices  27.7 us (7%)
  matrix products  18.8 us (5%)
  other arithmetic  14.1 us (4%)
  between operations  14 us (4%)
  local copies, waits for them, and re-layouts  7.37 us (2%)
    pallas_call x1, Pallas kernels, attention(): pl.pallas_call(attention_kernel, name='attention_grads', out_shape=[jax.S...  69.8 us
    all_gather x1, waiting for transfers between devices, body(): gathered = lax.all_gather(shared_part, 'ctx', axis=0, tiled=True)  45 us
    all_to_all x1, blocking collectives, body(): lax.all_to_all(sent_grad, 'ctx', split_axis=0, concat_axis=0, tiled=True)  35.2 us
    all_to_all x1, waiting for transfers between devices, body(): lax.all_to_all(back_parts, 'ctx', split_axis=0, concat_axis=0, tiled=True)  31.4 us
    all_gather x1, waiting for transfers between devices, body(): lax.all_gather(grad_gate, 'tp', axis=0, tiled=True)  30.5 us
    all_gather x1, waiting for transfers between devices, body(): full_grad = lax.all_gather(d_hidden, 'tp', axis=1, tiled=True)  29.2 us
    reduce_scatter x1, waiting for transfers between devices, body(): lax.psum_scatter(contract_last(down_local, slot_grad).astype(jnp.bfloat16...  22 us
    all_gather x1, waiting for transfers between devices, body(): lax.all_gather(grad_up, 'tp', axis=0, tiled=True)  20 us
  transfers between devices with their start and end apart: 8, of which 7 were waited for; matrix products, arithmetic and copies ran while one was open for 6% of the time, Pallas kernels for 0%

profile of v1, /device:TPU:88, one launch (start us, length us, event | category | flops | bytes accessed | tf_op | source)
XLA Modules:
  0.0 383.9 jit_solution(3420688985303115211)
XLA Ops:
  11.0 35.2 %all_to_all.25 = bf16[32,24,640]{2,1,0:T(8,128)(2,1)S(1)} all-to-all(bf16[32,24,640]{2,1,0:T(8,128)(2,1)S(1)} %bitcast.57), channel_id=1, replica_groups=mesh['ctx'=32,'tp'=8] {'ctx'}, dimensions={0} | all-to-all | bytes 1966080 | tf_op jit(solution)/shard_map/all_to_all | solution.py:322
  46.2 4.1 %fusion = bf16[2048,768]{0,1:T(8,128)(2,1)} fusion(bf16[768,640]{1,0:T(8,128)(2,1)S(1)} %bitcast.60, bf16[1,2048,640]{2,1,0:T(8,128)(2,1)S(1)} %copy-done), kind=kOutput, calls=%fused_computation.3 | convolution fusion | flops 2014838784 | bytes 6750208 | tf_op jit(solution)/shard_map/dot_general | solution.py:31
  51.8 7.5 %all-to-all-start.1 = ((bf16[32,1,24]{2,1,0:T(2,128)(2,1)}), bf16[32,1,24]{2,1,0:T(2,128)(2,1)S(1)}, u32[]{:S(2)}, u32[]{:S(2)}) async-start(bf16[32,1,24]{2,1,0:T(2,128)(2,1)} %copy.26), calls=%async_computation.2 | async-start | bytes 32768 | tf_op jit(solution)/shard_map/all_to_all | solution.py:323
  60.8 4.7 %all-to-all-done.1 = bf16[32,1,24]{2,1,0:T(2,128)(2,1)S(1)} async-done(((bf16[32,1,24]{2,1,0:T(2,128)(2,1)}), bf16[32,1,24]{2,1,0:T(2,128)(2,1)S(1)}, u32[]{:S(2)}, u32[]{:S(2)}) %all-to-all-start.1) | async-done | bytes 1568 | tf_op jit(solution)/shard_map/all_to_all | solution.py:323
  65.6 22.0 %reduce-scatter.2.cloned.1.call-done = bf16[256,768]{0,1:T(8,128)(2,1)} async-done(((bf16[2048,768]{0,1:T(8,128)(2,1)}), bf16[256,768]{0,1:T(8,128)(2,1)}) %reduce-scatter.2.cloned.1.call-update) | async-done | bytes 393232 | tf_op jit(solution)/shard_map/reduce_scatter | solution.py:328
  87.6 2.5 fusion.10
  90.9 1.7 fusion.31
  93.3 9.9 %all-to-all-start.3 = ((bf16[32,1,24]{2,1,0:T(2,128)(2,1)}), bf16[32,1,24]{2,1,0:T(2,128)(2,1)S(1)}, u32[]{:S(2)}, u32[]{:S(2)}) async-start(bf16[32,1,24]{2,1,0:T(2,128)(2,1)} %convert_element_type.127), calls=%async_computation.4 | async-start | bytes 32768 | tf_op jit(solution)/shard_map/all_to_all | solution.py:348
  103.2 20.0 %all-gather.7.cloned.1.call-done = bf16[2048,768]{0,1:T(8,128)(2,1)} async-done(((bf16[256,768]{0,1:T(8,128)(2,1)}), bf16[2048,768]{0,1:T(8,128)(2,1)}) %all-gather.7.cloned.1.call-update) | async-done | bytes 3145744 | tf_op jit(solution)/shard_map/all_gather | solution.py:344
  123.2 6.6 %fusion.1 = f32[768,640]{1,0:T(8,128)} fusion(bf16[2048,768]{0,1:T(8,128)(2,1)} %all-gather.7.cloned.1.call-done, bf16[1,640,2048]{2,1,0:T(8,128)(2,1)} %param.22), kind=kOutput, calls=%fused_computation.4 | convolution fusion | flops 2013265920 | bytes 7733248 | tf_op jit(solution)/shard_map/dot_general | solution.py:37
  129.8 30.5 %all-gather.5.cloned.1.call-done = bf16[2048,768]{0,1:T(8,128)(2,1)} async-done(((bf16[256,768]{0,1:T(8,128)(2,1)}), bf16[2048,768]{0,1:T(8,128)(2,1)}) %all-gather.5.cloned.1.call-update) | async-done | bytes 3145744 | tf_op jit(solution)/shard_map/all_gather | solution.py:343
  160.3 6.9 %add_convert_fusion = bf16[768,640]{1,0:T(8,128)(2,1)} fusion(f32[768,640]{1,0:T(8,128)} %fusion.1, bf16[2048,768]{0,1:T(8,128)(2,1)} %all-gather.5.cloned.1.call-done, bf16[1,640,2048]{2,1,0:T(8,128)(2,1)} %param.21), kind=kOutput, calls=%fused_computation.10 | convolution fusion | flops 2014248960 | bytes 8716288 | tf_op jit(solution)/shard_map/dot_general | solution.py:37
  167.2 10.0 %all-to-all-start.2 = ((bf16[32,24,640]{2,1,0:T(8,128)(2,1)}), bf16[32,24,640]{2,1,0:T(8,128)(2,1)}, u32[]{:S(2)}, u32[]{:S(2)}) async-start(bf16[32,24,640]{2,1,0:T(8,128)(2,1)} %bitcast.59), calls=%async_computation.3 | async-start | bytes 1966080 | tf_op jit(solution)/shard_map/all_to_all | solution.py:347
  177.5 1.3 gather_fusion.1
  178.8 31.4 %all-to-all-done.2 = bf16[32,24,640]{2,1,0:T(8,128)(2,1)} async-done(((bf16[32,24,640]{2,1,0:T(8,128)(2,1)}), bf16[32,24,640]{2,1,0:T(8,128)(2,1)}, u32[]{:S(2)}, u32[]{:S(2)}) %all-to-all-start.2) | async-done | bytes 983072 | tf_op jit(solution)/shard_map/all_to_all | solution.py:347
  210.2 1.4 convert_reduce_fusion
  213.5 13.4 %all-reduce.2 = (f32[128]{0:T(128)S(1)}, f32[128]{0:T(128)S(1)}, f32[128]{0:T(128)}) all-reduce(f32[128]{0:T(128)S(1)} %get-tuple-element.12, f32[128]{0:T(128)S(1)} %get-tuple-element.11, f32[128]{0:T(128)S(1)} %broadcast_select_fusion), channel_id=1, replica_groups=mesh['ctx'=32,'tp'=8] {'tp'}, use_global_device_ids=true, to_apply=%region_7.8 | all-reduce | flops 384 | bytes 3072 | tf_op jit(solution)/shard_map/psum | solution.py:364
  226.9 1.9 fusion.27
  228.8 45.0 %all-gather.11.cloned.1.call-done.gathered_ref = bf16[5120,896]{1,0:T(8,128)(2,1)} async-done(((bf16[160,896]{1,0:T(8,128)(2,1)}), bf16[5120,896]{1,0:T(8,128)(2,1)}) %all-gather.11.cloned.1.call-update) | async-done | bytes 9175056 | tf_op jit(solution)/shard_map/all_gather | solution.py:306
  273.9 29.2 %all-gather.9.cloned.1.call-done.full_ref = bf16[128,5120]{1,0:T(8,128)(2,1)} async-done(((bf16[128,640]{1,0:T(8,128)(2,1)}), bf16[128,5120]{1,0:T(8,128)(2,1)}) %all-gather.9.cloned.1.call-update) | async-done | bytes 1310736 | tf_op jit(solution)/shard_map/all_gather | solution.py:371
  303.1 69.8 %attention_grads.1 = (bf16[128,640]{1,0:T(8,128)(2,1)}, f32[128,128]{1,0:T(8,128)}, f32[128,128]{1,0:T(8,128)}) custom-call(bf16[128,5120]{1,0:T(8,128)(2,1)} %all-gather.9.cloned.1.call-done.full_ref, bf16[128,640]{1,0:T(8,128)(2,1)} %q_ref.1, bf16[5120,896]{1,0:T(8,128)(2,1)} %all-gather.11.cloned.1.call-done.gathered_ref), custom_call_target="tpu_custom_call" | custom-call | flops 6000000000 | bytes 12000000 | tf_op jit(solution)/shard_map/attention_grads/pallas_call | solution.py:238
  372.9 1.5 convert_element_type.121
  374.4 1.5 convert_element_type.122
  375.8 1.6 copy.31
  (51 shorter events, 10.5 us)
Async XLA Ops:
  7.2 39.1 %copy-start = (bf16[1,2048,640]{2,1,0:T(8,128)(2,1)S(1)}, bf16[1,2048,640]{2,1,0:T(8,128)(2,1)}, u32[]{:S(2)}) copy-start(bf16[1,2048,640]{2,1,0:T(8,128)(2,1)} %param.23) | copy-start | bytes 7864324
  7.2 80.4 %reduce-scatter.2.cloned.1.call-start = ((), (), s32[]{:S(2)}) async-start(), calls=%async_computation.5 | async-start | bytes 3538944 | tf_op jit(solution)/shard_map/reduce_scatter | solution.py:328
  50.3 0.7 copy-start.6
  50.3 9.1 %copy-start.1 = (bf16[1,256,768]{2,1,0:T(8,128)(2,1)S(1)}, bf16[1,256,768]{2,1,0:T(8,128)(2,1)}, u32[]{:S(2)}) copy-start(bf16[1,256,768]{2,1,0:T(8,128)(2,1)} %param.20) | copy-start | bytes 1179652
  50.9 39.9 %copy-start.2 = (bf16[128,128]{1,0:T(8,128)(2,1)S(1)}, bf16[128,128]{1,0:T(8,128)(2,1)}, u32[]{:S(2)}) copy-start(bf16[128,128]{1,0:T(8,128)(2,1)} %param.27) | copy-start | bytes 98308
  50.9 39.9 %copy-start.3 = (bf16[128,128]{1,0:T(8,128)(2,1)S(1)}, bf16[128,128]{1,0:T(8,128)(2,1)}, u32[]{:S(2)}) copy-start(bf16[128,128]{1,0:T(8,128)(2,1)} %param.26) | copy-start | bytes 98308
  51.8 13.6 %all-to-all-start.1 = ((bf16[32,1,24]{2,1,0:T(2,128)(2,1)}), bf16[32,1,24]{2,1,0:T(2,128)(2,1)S(1)}, u32[]{:S(2)}, u32[]{:S(2)}) async-start(bf16[32,1,24]{2,1,0:T(2,128)(2,1)} %copy.26), calls=%async_computation.2 | async-start | bytes 32768 | tf_op jit(solution)/shard_map/all_to_all | solution.py:323
  59.4 63.9 %all-gather.7.cloned.1.call-start = ((), (), s32[]{:S(2)}) async-start(), calls=%async_computation.7 | async-start | bytes 3538944 | tf_op jit(solution)/shard_map/all_gather | solution.py:344
  90.1 70.2 %all-gather.5.cloned.1.call-start = ((), (), s32[]{:S(2)}) async-start(), calls=%async_computation.6 | async-start | bytes 3538944 | tf_op jit(solution)/shard_map/all_gather | solution.py:343
  90.8 183.1 %all-gather.11.cloned.1.call-start = ((), (), s32[]{:S(2)}) async-start(), calls=%async_computation.9 | async-start | bytes 9461760 | tf_op jit(solution)/shard_map/all_gather | solution.py:306
  93.3 73.9 %all-to-all-start.3 = ((bf16[32,1,24]{2,1,0:T(2,128)(2,1)}), bf16[32,1,24]{2,1,0:T(2,128)(2,1)S(1)}, u32[]{:S(2)}, u32[]{:S(2)}) async-start(bf16[32,1,24]{2,1,0:T(2,128)(2,1)} %convert_element_type.127), calls=%async_computation.4 | async-start | bytes 32768 | tf_op jit(solution)/shard_map/all_to_all | solution.py:348
  129.8 47.5 %copy-start.5 = (bf16[640]{0:T(1024)(128)(2,1)S(1)}, bf16[640]{0:T(1024)(128)(2,1)}, u32[]{:S(2)}) copy-start(bf16[640]{0:T(1024)(128)(2,1)} %param.15) | copy-start | bytes 3844
  129.8 47.5 %copy-start.4 = (s32[128,1]{0,1:T(1,128)S(1)}, s32[128,1]{0,1:T(1,128)}, u32[]{:S(2)}) copy-start(s32[128,1]{0,1:T(1,128)} %param.18) | copy-start | bytes 1540
  167.2 43.0 %all-to-all-start.2 = ((bf16[32,24,640]{2,1,0:T(8,128)(2,1)}), bf16[32,24,640]{2,1,0:T(8,128)(2,1)}, u32[]{:S(2)}, u32[]{:S(2)}) async-start(bf16[32,24,640]{2,1,0:T(8,128)(2,1)} %bitcast.59), calls=%async_computation.3 | async-start | bytes 1966080 | tf_op jit(solution)/shard_map/all_to_all | solution.py:347
  177.3 125.8 %all-gather.9.cloned.1.call-start = ((), (), s32[]{:S(2)}) async-start(), calls=%async_computation.8 | async-start | bytes 1474560 | tf_op jit(solution)/shard_map/all_gather | solution.py:371
Sparse Core Ops, SparseCore 0:
  50.4 37.1 reduce-scatter.1
  90.2 32.9 all-gather.6
  125.1 35.1 all-gather.4
  162.7 111.0 all-gather.10
  276.1 26.8 all-gather.8

commit v2 on v1

--- a/solution.py
+++ b/solution.py
@@ -16,6 +16,16 @@
 PAIR = 2 * BLOCK
 ROWS_Q = GROUP_Q * BLOCK
 W_ROWS = 160
+N_Y, N_Z, N_X, N_TP = 4, 8, 4, 8
+GROUP = N_CTX // EXPERTS
+CAP = 24
+CAP_PAD = 32
+CHUNK = N_Z * CAP
+SLOTS = N_CTX * CAP
+FEAT = D // N_TP
+FF_GRP = 2048
+FF_DEV = FF_GRP // N_TP
+ROW_ORDER = (0, 1, 3, 2)
 MESH = pl.DeviceIdType.MESH
 EPSILON = 1e-05
 NEG = -1e30
@@ -27,18 +37,6 @@
     return (gate_pre * sigmoid_val, sigmoid_val * (1.0 + gate_pre * (1.0 - sigmoid_val)))
 
 
-def contract_last(left_mat, right_mat):
-    return lax.dot_general(
-        left_mat, right_mat, (((1,), (1,)), ((), ())), preferred_element_type=jnp.float32
-    )
-
-
-def contract_first(left_mat, right_mat):
-    return lax.dot_general(
-        left_mat, right_mat, (((0,), (1,)), ((), ())), preferred_element_type=jnp.float32
-    )
-
-
 def mm(a, b):
     return jnp.dot(a, b, preferred_element_type=jnp.float32)
 
@@ -47,7 +45,7 @@
     full_ref, q_ref, gathered_ref, dq_ref, dk_ref, dv_ref,
     w_buf, k_buf, v_buf, kt_buf, qt_buf, q5_buf, dt_buf, d5_buf,
     s_buf, dp_buf, p16_buf, ds16_buf, m_buf, l_buf, r_buf, dqt_buf,
-    send_buf, recv_buf, w_sem, kv_sem, send_sem, recv_sem,
+    send_buf, recv_buf, total_buf, w_sem, kv_sem, send_sem, recv_sem,
 ):
     me = lax.axis_index("ctx")
     tp = lax.axis_index("tp")
@@ -134,7 +132,10 @@
     m_buf[...] = jnp.broadcast_to(row_max, m_buf.shape)
 
     w_copy.wait()
-    dout = mm(full_ref[...], w_buf[...]).astype(jnp.bfloat16)
+    dout = mm(full_ref[0], w_buf[0:FEAT, :])
+    for t in range(1, N_TP):
+        dout = dout + mm(full_ref[t], w_buf[t * FEAT : (t + 1) * FEAT, :])
+    dout = dout.astype(jnp.bfloat16)
     for h in range(GROUP_Q):
         cols = slice(h * BLOCK, (h + 1) * BLOCK)
         head = dout[:, cols]
@@ -206,8 +207,7 @@
         cols = slice(h * BLOCK, (h + 1) * BLOCK)
         dq_ref[:, cols] = (dqt_buf[:, cols].T * scale).astype(jnp.bfloat16)
 
-    dk_ref[...] = send_buf[me, 0:BLOCK, :].astype(jnp.float32)
-    dv_ref[...] = send_buf[me, BLOCK:PAIR, :].astype(jnp.float32)
+    total_buf[...] = send_buf[me].astype(jnp.float32)
 
     def take(j, carry):
         pltpu.make_async_remote_copy(
@@ -218,11 +218,12 @@
             device_id=(j, tp),
             device_id_type=MESH,
         ).wait_recv()
-        dk_ref[...] += recv_buf[j, 0:BLOCK, :].astype(jnp.float32)
-        dv_ref[...] += recv_buf[j, BLOCK:PAIR, :].astype(jnp.float32)
+        total_buf[...] += recv_buf[j].astype(jnp.float32)
         return carry
 
     lax.fori_loop(me + 1, N_CTX, take, 0)
+    dk_ref[...] = total_buf[0:BLOCK, :].astype(jnp.bfloat16)
+    dv_ref[...] = total_buf[BLOCK:PAIR, :].astype(jnp.bfloat16)
 
     def drain(j, carry):
         sent(j).wait_send()
@@ -240,8 +241,8 @@
         name="attention_grads",
         out_shape=[
             jax.ShapeDtypeStruct((BLOCK, ROWS_Q), bf),
-            jax.ShapeDtypeStruct((BLOCK, HD), f32),
-            jax.ShapeDtypeStruct((BLOCK, HD), f32),
+            jax.ShapeDtypeStruct((BLOCK, HD), bf),
+            jax.ShapeDtypeStruct((BLOCK, HD), bf),
         ],
         in_specs=[vmem, vmem, pl.BlockSpec(memory_space=pl.ANY)],
         out_specs=[vmem, vmem, vmem],
@@ -264,6 +265,7 @@
             pltpu.VMEM((HD, ROWS_Q), f32),
             pltpu.VMEM((N_CTX, PAIR, HD), bf),
             pltpu.VMEM((N_CTX, PAIR, HD), bf),
+            pltpu.VMEM((PAIR, HD), f32),
             pltpu.SemaphoreType.DMA,
             pltpu.SemaphoreType.DMA((2, N_CTX)),
             pltpu.SemaphoreType.DMA((N_CTX,)),
@@ -276,6 +278,395 @@
             collective_id=4, has_side_effects=True, vmem_limit_bytes=56 * 2**20
         ),
     )(full_grad, queries, gathered)
+
+
+def dot_nt(a, b):
+    return lax.dot_general(a, b, (((1,), (1,)), ((), ())), preferred_element_type=jnp.float32)
+
+
+def expert_kernel(
+    slots_ref, pick_ref, score_ref, hidden_ref, gain_ref, grad_ref,
+    down_ref, gate_ref, up_ref, wg_ref, wu_ref,
+    dh_ref, stat_ref, full_ref,
+    down, wg, wu, recv_d, flat, slots, own, sib_out, sib_in, x_out, x_in,
+    act_buf, slope_buf, prod_buf, ag, acc, back, ret, picked, stats, square, full,
+    w_sem, d_send, d_recv, s_send, s_recv, x_send, x_recv, ax_send, ax_recv,
+    as_send, as_recv, b_send, b_recv, t_send, t_recv, fx_send, fx_recv, fs_send, fs_recv,
+):
+    me = lax.axis_index("ctx")
+    tp = lax.axis_index("tp")
+    y, z = me // N_Z, me % N_Z
+    x, k = tp // 2, tp % 2
+    sibling = 2 * x + (1 - k)
+    far = (2, 1, 3)
+
+    def chip(dx):
+        return (x + dx) % N_X
+
+    def remote(src, dst, send, recv, ctx, peer):
+        return pltpu.make_async_remote_copy(
+            src_ref=src, dst_ref=dst, send_sem=send, recv_sem=recv,
+            device_id=(ctx, peer), device_id_type=MESH,
+        )
+
+    w_copies = [
+        pltpu.make_async_copy(down_ref, down, w_sem.at[0]),
+        pltpu.make_async_copy(wg_ref, wg, w_sem.at[1]),
+        pltpu.make_async_copy(wu_ref, wu, w_sem.at[2]),
+    ]
+    for copy in w_copies:
+        copy.start()
+
+    barrier = pltpu.get_barrier_semaphore()
+
+    def greet_ctx(i, carry):
+        pl.semaphore_signal(
+            barrier, inc=1, device_id=((me + i) % N_CTX, tp), device_id_type=MESH
+        )
+        return carry
+
+    def greet_tp(i, carry):
+        pl.semaphore_signal(
+            barrier, inc=1, device_id=(me, (tp + i) % N_TP), device_id_type=MESH
+        )
+        return carry
+
+    lax.fori_loop(1, N_CTX, greet_ctx, 0)
+    lax.fori_loop(1, N_TP, greet_tp, 0)
+    hidden_val = hidden_ref[...].astype(jnp.float32)
+    square[...] = jnp.broadcast_to(
+        jnp.sum(hidden_val * hidden_val, axis=1, keepdims=True), square.shape
+    )
+    pl.semaphore_wait(barrier, N_CTX - 1 + N_TP - 1)
+
+    def dispatch(j):
+        return remote(
+            slots_ref.at[j // GROUP], recv_d.at[me], d_send.at[j], d_recv.at[me], j, tp
+        )
+
+    for dy in ROW_ORDER:
+        row = (y - dy + N_Y) % N_Y
+
+        def send_step(dz, carry, row=row):
+            dispatch(row * N_Z + (z + dz) % N_Z).start()
+            return carry
+
+        lax.fori_loop(1 if dy == 0 else 0, N_Z, send_step, 0)
+    recv_d[me] = slots_ref[me // GROUP]
+
+    def chunk_rows(ch):
+        start = ((y + ROW_ORDER[ch]) % N_Y) * CHUNK
+        return pl.ds(pl.multiple_of(start, CHUNK), CHUNK)
+
+    def arrive(ch):
+        first = ((y + ROW_ORDER[ch]) % N_Y) * N_Z
+        for i in range(N_Z):
+            j = first + i
+
+            @pl.when(j != me)
+            def _():
+                remote(
+                    slots_ref.at[0], recv_d.at[j], d_send.at[j], d_recv.at[j], j, tp
+                ).wait_recv()
+
+            flat[i * CAP : (i + 1) * CAP, :] = recv_d[j].astype(jnp.float32)
+        slots[chunk_rows(ch), :] = flat[...].astype(jnp.bfloat16)
+
+    def sib_copy(i, ch):
+        rows = chunk_rows(ch)
+        return remote(
+            sib_out.at[i, rows], sib_in.at[i, rows], s_send.at[i, ch], s_recv.at[i, ch],
+            me, sibling,
+        )
+
+    def x_copy(i, ch):
+        rows = chunk_rows(ch)
+        return remote(
+            x_out.at[i, rows], x_in.at[i, rows], x_send.at[i, ch], x_recv.at[i, ch],
+            me, 2 * chip(far[i]) + k,
+        )
+
+    def stage1(ch):
+        rows = chunk_rows(ch)
+        part = slots[rows, :]
+        for i, dx in enumerate(far + (0,)):
+            base = 2 * chip(dx)
+
+            def block(t):
+                start = pl.multiple_of(t * FF_DEV, FF_DEV)
+                return dot_nt(part, down[pl.ds(start, FF_DEV), :]).astype(jnp.bfloat16)
+
+            sib_out[i, rows, :] = block(base + 1 - k)
+            sib_copy(i, ch).start()
+            own[i, rows, :] = block(base + k)
+
+    def joined(i, ch):
+        rows = chunk_rows(ch)
+        sib_copy(i, ch).wait_recv()
+        return own[i, rows, :].astype(jnp.float32) + sib_in[i, rows, :].astype(jnp.float32)
+
+    def stage2(ch):
+        rows = chunk_rows(ch)
+        for i in range(3):
+            x_out[i, rows, :] = joined(i, ch).astype(jnp.bfloat16)
+            x_copy(i, ch).start()
+
+    def prepare():
+        gate = gate_ref[...].astype(jnp.float32).T
+        up = up_ref[...].astype(jnp.float32).T
+        act, slope = silu_parts(gate)
+        act_buf[...] = act
+        slope_buf[...] = up * slope
+        prod_buf[...] = act * up
+
+    def ag_out(i, ch):
+        rows = chunk_rows(ch)
+        return remote(
+            ag.at[tp, rows], ag.at[tp, rows], ax_send.at[i, ch], ax_recv.at[i, ch],
+            me, 2 * chip(far[i]) + k,
+        )
+
+    def ag_chip(i, ch):
+        return 2 * chip(N_X - far[i]) + k
+
+    def ag_in(i, ch):
+        rows = chunk_rows(ch)
+        t = ag_chip(i, ch)
+        return remote(
+            ag.at[t, rows], ag.at[t, rows], ax_send.at[i, ch], ax_recv.at[i, ch], me, t
+        )
+
+    def ag_share(t, i, ch):
+        rows = chunk_rows(ch)
+        return remote(
+            ag.at[t, rows], ag.at[t, rows], as_send.at[i, ch], as_recv.at[i, ch], me, sibling
+        )
+
+    def stage3(ch):
+        rows = chunk_rows(ch)
+        hid = joined(3, ch)
+        for i in range(3):
+            x_copy(i, ch).wait_recv()
+            hid = hid + x_in[i, rows, :].astype(jnp.float32)
+        ag[tp, rows, 0:FF_DEV] = (hid * slope_buf[rows, :]).astype(jnp.bfloat16)
+        ag[tp, rows, FF_DEV : 2 * FF_DEV] = (hid * act_buf[rows, :]).astype(jnp.bfloat16)
+        for i in range(3):
+            ag_out(i, ch).start()
+        ag_share(tp, 3, ch).start()
+        term = jnp.sum(hid * prod_buf[rows, :], axis=1, keepdims=True)
+        prod_buf[rows, 0:HD] = jnp.broadcast_to(term, (CHUNK, HD))
+
+    def product(t, rows):
+        cols = pl.ds(pl.multiple_of(t * FF_DEV, FF_DEV), FF_DEV)
+        return dot_nt(ag[t, rows, 0:FF_DEV], wg[:, cols]) + dot_nt(
+            ag[t, rows, FF_DEV : 2 * FF_DEV], wu[:, cols]
+        )
+
+    def back_copy(j):
+        return remote(back.at[j], ret.at[me], b_send.at[j], b_recv.at[me], j, tp)
+
+    def stage4(ch):
+        rows = chunk_rows(ch)
+        acc[:, FEAT : FEAT + HD] = prod_buf[rows, 0:HD]
+        acc[:, 0:FEAT] = product(tp, rows)
+        for i in (1, 2, 0):
+            ag_in(i, ch).wait_recv()
+            ag_share(ag_chip(i, ch), i, ch).start()
+            acc[:, 0:FEAT] += product(ag_chip(i, ch), rows)
+        for i in (3, 1, 2, 0):
+            t = sibling if i == 3 else ag_chip(i, ch) + 1 - 2 * k
+            ag_share(t, i, ch).wait_recv()
+            acc[:, 0:FEAT] += product(t, rows)
+        first = ((y + ROW_ORDER[ch]) % N_Y) * N_Z
+        for i in range(N_Z):
+            j = first + i
+            back[j] = acc[i * CAP : (i + 1) * CAP, :].astype(jnp.bfloat16)
+
+            @pl.when(j != me)
+            def _():
+                back_copy(j).start()
+
+    w_copies[0].wait()
+    arrive(0)
+    stage1(0)
+    arrive(1)
+    stage1(1)
+    stage2(0)
+    arrive(2)
+    stage1(2)
+    stage2(1)
+    arrive(3)
+    stage1(3)
+    stage2(2)
+    stage2(3)
+    prepare()
+    w_copies[1].wait()
+    w_copies[2].wait()
+    for ch in range(N_Y):
+        stage3(ch)
+    for ch in range(N_Y):
+        stage4(ch)
+    ret[me] = back[me]
+
+    picked[...] = jnp.zeros_like(picked)
+    for ch in range(N_Y):
+        first = ((y - ROW_ORDER[ch] + N_Y) % N_Y) * N_Z
+        for i in range(N_Z):
+            j = first + i
+
+            @pl.when(j != me)
+            def _():
+                remote(back.at[j], ret.at[j], b_send.at[j], b_recv.at[j], j, tp).wait_recv()
+
+            acc[i * CAP : (i + 1) * CAP, :] = ret[j].astype(jnp.float32)
+        cols = pl.ds(pl.multiple_of(first * CAP_PAD, N_Z * CAP_PAD), N_Z * CAP_PAD)
+        picked[...] += mm(pick_ref[:, cols][:, 0:CHUNK], acc[...].astype(jnp.bfloat16))
+
+    norm_grad = picked[:, 0:FEAT] * score_ref[...]
+    hidden_now = hidden_ref[...].astype(jnp.float32)
+    gain_val = gain_ref[...].astype(jnp.float32)
+    cross = jnp.sum(hidden_now * gain_val * norm_grad, axis=1, keepdims=True)
+    lane = lax.broadcasted_iota(jnp.int32, (BLOCK, HD), 1)
+    packed = jnp.where(
+        lane == 0, picked[:, FEAT : FEAT + HD], jnp.where(lane == 1, square[...], cross)
+    )
+    stats[tp] = packed.T[0:8, :]
+
+    def stat_copy(peer, src):
+        return remote(
+            stats.at[src], stats.at[src], t_send.at[peer], t_recv.at[src], me, peer
+        )
+
+    def stat_start(i, carry):
+        stat_copy((tp + i) % N_TP, tp).start()
+        return carry
+
+    def stat_wait(i, carry):
+        stat_copy((tp + i) % N_TP, (tp + i) % N_TP).wait_recv()
+        return carry
+
+    lax.fori_loop(1, N_TP, stat_start, 0)
+    lax.fori_loop(1, N_TP, stat_wait, 0)
+    total = stats[0]
+    for t in range(1, N_TP):
+        total = total + stats[t]
+    stat_ref[...] = total
+    spread = jnp.concatenate([total] * (BLOCK // 8), axis=0).T
+    inverse_rms = lax.rsqrt(spread[:, 1:2] / D + EPSILON)
+    cross_sum = spread[:, 2:3]
+    d_hidden = (
+        grad_ref[...].astype(jnp.float32)
+        + inverse_rms * gain_val * norm_grad
+        - hidden_now * inverse_rms * inverse_rms * inverse_rms * cross_sum / D
+    ).astype(jnp.bfloat16)
+    dh_ref[...] = d_hidden
+    full[tp] = d_hidden
+
+    def full_out(i):
+        return remote(
+            full.at[tp], full.at[tp], fx_send.at[i], fx_recv.at[i], me, 2 * chip(far[i]) + k
+        )
+
+    def full_in(i):
+        t = ag_chip(i, 0)
+        return remote(full.at[t], full.at[t], fx_send.at[i], fx_recv.at[i], me, t)
+
+    def full_share(t, i):
+        return remote(full.at[t], full.at[t], fs_send.at[i], fs_recv.at[i], me, sibling)
+
+    for i in range(3):
+        full_out(i).start()
+    full_share(tp, 3).start()
+    for i in (1, 2, 0):
+        full_in(i).wait_recv()
+        full_share(ag_chip(i, 0), i).start()
+    for i in (3, 1, 2, 0):
+        t = sibling if i == 3 else ag_chip(i, 0) + 1 - 2 * k
+        full_share(t, i).wait_recv()
+    full_ref[...] = full[...]
+
+    def drain_ctx(i, carry):
+        j = (me + i) % N_CTX
+        dispatch(j).wait_send()
+        back_copy(j).wait_send()
+        return carry
+
+    def drain_tp(i, carry):
+        stat_copy((tp + i) % N_TP, tp).wait_send()
+        return carry
+
+    lax.fori_loop(1, N_CTX, drain_ctx, 0)
+    lax.fori_loop(1, N_TP, drain_tp, 0)
+    for ch in range(N_Y):
+        for i in range(4):
+            sib_copy(i, ch).wait_send()
+            ag_share(tp, i, ch).wait_send()
+        for i in range(3):
+            x_copy(i, ch).wait_send()
+            ag_out(i, ch).wait_send()
+    for i in range(3):
+        full_out(i).wait_send()
+    for i in range(4):
+        full_share(tp, i).wait_send()
+
+
+def expert_block(slots, pick, score, hidden, gain, grad, down, gate, up, wg, wu):
+    bf, f32 = jnp.bfloat16, jnp.float32
+    vmem = pl.BlockSpec(memory_space=pltpu.VMEM)
+    hbm = pl.BlockSpec(memory_space=pl.ANY)
+    dma = pltpu.SemaphoreType.DMA
+    wide = FEAT + HD
+    return pl.pallas_call(
+        expert_kernel,
+        name="expert_block",
+        out_shape=[
+            jax.ShapeDtypeStruct((BLOCK, FEAT), bf),
+            jax.ShapeDtypeStruct((8, BLOCK), f32),
+            jax.ShapeDtypeStruct((N_TP, BLOCK, FEAT), bf),
+        ],
+        in_specs=[vmem] * 6 + [hbm, vmem, vmem, hbm, hbm],
+        out_specs=[vmem] * 3,
+        scratch_shapes=[
+            pltpu.VMEM((FF_GRP, FEAT), bf),
+            pltpu.VMEM((FEAT, FF_GRP), bf),
+            pltpu.VMEM((FEAT, FF_GRP), bf),
+            pltpu.VMEM((N_CTX, CAP, FEAT), bf),
+            pltpu.VMEM((CHUNK, FEAT), f32),
+            pltpu.VMEM((SLOTS, FEAT), bf),
+            pltpu.VMEM((4, SLOTS, FF_DEV), bf),
+            pltpu.VMEM((4, SLOTS, FF_DEV), bf),
+            pltpu.VMEM((4, SLOTS, FF_DEV), bf),
+            pltpu.VMEM((3, SLOTS, FF_DEV), bf),
+            pltpu.VMEM((3, SLOTS, FF_DEV), bf),
+            pltpu.VMEM((SLOTS, FF_DEV), f32),
+            pltpu.VMEM((SLOTS, FF_DEV), f32),
+            pltpu.VMEM((SLOTS, FF_DEV), f32),
+            pltpu.VMEM((N_TP, SLOTS, 2 * FF_DEV), bf),
+            pltpu.VMEM((CHUNK, wide), f32),
+            pltpu.VMEM((N_CTX, CAP, wide), bf),
+            pltpu.VMEM((N_CTX, CAP, wide), bf),
+            pltpu.VMEM((BLOCK, wide), f32),
+            pltpu.VMEM((N_TP, 8, BLOCK), f32),
+            pltpu.VMEM((BLOCK, HD), f32),
+            pltpu.VMEM((N_TP, BLOCK, FEAT), bf),
+            dma((3,)),
+            dma((N_CTX,)), dma((N_CTX,)),
+            dma((4, N_Y)), dma((4, N_Y)),
+            dma((3, N_Y)), dma((3, N_Y)),
+            dma((3, N_Y)), dma((3, N_Y)),
+            dma((4, N_Y)), dma((4, N_Y)),
+            dma((N_CTX,)), dma((N_CTX,)),
+            dma((N_TP,)), dma((N_TP,)),
+            dma((3,)), dma((3,)),
+            dma((4,)), dma((4,)),
+        ],
+        cost_estimate=pl.CostEstimate(
+            flops=60_000_000_000, bytes_accessed=200_000_000, transcendentals=3_000_000
+        ),
+        compiler_params=pltpu.CompilerParams(
+            collective_id=3, has_side_effects=True, vmem_limit_bytes=56 * 2**20
+        ),
+    )(slots, pick, score, hidden, gain, grad, down, gate, up, wg, wu)
 
 
 def body(
@@ -294,88 +685,51 @@
     keys,
     values,
 ):
-    devices = lax.axis_size("ctx")
-    sharing = devices // EXPERTS
-    tok_rows, feature_cols = out_grad.shape
-    capacity = gate_saved.shape[2] // devices
-
+    tok_rows = out_grad.shape[0]
     pad = W_ROWS - tok_rows
     shared_part = jnp.concatenate(
         [w_out.T, jnp.pad(keys, ((0, pad), (0, 0))), jnp.pad(values, ((0, pad), (0, 0)))], axis=1
     )
     gathered = lax.all_gather(shared_part, "ctx", axis=0, tiled=True)
 
-    chosen = expert_ids[:, 0]
-    onehot = (chosen[:, None] == jnp.arange(EXPERTS, dtype=jnp.int32)[None, :]).astype(jnp.int32)
-    ranked = jnp.sum((jnp.cumsum(onehot, axis=0) - onehot) * onehot, axis=1)
-    slot_index = chosen * capacity + ranked
+    chosen = expert_ids
+    chosen_row = chosen.reshape(1, tok_rows)
+    earlier = (
+        jnp.arange(tok_rows, dtype=jnp.int32)[None, :] < jnp.arange(tok_rows, dtype=jnp.int32)[:, None]
+    )
+    ranked = jnp.sum(((chosen == chosen_row) & earlier).astype(jnp.int32), axis=1)
+    chosen = chosen[:, 0]
+    slot_index = chosen * CAP + ranked
     placing = (
-        jnp.arange(EXPERTS * capacity, dtype=jnp.int32)[:, None] == slot_index[None, :]
+        jnp.arange(EXPERTS * CAP, dtype=jnp.int32)[:, None] == slot_index[None, :]
     ).astype(jnp.bfloat16)
-    grad_slots = jnp.dot(placing, out_grad, preferred_element_type=jnp.float32).astype(jnp.bfloat16)
-    score_slots = jnp.dot(
-        placing, router_score[:, None], preferred_element_type=jnp.float32
-    ).astype(jnp.bfloat16)
-    sent_grad = jnp.repeat(grad_slots.reshape(EXPERTS, capacity, feature_cols), sharing, axis=0)
-    sent_score = jnp.repeat(score_slots.reshape(EXPERTS, capacity), sharing, axis=0)
-    arrived, arrived_score = (
-        lax.all_to_all(sent_grad, "ctx", split_axis=0, concat_axis=0, tiled=True),
-        lax.all_to_all(sent_score, "ctx", split_axis=0, concat_axis=0, tiled=True),
+    grad_slots = mm(placing, out_grad).astype(jnp.bfloat16).reshape(EXPERTS, CAP, FEAT)
+    column = jnp.arange(N_Y * N_Z * CAP_PAD, dtype=jnp.int32)
+    within = column % (N_Z * CAP_PAD)
+    member = column // (N_Z * CAP_PAD) * N_Z + within // CAP
+    column_slot = jnp.where(within < CHUNK, member // GROUP * CAP + within % CAP, -1)
+    pick = (slot_index[:, None] == column_slot[None, :]).astype(jnp.bfloat16)
+    d_hidden, stats, full_grad = expert_block(
+        grad_slots,
+        pick,
+        router_score.astype(jnp.float32)[:, None],
+        hidden_in,
+        norm_gain[None, :],
+        out_grad,
+        w_down[0],
+        gate_saved[0],
+        up_saved[0],
+        w_gate[0],
+        w_up[0],
     )
-    slot_grad = arrived.reshape(devices * capacity, feature_cols)
-    slot_score = arrived_score.reshape(devices * capacity).astype(jnp.float32)
-    down_local = w_down[0]
-    hidden_grad = lax.psum_scatter(
-        contract_last(down_local, slot_grad).astype(jnp.bfloat16),
-        "tp",
-        scatter_dimension=0,
-        tiled=True,
-    ).astype(jnp.float32)
-    gate_val = gate_saved[0].astype(jnp.float32)
-    up_val = up_saved[0].astype(jnp.float32)
-    activation, slope = silu_parts(gate_val)
-    scaled = hidden_grad * slot_score[None, :]
-    grad_gate = (scaled * up_val * slope).astype(jnp.bfloat16)
-    grad_up = (scaled * activation).astype(jnp.bfloat16)
-    router_part = jnp.sum(activation * up_val * hidden_grad, axis=0).astype(jnp.bfloat16)
-    gate_local = w_gate[0]
-    up_local = w_up[0]
-    running = contract_first(lax.all_gather(grad_gate, "tp", axis=0, tiled=True), gate_local)
-    back = running + contract_first(lax.all_gather(grad_up, "tp", axis=0, tiled=True), up_local)
-    back_parts = back.astype(jnp.bfloat16).reshape(devices, capacity, feature_cols)
-    returned, returned_router = (
-        lax.all_to_all(back_parts, "ctx", split_axis=0, concat_axis=0, tiled=True),
-        lax.all_to_all(
-            router_part.reshape(devices, capacity), "ctx", split_axis=0, concat_axis=0, tiled=True
-        ),
-    )
-    summed = jnp.sum(
-        returned.astype(jnp.float32).reshape(EXPERTS, sharing, capacity, feature_cols), axis=1
-    ).reshape(EXPERTS * capacity, feature_cols)
-    router_sum = jnp.sum(
-        returned_router.astype(jnp.float32).reshape(EXPERTS, sharing, capacity), axis=1
-    ).reshape(EXPERTS * capacity)
-    norm_grad = jnp.take(summed, slot_index, axis=0)
-    router_tok = jnp.take(router_sum, slot_index, axis=0)
-    hidden_val = hidden_in.astype(jnp.float32)
-    gain_val = norm_gain.astype(jnp.float32)[None, :]
-    squares_part = jnp.sum(hidden_val * hidden_val, axis=1)
-    cross_part = jnp.sum(hidden_val * gain_val * norm_grad, axis=1)
-    router_grad, sum_squares, cross_sum = lax.psum((router_tok, squares_part, cross_part), "tp")
-    inverse_rms = lax.rsqrt(sum_squares / D + EPSILON)[:, None]
-    d_hidden = (
-        out_grad.astype(jnp.float32)
-        + inverse_rms * gain_val * norm_grad
-        - hidden_val * inverse_rms * inverse_rms * inverse_rms * cross_sum[:, None] / D
-    ).astype(jnp.bfloat16)
-    full_grad = lax.all_gather(d_hidden, "tp", axis=1, tiled=True)
+    router_grad = stats[0]
     query_grad, key_grad, value_grad = attention(full_grad, queries, gathered)
     return (
         d_hidden,
         router_grad,
         query_grad,
-        key_grad.astype(jnp.bfloat16),
-        value_grad.astype(jnp.bfloat16),
+        key_grad,
+        value_grad,
     )
 
 

time: 385 us -> 228 us (0.59)
  waiting for transfers between devices: 184 us -> 0.02 us
  Pallas kernels: 69.8 us -> 198 us
  blocking collectives: 48.6 us -> 0 us
  starting transfers between devices: 27.7 us -> 0.04 us
  matrix products: 18.8 us -> 1.83 us
  other arithmetic: 14.1 us -> 5.44 us
    pallas_call x0 -> x1, Pallas kernels: none -> 126 us  [expert_block(): pl.pallas_call(expert_kernel, name='expert_block', out_shape=[jax.ShapeDt...]
    all_gather x3 -> x0, waiting for transfers between devices: 79.7 us -> none  [the longest x1 30.5 us: body(): lax.all_gather(grad_gate, 'tp', axis=0, tiled=True)]
    all_gather x1, waiting for transfers between devices: 45 us -> 0.01 us  [body(): gathered = lax.all_gather(shared_part, 'ctx', axis=0, tiled=True)]
    all_to_all x3 -> x0, waiting for transfers between devices: 36.1 us -> none  [the longest x1 31.4 us: body(): lax.all_to_all(back_parts, 'ctx', split_axis=0, concat_axis=0, tiled=True)]
    all_to_all x1 -> x0, blocking collectives: 35.2 us -> none  [body(): lax.all_to_all(sent_grad, 'ctx', split_axis=0, concat_axis=0, tiled=True)]
    all_to_all x3 -> x0, starting transfers between devices: 27.5 us -> none  [the longest x1 10 us: body(): lax.all_to_all(back_parts, 'ctx', split_axis=0, concat_axis=0, tiled=True)]
    reduce_scatter x1 -> x0, waiting for transfers between devices: 22 us -> none  [body(): lax.psum_scatter(contract_last(down_local, slot_grad).astype(jnp.bfloat16...]
    dot_general x5 -> x1, matrix products: 18.8 us -> 1.83 us  [mm(): return jnp.dot(a, b, preferred_element_type=jnp.float32)]
  transfers between devices with their start and end apart: 8 -> 1, of which waited for: 7 -> 0; matrix products, arithmetic and copies ran while one was open for 6% -> 4% of each run, Pallas kernels for 0% -> 56%
where the time goes in v2:
time: 228 us; the launch traced here: 227 us
  Pallas kernels  198 us (87%)
  between operations  14.1 us (6%)
  local copies, waits for them, and re-layouts  8.21 us (4%)
  other arithmetic  5.44 us (2%)
    pallas_call x1, Pallas kernels, expert_block(): pl.pallas_call(expert_kernel, name='expert_block', out_shape=[jax.ShapeDt...  126 us
    pallas_call x1, Pallas kernels, attention(): pl.pallas_call(attention_kernel, name='attention_grads', out_shape=[jax.S...  71.2 us
    unnamed x6, local copies, waits for them, and re-layouts  5.02 us
  transfers between devices with their start and end apart: 1, of which 0 were waited for; matrix products, arithmetic and copies ran while one was open for 4% of the time, Pallas kernels for 56%

profile of v2, /device:TPU:88, one launch (start us, length us, event | category | flops | bytes accessed | tf_op | source)
XLA Modules:
  0.0 227.2 jit_solution(11226285023467945118)
XLA Ops:
  7.2 0.0 all-gather.2.cloned.1.call-start
  7.2 1.7 fusion.4
  8.9 0.0 all-gather.2.cloned.1.call-update
  9.0 0.7 bitcast_convert_fusion
  9.6 0.7 copy.20.score_ref
  10.4 1.3 broadcast_in_dim.18.gain_ref
  11.6 0.9 convert_reduce_fusion
  12.5 0.7 multiply_add_fusion
  13.2 0.7 fusion.30
  13.9 0.8 compare_convert_fusion.pick_ref
  14.7 1.8 convolution_convert_fusion
  16.5 126.4 %expert_block.1 = (bf16[128,640]{1,0:T(8,128)(2,1)}, f32[8,128]{1,0:T(8,128)}, bf16[8,128,640]{2,1,0:T(8,128)(2,1)}) custom-call(bf16[8,24,640]{2,1,0:T(8,128)(2,1)} %bitcast.21, bf16[128,1024]{1,0:T(8,128)(2,1)} %compare_convert_fusion.pick_ref, f32[128,1]{1,0:T(8,128)} %copy.20.score_ref, bf16[128,640]{1,0:T(8,128)(2,1)} %hidden_ref.1, ...), custom_call_target="tpu_custom_call" | custom-call | flops 60000002048 | bytes 200000000 | tf_op jit(solution)/shard_map/expert_block/pallas_call | solution.py:619
  143.0 1.2 slice_bitcast_fusion
  144.1 0.0 all-gather.2.cloned.1.call-done.gathered_ref
  144.1 0.0 copy-start
  144.2 71.2 %attention_grads.1 = (bf16[128,640]{1,0:T(8,128)(2,1)}, bf16[128,128]{1,0:T(8,128)(2,1)}, bf16[128,128]{1,0:T(8,128)(2,1)}) custom-call(bf16[8,128,640]{2,1,0:T(8,128)(2,1)} %get-tuple-element.13.full_ref, bf16[128,640]{1,0:T(8,128)(2,1)} %q_ref.1, bf16[5120,896]{1,0:T(8,128)(2,1)} %all-gather.2.cloned.1.call-done.gathered_ref), custom_call_target="tpu_custom_call" | custom-call | flops 6000000000 | bytes 12000000 | tf_op jit(solution)/shard_map/attention_grads/pallas_call | solution.py:239
  215.3 0.0 copy-done
  215.3 0.7 copy.25
  216.0 1.6 copy.26
  217.6 1.4 copy.27
  219.0 1.4 copy.28
  (1 shorter events, 0.0 us)
Async XLA Ops:
  7.2 137.0 %all-gather.2.cloned.1.call-start = ((), (), s32[]{:S(2)}) async-start(), calls=%async_computation | async-start | bytes 9461760 | tf_op jit(solution)/shard_map/all_gather | solution.py:693
  144.1 71.2 %copy-start = (bf16[128,640]{1,0:T(8,128)(2,1)S(1)}, bf16[128,640]{1,0:T(8,128)(2,1)}, u32[]{:S(2)}) copy-start(bf16[128,640]{1,0:T(8,128)(2,1)} %get-tuple-element.22) | copy-start | bytes 491524
Sparse Core Ops, SparseCore 0:
  10.6 132.3 all-gather.1

commit v3 on v2

--- a/solution.py
+++ b/solution.py
@@ -42,94 +42,64 @@
 
 
 def attention_kernel(
-    full_ref, q_ref, gathered_ref, dq_ref, dk_ref, dv_ref,
-    w_buf, k_buf, v_buf, kt_buf, qt_buf, q5_buf, dt_buf, d5_buf,
-    s_buf, dp_buf, p16_buf, ds16_buf, m_buf, l_buf, r_buf, dqt_buf,
-    send_buf, recv_buf, total_buf, w_sem, kv_sem, send_sem, recv_sem,
+    full_ref, q5_ref, qt_ref, gathered_ref, dq_ref, dk_ref, dv_ref,
+    w_buf, k_buf, v_buf, kt_buf, dt_buf, d5_buf, s_buf, dp_buf, p16_buf, ds16_buf,
+    m_buf, l_buf, r_buf, f_buf, delta_buf, stat_buf, part_buf, dqt_buf, dk_acc, dv_acc,
+    dq_send, dq_recv, kv_send, kv_recv,
+    w_sem, kv_sem, d_send, d_recv, st_send, st_recv, pt_send, pt_recv,
+    q_send, q_recv, o_send, o_recv,
 ):
     me = lax.axis_index("ctx")
     tp = lax.axis_index("tp")
+    y, z = me // N_Z, me % N_Z
     scale = HD ** -0.5
-
+    factor = scale * LOG2E
+
+    def line(i):
+        return ((y + i) % N_Y) * N_Z + z
+
+    def pair_of(yk):
+        return (yk - y + N_Y) % N_Y
+
+    def remote(src, dst, send, recv, ctx):
+        return pltpu.make_async_remote_copy(
+            src_ref=src, dst_ref=dst, send_sem=send, recv_sem=recv,
+            device_id=(ctx, tp), device_id_type=MESH,
+        )
+
+    source_row = (y - z // 2 + N_Y) % N_Y
     barrier = pltpu.get_barrier_semaphore()
-
-    def greet(j, carry):
-        pl.semaphore_signal(barrier, inc=1, device_id=(j, tp), device_id_type=MESH)
-        return carry
-
-    lax.fori_loop(me + 1, N_CTX, greet, 0)
+    for i in range(1, N_Y):
+        pl.semaphore_signal(barrier, inc=1, device_id=(line(i), tp), device_id_type=MESH)
+    for i in range(N_Z):
+        peer = source_row * N_Z + i
+
+        @pl.when(peer != me)
+        def _():
+            pl.semaphore_signal(barrier, inc=1, device_id=(peer, tp), device_id_type=MESH)
 
     w_copy = pltpu.make_async_copy(gathered_ref.at[:, pl.ds(0, ROWS_Q)], w_buf, w_sem)
-
-    def kv_copies(j):
-        rows = pl.ds(pl.multiple_of(j * W_ROWS, 32), BLOCK)
-        own = pl.ds(pl.multiple_of(j * BLOCK, BLOCK), BLOCK)
-        return (
-            pltpu.make_async_copy(
-                gathered_ref.at[rows, pl.ds(ROWS_Q, HD)], k_buf.at[own], kv_sem.at[0, j]
-            ),
-            pltpu.make_async_copy(
-                gathered_ref.at[rows, pl.ds(ROWS_Q + HD, HD)], v_buf.at[own], kv_sem.at[1, j]
-            ),
-        )
-
-    def kv_start(j, carry):
-        for copy in kv_copies(j):
-            copy.start()
-        return carry
-
-    lax.fori_loop(0, N_CTX, kv_start, 0)
+    kv_copies = []
+    for yk in range(N_Y):
+        for h in range(2):
+            block = yk * N_Z + 2 * pair_of(yk) + h
+            rows = pl.ds(pl.multiple_of(block * W_ROWS, W_ROWS), BLOCK)
+            own = pl.ds(h * BLOCK, BLOCK)
+            kv_copies += [
+                pltpu.make_async_copy(
+                    gathered_ref.at[rows, pl.ds(ROWS_Q, HD)], k_buf.at[yk, own], kv_sem.at[0, yk, h]
+                ),
+                pltpu.make_async_copy(
+                    gathered_ref.at[rows, pl.ds(ROWS_Q + HD, HD)], v_buf.at[yk, own], kv_sem.at[1, yk, h]
+                ),
+            ]
     w_copy.start()
-
-    for h in range(GROUP_Q):
-        cols = slice(h * BLOCK, (h + 1) * BLOCK)
-        head = q_ref[:, cols]
-        q5_buf[cols, :] = head
-        qt_buf[:, cols] = head.astype(jnp.float32).T.astype(jnp.bfloat16)
-
-    def kv_wait(j, carry):
-        for copy in kv_copies(j):
-            copy.wait()
-        return carry
-
-    lax.fori_loop(0, N_CTX, kv_wait, 0)
-
-    last = me // 2
+    for copy in kv_copies:
+        copy.start()
     m_buf[...] = jnp.full(m_buf.shape, NEG, jnp.float32)
-    l_buf[...] = jnp.zeros_like(l_buf)
-    r_buf[...] = jnp.zeros_like(r_buf)
-    dqt_buf[...] = jnp.zeros_like(dqt_buf)
-
-    def pair_rows(p):
-        return pl.ds(pl.multiple_of(p * PAIR, PAIR), PAIR)
-
-    def fold(x, op):
-        total = x[0:8]
-        for i in range(1, x.shape[0] // 8):
-            total = op(total, x[8 * i : 8 * i + 8])
-        return total
-
-    def score_pass(p, masked):
-        keys = k_buf[pair_rows(p), :]
-        kt_buf[p] = keys.astype(jnp.float32).T.astype(jnp.bfloat16)
-        for n in range(GROUP_Q):
-            cols = slice(n * BLOCK, (n + 1) * BLOCK)
-            part = mm(keys, qt_buf[:, cols])
-            if masked:
-                key_pos = lax.broadcasted_iota(jnp.int32, (PAIR, BLOCK), 0)
-                row_pos = lax.broadcasted_iota(jnp.int32, (PAIR, BLOCK), 1)
-                part = jnp.where(key_pos <= row_pos + (me % 2) * BLOCK, part, NEG)
-            s_buf[p, :, cols] = part
-            m_buf[:, cols] = jnp.maximum(m_buf[:, cols], fold(part, jnp.maximum))
-
-    def score_step(p, carry):
-        score_pass(p, False)
-        return carry
-
-    lax.fori_loop(0, last, score_step, 0)
-    score_pass(last, True)
-    row_max = jnp.max(m_buf[...], axis=0, keepdims=True)
-    m_buf[...] = jnp.broadcast_to(row_max, m_buf.shape)
+    for ref in (l_buf, r_buf, dqt_buf, dk_acc, dv_acc):
+        ref[...] = jnp.zeros_like(ref)
+    pl.semaphore_wait(barrier, N_Y - 1 + N_Z - jnp.where(z < 2, 1, 0))
 
     w_copy.wait()
     dout = mm(full_ref[0], w_buf[0:FEAT, :])
@@ -137,105 +107,264 @@
         dout = dout + mm(full_ref[t], w_buf[t * FEAT : (t + 1) * FEAT, :])
     dout = dout.astype(jnp.bfloat16)
     for h in range(GROUP_Q):
-        cols = slice(h * BLOCK, (h + 1) * BLOCK)
-        head = dout[:, cols]
-        d5_buf[cols, :] = head
-        dt_buf[:, cols] = head.astype(jnp.float32).T.astype(jnp.bfloat16)
+        rows = slice(h * BLOCK, (h + 1) * BLOCK)
+        d5_buf[y, rows, :] = dout[:, rows]
+
+    def d_copy(i, owner):
+        return remote(d5_buf.at[owner], d5_buf.at[owner], d_send.at[i], d_recv.at[owner], line(i))
+
+    for i in range(1, N_Y):
+        d_copy(i, y).start()
+
+    for copy in kv_copies:
+        copy.wait()
+    for yk in range(N_Y):
+        kt_buf[yk] = k_buf[yk].astype(jnp.float32).T.astype(jnp.bfloat16)
+
+    def fold(x, op):
+        total = x[0:8]
+        for i in range(1, x.shape[0] // 8):
+            total = op(total, x[8 * i : 8 * i + 8])
+        return total
+
+    def partly(yk, step):
+        @pl.when(2 * pair_of(yk) <= z)
+        def _():
+            step()
 
     step_rows = 32
-
-    def prob_step(p, carry):
-        vals = v_buf[pair_rows(p), :]
-        dp_buf[p] = mm(vals, dt_buf[...])
-        top = m_buf[0:1, :]
-        l_now = l_buf[...]
-        r_now = r_buf[...]
-        for i in range(PAIR // step_rows):
-            rows = slice(i * step_rows, (i + 1) * step_rows)
-            e = jnp.exp2((s_buf[p, rows, :] - top) * (scale * LOG2E))
-            s_buf[p, rows, :] = e
-            l_now = l_now + fold(e, jnp.add)
-            r_now = r_now + fold(e * dp_buf[p, rows, :], jnp.add)
-        l_buf[...] = l_now
-        r_buf[...] = r_now
-        return carry
-
-    lax.fori_loop(0, last + 1, prob_step, 0)
-    row_sum = jnp.sum(l_buf[...], axis=0, keepdims=True)
-    inverse = 1.0 / row_sum
-    delta = jnp.sum(r_buf[...], axis=0, keepdims=True) * inverse
-
-    @pl.when(me > 0)
-    def _():
-        pl.semaphore_wait(barrier, me)
-
-    def sent(j):
-        return pltpu.make_async_remote_copy(
-            src_ref=send_buf.at[j],
-            dst_ref=recv_buf.at[me],
-            send_sem=send_sem.at[j],
-            recv_sem=recv_sem.at[me],
-            device_id=(j, tp),
-            device_id_type=MESH,
-        )
-
-    def grad_step(p, carry):
-        for i in range(PAIR // step_rows):
-            rows = slice(i * step_rows, (i + 1) * step_rows)
-            prob = s_buf[p, rows, :] * inverse
+    chunks = [slice(i * step_rows, (i + 1) * step_rows) for i in range(PAIR // step_rows)]
+
+    def scores(yq, yk, masked):
+        u = yq * N_Y + yk
+        s_buf[u] = mm(k_buf[yk], qt_ref[yq])
+        top = m_buf[yq]
+        for rows in chunks:
+            part = s_buf[u, rows, :]
+            if masked:
+                shape = (step_rows, ROWS_Q)
+                key_pos = lax.broadcasted_iota(jnp.int32, shape, 0) + rows.start
+                row_pos = lax.broadcasted_iota(jnp.int32, shape, 1) % BLOCK
+                part = jnp.where(key_pos <= row_pos + (z - 2 * pair_of(yk)) * BLOCK, part, NEG)
+                s_buf[u, rows, :] = part
+            top = jnp.maximum(top, fold(part, jnp.maximum))
+        m_buf[yq] = top
+
+    def exponents(yq, yk):
+        u = yq * N_Y + yk
+        top = stat_buf[y, pl.ds(yq, 1), :]
+        total = l_buf[yq]
+        for rows in chunks:
+            e = jnp.exp2((s_buf[u, rows, :] - top) * factor)
+            s_buf[u, rows, :] = e
+            total = total + fold(e, jnp.add)
+        l_buf[yq] = total
+
+    def each_query(yq, full_step, own_step):
+        def step(yk, carry):
+            full_step(yk)
+            return carry
+
+        lax.fori_loop(0, yq, step, 0)
+        partly(yq, own_step)
+
+    def score_row(yq, carry):
+        each_query(yq, lambda yk: scores(yq, yk, False), lambda: scores(yq, yq, True))
+        return carry
+
+    lax.fori_loop(0, N_Y, score_row, 0)
+    for yq in range(N_Y):
+        stat_buf[y, yq : yq + 1, :] = jnp.max(m_buf[yq], axis=0, keepdims=True)
+
+    def exponent_row(yq, carry):
+        each_query(yq, lambda yk: exponents(yq, yk), lambda: exponents(yq, yq))
+        return carry
+
+    lax.fori_loop(0, N_Y, exponent_row, 0)
+    for yq in range(N_Y):
+        stat_buf[y, N_Y + yq : N_Y + yq + 1, :] = jnp.sum(l_buf[yq], axis=0, keepdims=True)
+
+    def st_copy(i, owner):
+        return remote(
+            stat_buf.at[owner], stat_buf.at[owner], st_send.at[i], st_recv.at[owner], line(i)
+        )
+
+    for i in range(1, N_Y):
+        st_copy(i, y).start()
+
+    def prob_grads(yq, yk):
+        u = yq * N_Y + yk
+        dp_buf[u] = mm(v_buf[yk], dt_buf[yq])
+        total = r_buf[yq]
+        for rows in chunks:
+            total = total + fold(s_buf[u, rows, :] * dp_buf[u, rows, :], jnp.add)
+        r_buf[yq] = total
+
+    def prob_row(i, carry):
+        yq = (y + i) % N_Y
+
+        @pl.when(i > 0)
+        def _():
+            d_copy(i, yq).wait_recv()
+
+        for h in range(GROUP_Q):
+            rows = slice(h * BLOCK, (h + 1) * BLOCK)
+            dt_buf[yq, :, rows] = d5_buf[yq, rows, :].astype(jnp.float32).T.astype(jnp.bfloat16)
+        each_query(yq, lambda yk: prob_grads(yq, yk), lambda: prob_grads(yq, yq))
+        return carry
+
+    lax.fori_loop(0, N_Y, prob_row, 0)
+
+    for i in range(1, N_Y):
+        st_copy(i, (y + i) % N_Y).wait_recv()
+    top_all = stat_buf[0, 0:N_Y, :]
+    for t in range(1, N_Y):
+        top_all = jnp.maximum(top_all, stat_buf[t, 0:N_Y, :])
+    sum_all = jnp.zeros_like(top_all)
+    for t in range(N_Y):
+        sum_all = sum_all + stat_buf[t, N_Y : 2 * N_Y, :] * jnp.exp2(
+            (stat_buf[t, 0:N_Y, :] - top_all) * factor
+        )
+    share = jnp.exp2((stat_buf[y, 0:N_Y, :] - top_all) * factor) / sum_all
+    f_buf[0:N_Y, :] = share
+    part_buf[y] = jnp.zeros((8, ROWS_Q), jnp.float32)
+    for yq in range(N_Y):
+        part_buf[y, yq : yq + 1, :] = (
+            jnp.sum(r_buf[yq], axis=0, keepdims=True) * share[yq : yq + 1, :]
+        )
+
+    def pt_copy(i, owner):
+        return remote(
+            part_buf.at[owner], part_buf.at[owner], pt_send.at[i], pt_recv.at[owner], line(i)
+        )
+
+    for i in range(1, N_Y):
+        pt_copy(i, y).start()
+
+    def block_copy(which, yk, h):
+        return remote(
+            kv_send.at[which, 2 * yk + h],
+            kv_recv.at[which, z],
+            o_send.at[which, 2 * yk + h],
+            o_recv.at[which, z],
+            yk * N_Z + 2 * pair_of(yk) + h,
+        )
+
+    def give(which, yk, acc):
+        for h in range(2):
+            kv_send[which, 2 * yk + h] = acc[h * BLOCK : (h + 1) * BLOCK].astype(jnp.bfloat16)
+            owner = yk * N_Z + 2 * pair_of(yk) + h
+
+            @pl.when(owner != me)
+            def _():
+                block_copy(which, yk, h).start()
+
+            @pl.when(owner == me)
+            def _():
+                kv_recv[which, z] = kv_send[which, 2 * yk + h]
+
+    def value_grads(yq, yk):
+        u = yq * N_Y + yk
+        share_row = f_buf[pl.ds(yq, 1), :]
+        for rows in chunks:
+            prob = s_buf[u, rows, :] * share_row
+            s_buf[u, rows, :] = prob
             p16_buf[rows, :] = prob.astype(jnp.bfloat16)
-            ds16_buf[rows, :] = (prob * (dp_buf[p, rows, :] - delta)).astype(jnp.bfloat16)
+        dv_acc[yk] += mm(p16_buf[...], d5_buf[yq])
+
+    def each_key(yk, full_step, own_step):
+        def step(yq, carry):
+            full_step(yq)
+            return carry
+
+        partly(yk, own_step)
+        lax.fori_loop(yk + 1, N_Y, step, 0)
+
+    def value_row(yk, carry):
+        each_key(yk, lambda yq: value_grads(yq, yk), lambda: value_grads(yk, yk))
+        give(0, yk, dv_acc[yk])
+        return carry
+
+    lax.fori_loop(0, N_Y, value_row, 0)
+
+    for i in range(1, N_Y):
+        pt_copy(i, (y + i) % N_Y).wait_recv()
+    delta_buf[...] = part_buf[0] + part_buf[1] + part_buf[2] + part_buf[3]
+
+    def key_grads(yq, yk):
+        u = yq * N_Y + yk
+        delta = delta_buf[pl.ds(yq, 1), :]
+        for rows in chunks:
+            ds16_buf[rows, :] = (
+                s_buf[u, rows, :] * (dp_buf[u, rows, :] - delta)
+            ).astype(jnp.bfloat16)
         ds16 = ds16_buf[...]
-        dk = (mm(ds16, q5_buf[...]) * scale).astype(jnp.bfloat16)
-        dv = mm(p16_buf[...], d5_buf[...]).astype(jnp.bfloat16)
-        dqt_buf[...] += mm(kt_buf[p], ds16)
-        for half in range(2):
-            j = 2 * p + half
-            rows = slice(half * BLOCK, (half + 1) * BLOCK)
-            send_buf[j, 0:BLOCK, :] = dk[rows]
-            send_buf[j, BLOCK:PAIR, :] = dv[rows]
-
-            @pl.when(j < me)
-            def _():
-                sent(j).start()
-
-        return carry
-
-    lax.fori_loop(0, last + 1, grad_step, 0)
-
+        dk_acc[yk] += mm(ds16, q5_ref[yq])
+        dqt_buf[yq] += mm(kt_buf[yk], ds16)
+
+    def dq_copy(yq):
+        return remote(
+            dq_send.at[yq], dq_recv.at[y], q_send.at[yq], q_recv.at[y], yq * N_Z + z
+        )
+
+    def key_row(yk, carry):
+        each_key(yk, lambda yq: key_grads(yq, yk), lambda: key_grads(yk, yk))
+        give(1, yk, dk_acc[yk] * scale)
+        dq_send[yk] = (dqt_buf[yk] * scale).astype(jnp.bfloat16)
+
+        @pl.when(yk != y)
+        def _():
+            dq_copy(yk).start()
+
+        return carry
+
+    lax.fori_loop(0, N_Y, key_row, 0)
+
+    total = dq_send[y].astype(jnp.float32)
+    for i in range(1, N_Y):
+        peer = (y + i) % N_Y
+        remote(
+            dq_send.at[y], dq_recv.at[peer], q_send.at[y], q_recv.at[peer], line(i)
+        ).wait_recv()
+        total = total + dq_recv[peer].astype(jnp.float32)
     for h in range(GROUP_Q):
         cols = slice(h * BLOCK, (h + 1) * BLOCK)
-        dq_ref[:, cols] = (dqt_buf[:, cols].T * scale).astype(jnp.bfloat16)
-
-    total_buf[...] = send_buf[me].astype(jnp.float32)
-
-    def take(j, carry):
-        pltpu.make_async_remote_copy(
-            src_ref=send_buf.at[j],
-            dst_ref=recv_buf.at[j],
-            send_sem=send_sem.at[j],
-            recv_sem=recv_sem.at[j],
-            device_id=(j, tp),
-            device_id_type=MESH,
-        ).wait_recv()
-        total_buf[...] += recv_buf[j].astype(jnp.float32)
-        return carry
-
-    lax.fori_loop(me + 1, N_CTX, take, 0)
-    dk_ref[...] = total_buf[0:BLOCK, :].astype(jnp.bfloat16)
-    dv_ref[...] = total_buf[BLOCK:PAIR, :].astype(jnp.bfloat16)
-
-    def drain(j, carry):
-        sent(j).wait_send()
-        return carry
-
-    lax.fori_loop(0, me, drain, 0)
-
-
-def attention(full_grad, queries, gathered):
-    pairs = N_CTX // 2
+        dq_ref[:, cols] = total[:, cols].T.astype(jnp.bfloat16)
+
+    for which, out_ref in ((0, dv_ref), (1, dk_ref)):
+        total = jnp.zeros((BLOCK, HD), jnp.float32)
+        for i in range(N_Z):
+            peer = source_row * N_Z + i
+
+            @pl.when(peer != me)
+            def _():
+                remote(
+                    kv_send.at[which, 0], kv_recv.at[which, i], o_send.at[which, 0],
+                    o_recv.at[which, i], peer,
+                ).wait_recv()
+
+            total = total + kv_recv[which, i].astype(jnp.float32)
+        out_ref[...] = total.astype(jnp.bfloat16)
+
+    for i in range(1, N_Y):
+        d_copy(i, y).wait_send()
+        st_copy(i, y).wait_send()
+        pt_copy(i, y).wait_send()
+        dq_copy((y + i) % N_Y).wait_send()
+    for which in range(2):
+        for yk in range(N_Y):
+            for h in range(2):
+
+                @pl.when(yk * N_Z + 2 * pair_of(yk) + h != me)
+                def _():
+                    block_copy(which, yk, h).wait_send()
+
+
+def attention(full_grad, q5, qt, gathered):
     bf, f32 = jnp.bfloat16, jnp.float32
     vmem = pl.BlockSpec(memory_space=pltpu.VMEM)
+    dma = pltpu.SemaphoreType.DMA
+    units = N_Y * N_Y
     return pl.pallas_call(
         attention_kernel,
         name="attention_grads",
@@ -244,32 +373,40 @@
             jax.ShapeDtypeStruct((BLOCK, HD), bf),
             jax.ShapeDtypeStruct((BLOCK, HD), bf),
         ],
-        in_specs=[vmem, vmem, pl.BlockSpec(memory_space=pl.ANY)],
+        in_specs=[vmem, vmem, vmem, pl.BlockSpec(memory_space=pl.ANY)],
         out_specs=[vmem, vmem, vmem],
         scratch_shapes=[
             pltpu.VMEM((D, ROWS_Q), bf),
-            pltpu.VMEM((N_CTX * BLOCK, HD), bf),
-            pltpu.VMEM((N_CTX * BLOCK, HD), bf),
-            pltpu.VMEM((pairs, HD, PAIR), bf),
-            pltpu.VMEM((HD, ROWS_Q), bf),
-            pltpu.VMEM((ROWS_Q, HD), bf),
-            pltpu.VMEM((HD, ROWS_Q), bf),
-            pltpu.VMEM((ROWS_Q, HD), bf),
-            pltpu.VMEM((pairs, PAIR, ROWS_Q), f32),
-            pltpu.VMEM((pairs, PAIR, ROWS_Q), f32),
+            pltpu.VMEM((N_Y, PAIR, HD), bf),
+            pltpu.VMEM((N_Y, PAIR, HD), bf),
+            pltpu.VMEM((N_Y, HD, PAIR), bf),
+            pltpu.VMEM((N_Y, HD, ROWS_Q), bf),
+            pltpu.VMEM((N_Y, ROWS_Q, HD), bf),
+            pltpu.VMEM((units, PAIR, ROWS_Q), f32),
+            pltpu.VMEM((units, PAIR, ROWS_Q), f32),
             pltpu.VMEM((PAIR, ROWS_Q), bf),
             pltpu.VMEM((PAIR, ROWS_Q), bf),
+            pltpu.VMEM((N_Y, 8, ROWS_Q), f32),
+            pltpu.VMEM((N_Y, 8, ROWS_Q), f32),
+            pltpu.VMEM((N_Y, 8, ROWS_Q), f32),
             pltpu.VMEM((8, ROWS_Q), f32),
             pltpu.VMEM((8, ROWS_Q), f32),
-            pltpu.VMEM((8, ROWS_Q), f32),
-            pltpu.VMEM((HD, ROWS_Q), f32),
-            pltpu.VMEM((N_CTX, PAIR, HD), bf),
-            pltpu.VMEM((N_CTX, PAIR, HD), bf),
-            pltpu.VMEM((PAIR, HD), f32),
-            pltpu.SemaphoreType.DMA,
-            pltpu.SemaphoreType.DMA((2, N_CTX)),
-            pltpu.SemaphoreType.DMA((N_CTX,)),
-            pltpu.SemaphoreType.DMA((N_CTX,)),
+            pltpu.VMEM((N_Y, 8, ROWS_Q), f32),
+            pltpu.VMEM((N_Y, 8, ROWS_Q), f32),
+            pltpu.VMEM((N_Y, HD, ROWS_Q), f32),
+            pltpu.VMEM((N_Y, PAIR, HD), f32),
+            pltpu.VMEM((N_Y, PAIR, HD), f32),
+            pltpu.VMEM((N_Y, HD, ROWS_Q), bf),
+            pltpu.VMEM((N_Y, HD, ROWS_Q), bf),
+            pltpu.VMEM((2, 2 * N_Y, BLOCK, HD), bf),
+            pltpu.VMEM((2, N_Z, BLOCK, HD), bf),
+            dma,
+            dma((2, N_Y, 2)),
+            dma((N_Y,)), dma((N_Y,)),
+            dma((N_Y,)), dma((N_Y,)),
+            dma((N_Y,)), dma((N_Y,)),
+            dma((N_Y,)), dma((N_Y,)),
+            dma((2, 2 * N_Y)), dma((2, N_Z)),
         ],
         cost_estimate=pl.CostEstimate(
             flops=6_000_000_000, bytes_accessed=12_000_000, transcendentals=3_000_000
@@ -277,7 +414,7 @@
         compiler_params=pltpu.CompilerParams(
             collective_id=4, has_side_effects=True, vmem_limit_bytes=56 * 2**20
         ),
-    )(full_grad, queries, gathered)
+    )(full_grad, q5, qt, gathered)
 
 
 def dot_nt(a, b):
@@ -285,13 +422,13 @@
 
 
 def expert_kernel(
-    slots_ref, pick_ref, score_ref, hidden_ref, gain_ref, grad_ref,
+    slots_ref, pick_ref, score_ref, hidden_ref, gain_ref, grad_ref, q_ref,
     down_ref, gate_ref, up_ref, wg_ref, wu_ref,
-    dh_ref, stat_ref, full_ref,
+    dh_ref, stat_ref, full_ref, q5_ref, qt_ref,
     down, wg, wu, recv_d, flat, slots, own, sib_out, sib_in, x_out, x_in,
-    act_buf, slope_buf, prod_buf, ag, acc, back, ret, picked, stats, square, full,
+    act_buf, slope_buf, prod_buf, ag, acc, back, ret, picked, stats, square, full, q5,
     w_sem, d_send, d_recv, s_send, s_recv, x_send, x_recv, ax_send, ax_recv,
-    as_send, as_recv, b_send, b_recv, t_send, t_recv, fx_send, fx_recv, fs_send, fs_recv,
+    as_send, as_recv, b_send, b_recv, t_send, t_recv, fx_send, fx_recv, fs_send, fs_recv, q_send, q_recv,
 ):
     me = lax.axis_index("ctx")
     tp = lax.axis_index("tp")
@@ -353,6 +490,25 @@
 
         lax.fori_loop(1 if dy == 0 else 0, N_Z, send_step, 0)
     recv_d[me] = slots_ref[me // GROUP]
+
+    def q_copy(i, owner):
+        ctx = ((y + i) % N_Y) * N_Z + z
+        return remote(q5.at[owner], q5.at[owner], q_send.at[i], q_recv.at[owner], ctx, tp)
+
+    for h in range(GROUP_Q):
+        heads = slice(h * BLOCK, (h + 1) * BLOCK)
+        q5[y, heads, :] = q_ref[:, heads]
+    for i in range(1, N_Y):
+        q_copy(i, y).start()
+
+    def turn_queries():
+        for i in range(1, N_Y):
+            q_copy(i, (y + i) % N_Y).wait_recv()
+        q5_ref[...] = q5[...]
+        for r in range(N_Y):
+            for h in range(GROUP_Q):
+                heads = slice(h * BLOCK, (h + 1) * BLOCK)
+                qt_ref[r, :, heads] = q5[r, heads, :].astype(jnp.float32).T.astype(jnp.bfloat16)
 
     def chunk_rows(ch):
         start = ((y + ROW_ORDER[ch]) % N_Y) * CHUNK
@@ -500,6 +656,7 @@
     stage2(2)
     stage2(3)
     prepare()
+    turn_queries()
     w_copies[1].wait()
     w_copies[2].wait()
     for ch in range(N_Y):
@@ -604,13 +761,15 @@
         for i in range(3):
             x_copy(i, ch).wait_send()
             ag_out(i, ch).wait_send()
+    for i in range(1, N_Y):
+        q_copy(i, y).wait_send()
     for i in range(3):
         full_out(i).wait_send()
     for i in range(4):
         full_share(tp, i).wait_send()
 
 
-def expert_block(slots, pick, score, hidden, gain, grad, down, gate, up, wg, wu):
+def expert_block(slots, pick, score, hidden, gain, grad, queries, down, gate, up, wg, wu):
     bf, f32 = jnp.bfloat16, jnp.float32
     vmem = pl.BlockSpec(memory_space=pltpu.VMEM)
     hbm = pl.BlockSpec(memory_space=pl.ANY)
@@ -623,9 +782,11 @@
             jax.ShapeDtypeStruct((BLOCK, FEAT), bf),
             jax.ShapeDtypeStruct((8, BLOCK), f32),
             jax.ShapeDtypeStruct((N_TP, BLOCK, FEAT), bf),
+            jax.ShapeDtypeStruct((N_Y, ROWS_Q, HD), bf),
+            jax.ShapeDtypeStruct((N_Y, HD, ROWS_Q), bf),
         ],
-        in_specs=[vmem] * 6 + [hbm, vmem, vmem, hbm, hbm],
-        out_specs=[vmem] * 3,
+        in_specs=[vmem] * 7 + [hbm, vmem, vmem, hbm, hbm],
+        out_specs=[vmem] * 5,
         scratch_shapes=[
             pltpu.VMEM((FF_GRP, FEAT), bf),
             pltpu.VMEM((FEAT, FF_GRP), bf),
@@ -649,6 +810,7 @@
             pltpu.VMEM((N_TP, 8, BLOCK), f32),
             pltpu.VMEM((BLOCK, HD), f32),
             pltpu.VMEM((N_TP, BLOCK, FEAT), bf),
+            pltpu.VMEM((N_Y, ROWS_Q, HD), bf),
             dma((3,)),
             dma((N_CTX,)), dma((N_CTX,)),
             dma((4, N_Y)), dma((4, N_Y)),
@@ -659,6 +821,7 @@
             dma((N_TP,)), dma((N_TP,)),
             dma((3,)), dma((3,)),
             dma((4,)), dma((4,)),
+            dma((N_Y,)), dma((N_Y,)),
         ],
         cost_estimate=pl.CostEstimate(
             flops=60_000_000_000, bytes_accessed=200_000_000, transcendentals=3_000_000
@@ -666,7 +829,7 @@
         compiler_params=pltpu.CompilerParams(
             collective_id=3, has_side_effects=True, vmem_limit_bytes=56 * 2**20
         ),
-    )(slots, pick, score, hidden, gain, grad, down, gate, up, wg, wu)
+    )(slots, pick, score, hidden, gain, grad, queries, down, gate, up, wg, wu)
 
 
 def body(
@@ -709,13 +872,14 @@
     member = column // (N_Z * CAP_PAD) * N_Z + within // CAP
     column_slot = jnp.where(within < CHUNK, member // GROUP * CAP + within % CAP, -1)
     pick = (slot_index[:, None] == column_slot[None, :]).astype(jnp.bfloat16)
-    d_hidden, stats, full_grad = expert_block(
+    d_hidden, stats, full_grad, q5, qt = expert_block(
         grad_slots,
         pick,
         router_score.astype(jnp.float32)[:, None],
         hidden_in,
         norm_gain[None, :],
         out_grad,
+        queries,
         w_down[0],
         gate_saved[0],
         up_saved[0],
@@ -723,7 +887,7 @@
         w_up[0],
     )
     router_grad = stats[0]
-    query_grad, key_grad, value_grad = attention(full_grad, queries, gathered)
+    query_grad, key_grad, value_grad = attention(full_grad, q5, qt, gathered)
     return (
         d_hidden,
         router_grad,

time: 228 us -> 204 us (0.89)
  Pallas kernels: 198 us -> 172 us
    pallas_call x1, Pallas kernels: 71.2 us -> 44.5 us  [attention(): pl.pallas_call(attention_kernel, name='attention_grads', out_shape=[jax.S...]
  transfers between devices with their start and end apart: 1 -> 1, of which waited for: 0 -> 0; matrix products, arithmetic and copies ran while one was open for 4% -> 4% of each run, Pallas kernels for 56% -> 63%
where the time goes in v3:
time: 204 us; the launch traced here: 201 us
  Pallas kernels  172 us (84%)
  between operations  14.1 us (7%)
  local copies, waits for them, and re-layouts  8.21 us (4%)
  other arithmetic  5.41 us (3%)
    pallas_call x1, Pallas kernels, expert_block(): pl.pallas_call(expert_kernel, name='expert_block', out_shape=[jax.ShapeDt...  127 us
    pallas_call x1, Pallas kernels, attention(): pl.pallas_call(attention_kernel, name='attention_grads', out_shape=[jax.S...  44.5 us
    unnamed x6, local copies, waits for them, and re-layouts  5.02 us
  transfers between devices with their start and end apart: 1, of which 0 were waited for; matrix products, arithmetic and copies ran while one was open for 4% of the time, Pallas kernels for 63%

profile of v3, /device:TPU:88, one launch (start us, length us, event | category | flops | bytes accessed | tf_op | source)
XLA Modules:
  0.0 201.2 jit_solution(8541833325954320925)
XLA Ops:
  7.2 0.0 all-gather.2.cloned.1.call-start
  7.2 1.7 fusion.4
  8.9 0.0 all-gather.2.cloned.1.call-update
  8.9 0.7 bitcast_convert_fusion
  9.6 0.7 copy.20.score_ref
  10.3 1.3 broadcast_in_dim.18.gain_ref
  11.6 0.9 convert_reduce_fusion
  12.5 0.7 multiply_add_fusion
  13.2 0.7 fusion.30
  13.9 0.8 compare_convert_fusion.pick_ref
  14.7 1.8 convolution_convert_fusion
  16.5 127.1 %expert_block.1 = (bf16[128,640]{1,0:T(8,128)(2,1)}, f32[8,128]{1,0:T(8,128)}, bf16[8,128,640]{2,1,0:T(8,128)(2,1)}, bf16[4,640,128]{2,1,0:T(8,128)(2,1)}, bf16[4,128,640]{2,1,0:T(8,128)(2,1)}) custom-call(bf16[8,24,640]{2,1,0:T(8,128)(2,1)} %bitcast.21, bf16[128,1024]{1,0:T(8,128)(2,1)} %compare_convert_fusion.pick_ref, f32[128,1]{1,0:T(8,128)} %copy.20.score_ref, ...), custom_call_target="tpu_custom_call" | custom-call | flops 60000002048 | bytes 200000000 | tf_op jit(solution)/shard_map/expert_block/pallas_call | solution.py:778
  143.6 1.2 slice_bitcast_fusion
  144.8 0.0 all-gather.2.cloned.1.call-done.gathered_ref
  144.8 0.0 copy-start
  144.8 44.5 %attention_grads.1 = (bf16[128,640]{1,0:T(8,128)(2,1)}, bf16[128,128]{1,0:T(8,128)(2,1)}, bf16[128,128]{1,0:T(8,128)(2,1)}) custom-call(bf16[8,128,640]{2,1,0:T(8,128)(2,1)} %get-tuple-element.15.full_ref, bf16[4,640,128]{2,1,0:T(8,128)(2,1)} %get-tuple-element.16.q5_ref, bf16[4,128,640]{2,1,0:T(8,128)(2,1)} %get-tuple-element.17.qt_ref, ...), custom_call_target="tpu_custom_call" | custom-call | flops 6000000000 | bytes 12000000 | tf_op jit(solution)/shard_map/attention_grads/pallas_call | solution.py:368
  189.4 0.0 copy-done
  189.4 0.7 copy.25
  190.0 1.6 copy.26
  191.6 1.4 copy.27
  193.0 1.4 copy.28
  (1 shorter events, 0.0 us)
Async XLA Ops:
  7.2 137.7 %all-gather.2.cloned.1.call-start = ((), (), s32[]{:S(2)}) async-start(), calls=%async_computation | async-start | bytes 9461760 | tf_op jit(solution)/shard_map/all_gather | solution.py:856
  144.8 44.5 %copy-start = (bf16[128,640]{1,0:T(8,128)(2,1)S(1)}, bf16[128,640]{1,0:T(8,128)(2,1)}, u32[]{:S(2)}) copy-start(bf16[128,640]{1,0:T(8,128)(2,1)} %get-tuple-element.26) | copy-start | bytes 491524
Sparse Core Ops, SparseCore 0:
  10.6 132.3 all-gather.1

commit v4 on v3

--- a/solution.py
+++ b/solution.py
@@ -15,7 +15,6 @@
 BLOCK = 128
 PAIR = 2 * BLOCK
 ROWS_Q = GROUP_Q * BLOCK
-W_ROWS = 160
 N_Y, N_Z, N_X, N_TP = 4, 8, 4, 8
 GROUP = N_CTX // EXPERTS
 CAP = 24
@@ -25,7 +24,7 @@
 FEAT = D // N_TP
 FF_GRP = 2048
 FF_DEV = FF_GRP // N_TP
-ROW_ORDER = (0, 1, 3, 2)
+PAIR_ROWS = 2 * CHUNK
 MESH = pl.DeviceIdType.MESH
 EPSILON = 1e-05
 NEG = -1e30
@@ -42,11 +41,11 @@
 
 
 def attention_kernel(
-    full_ref, q5_ref, qt_ref, gathered_ref, dq_ref, dk_ref, dv_ref,
+    full_ref, q5_ref, qt_ref, kv_ref, gathered_ref, out_ref,
     w_buf, k_buf, v_buf, kt_buf, dt_buf, d5_buf, s_buf, dp_buf, p16_buf, ds16_buf,
     m_buf, l_buf, r_buf, f_buf, delta_buf, stat_buf, part_buf, dqt_buf, dk_acc, dv_acc,
     dq_send, dq_recv, kv_send, kv_recv,
-    w_sem, kv_sem, d_send, d_recv, st_send, st_recv, pt_send, pt_recv,
+    w_sem, d_send, d_recv, st_send, st_recv, pt_send, pt_recv,
     q_send, q_recv, o_send, o_recv,
 ):
     me = lax.axis_index("ctx")
@@ -78,28 +77,17 @@
         def _():
             pl.semaphore_signal(barrier, inc=1, device_id=(peer, tp), device_id_type=MESH)
 
-    w_copy = pltpu.make_async_copy(gathered_ref.at[:, pl.ds(0, ROWS_Q)], w_buf, w_sem)
-    kv_copies = []
+    w_copy = pltpu.make_async_copy(gathered_ref, w_buf, w_sem)
+    w_copy.start()
     for yk in range(N_Y):
         for h in range(2):
-            block = yk * N_Z + 2 * pair_of(yk) + h
-            rows = pl.ds(pl.multiple_of(block * W_ROWS, W_ROWS), BLOCK)
-            own = pl.ds(h * BLOCK, BLOCK)
-            kv_copies += [
-                pltpu.make_async_copy(
-                    gathered_ref.at[rows, pl.ds(ROWS_Q, HD)], k_buf.at[yk, own], kv_sem.at[0, yk, h]
-                ),
-                pltpu.make_async_copy(
-                    gathered_ref.at[rows, pl.ds(ROWS_Q + HD, HD)], v_buf.at[yk, own], kv_sem.at[1, yk, h]
-                ),
-            ]
-    w_copy.start()
-    for copy in kv_copies:
-        copy.start()
+            rows = slice(h * BLOCK, (h + 1) * BLOCK)
+            k_buf[yk, rows, :] = kv_ref[yk, h, 0]
+            v_buf[yk, rows, :] = kv_ref[yk, h, 1]
+        kt_buf[yk] = k_buf[yk].astype(jnp.float32).T.astype(jnp.bfloat16)
     m_buf[...] = jnp.full(m_buf.shape, NEG, jnp.float32)
     for ref in (l_buf, r_buf, dqt_buf, dk_acc, dv_acc):
         ref[...] = jnp.zeros_like(ref)
-    pl.semaphore_wait(barrier, N_Y - 1 + N_Z - jnp.where(z < 2, 1, 0))
 
     w_copy.wait()
     dout = mm(full_ref[0], w_buf[0:FEAT, :])
@@ -110,16 +98,13 @@
         rows = slice(h * BLOCK, (h + 1) * BLOCK)
         d5_buf[y, rows, :] = dout[:, rows]
 
+    pl.semaphore_wait(barrier, N_Y - 1 + N_Z - jnp.where(z < 2, 1, 0))
+
     def d_copy(i, owner):
         return remote(d5_buf.at[owner], d5_buf.at[owner], d_send.at[i], d_recv.at[owner], line(i))
 
     for i in range(1, N_Y):
         d_copy(i, y).start()
-
-    for copy in kv_copies:
-        copy.wait()
-    for yk in range(N_Y):
-        kt_buf[yk] = k_buf[yk].astype(jnp.float32).T.astype(jnp.bfloat16)
 
     def fold(x, op):
         total = x[0:8]
@@ -329,9 +314,9 @@
         total = total + dq_recv[peer].astype(jnp.float32)
     for h in range(GROUP_Q):
         cols = slice(h * BLOCK, (h + 1) * BLOCK)
-        dq_ref[:, cols] = total[:, cols].T.astype(jnp.bfloat16)
-
-    for which, out_ref in ((0, dv_ref), (1, dk_ref)):
+        out_ref[:, cols] = total[:, cols].T.astype(jnp.bfloat16)
+
+    for which, first in ((0, ROWS_Q + HD), (1, ROWS_Q)):
         total = jnp.zeros((BLOCK, HD), jnp.float32)
         for i in range(N_Z):
             peer = source_row * N_Z + i
@@ -344,7 +329,7 @@
                 ).wait_recv()
 
             total = total + kv_recv[which, i].astype(jnp.float32)
-        out_ref[...] = total.astype(jnp.bfloat16)
+        out_ref[:, first : first + HD] = total.astype(jnp.bfloat16)
 
     for i in range(1, N_Y):
         d_copy(i, y).wait_send()
@@ -360,7 +345,7 @@
                     block_copy(which, yk, h).wait_send()
 
 
-def attention(full_grad, q5, qt, gathered):
+def attention(full_grad, q5, qt, kv, gathered):
     bf, f32 = jnp.bfloat16, jnp.float32
     vmem = pl.BlockSpec(memory_space=pltpu.VMEM)
     dma = pltpu.SemaphoreType.DMA
@@ -368,13 +353,9 @@
     return pl.pallas_call(
         attention_kernel,
         name="attention_grads",
-        out_shape=[
-            jax.ShapeDtypeStruct((BLOCK, ROWS_Q), bf),
-            jax.ShapeDtypeStruct((BLOCK, HD), bf),
-            jax.ShapeDtypeStruct((BLOCK, HD), bf),
-        ],
-        in_specs=[vmem, vmem, vmem, pl.BlockSpec(memory_space=pl.ANY)],
-        out_specs=[vmem, vmem, vmem],
+        out_shape=jax.ShapeDtypeStruct((BLOCK, ROWS_Q + 2 * HD), bf),
+        in_specs=[vmem, vmem, vmem, vmem, pl.BlockSpec(memory_space=pl.ANY)],
+        out_specs=vmem,
         scratch_shapes=[
             pltpu.VMEM((D, ROWS_Q), bf),
             pltpu.VMEM((N_Y, PAIR, HD), bf),
@@ -401,7 +382,6 @@
             pltpu.VMEM((2, 2 * N_Y, BLOCK, HD), bf),
             pltpu.VMEM((2, N_Z, BLOCK, HD), bf),
             dma,
-            dma((2, N_Y, 2)),
             dma((N_Y,)), dma((N_Y,)),
             dma((N_Y,)), dma((N_Y,)),
             dma((N_Y,)), dma((N_Y,)),
@@ -414,7 +394,7 @@
         compiler_params=pltpu.CompilerParams(
             collective_id=4, has_side_effects=True, vmem_limit_bytes=56 * 2**20
         ),
-    )(full_grad, q5, qt, gathered)
+    )(full_grad, q5, qt, kv, gathered)
 
 
 def dot_nt(a, b):
@@ -422,13 +402,15 @@
 
 
 def expert_kernel(
-    slots_ref, pick_ref, score_ref, hidden_ref, gain_ref, grad_ref, q_ref,
+    pack_ref, hidden_ref, grad_ref, q_ref, key_ref, value_ref,
     down_ref, gate_ref, up_ref, wg_ref, wu_ref,
-    dh_ref, stat_ref, full_ref, q5_ref, qt_ref,
-    down, wg, wu, recv_d, flat, slots, own, sib_out, sib_in, x_out, x_in,
-    act_buf, slope_buf, prod_buf, ag, acc, back, ret, picked, stats, square, full, q5,
-    w_sem, d_send, d_recv, s_send, s_recv, x_send, x_recv, ax_send, ax_recv,
-    as_send, as_recv, b_send, b_recv, t_send, t_recv, fx_send, fx_recv, fs_send, fs_recv, q_send, q_recv,
+    dh_ref, stat_ref, full_ref, q5_ref, qt_ref, kv_ref,
+    down, wg, wu, slots_out, recv_d, flat, slots, own, sib_out, sib_in, x_out, x_in,
+    prod_buf, gu, hid, acc, back, ret, rt_out, rt_in, terms, pick, picked, stats, square, full, q5, kv_out, kv,
+    w_sem, d_send, d_recv, s_send, s_recv, x_send, x_recv, gx_send, gx_recv,
+    gf_send, gf_recv, gs_send, gs_recv, ax_send, ax_recv, af_send, af_recv,
+    as_send, as_recv, b_send, b_recv, t_send, t_recv, fx_send, fx_recv, fs_send, fs_recv,
+    q_send, q_recv, k_send, k_recv, r_send, r_recv,
 ):
     me = lax.axis_index("ctx")
     tp = lax.axis_index("tp")
@@ -436,6 +418,8 @@
     x, k = tp // 2, tp % 2
     sibling = 2 * x + (1 - k)
     far = (2, 1, 3)
+    near = (1, 3)
+    rows_by_chunk = (y, y + 1 - 2 * (y % 2), (y + 2) % N_Y, N_Y - 1 - y)
 
     def chip(dx):
         return (x + dx) % N_X
@@ -445,6 +429,23 @@
             src_ref=src, dst_ref=dst, send_sem=send, recv_sem=recv,
             device_id=(ctx, peer), device_id_type=MESH,
         )
+
+    barrier = pltpu.get_barrier_semaphore()
+
+    def greet_ctx(i, carry):
+        pl.semaphore_signal(
+            barrier, inc=1, device_id=((me + i) % N_CTX, tp), device_id_type=MESH
+        )
+        return carry
+
+    def greet_tp(i, carry):
+        pl.semaphore_signal(
+            barrier, inc=1, device_id=(me, (tp + i) % N_TP), device_id_type=MESH
+        )
+        return carry
+
+    lax.fori_loop(1, N_CTX, greet_ctx, 0)
+    lax.fori_loop(1, N_TP, greet_tp, 0)
 
     w_copies = [
         pltpu.make_async_copy(down_ref, down, w_sem.at[0]),
@@ -454,52 +455,162 @@
     for copy in w_copies:
         copy.start()
 
-    barrier = pltpu.get_barrier_semaphore()
-
-    def greet_ctx(i, carry):
-        pl.semaphore_signal(
-            barrier, inc=1, device_id=((me + i) % N_CTX, tp), device_id_type=MESH
-        )
-        return carry
-
-    def greet_tp(i, carry):
-        pl.semaphore_signal(
-            barrier, inc=1, device_id=(me, (tp + i) % N_TP), device_id_type=MESH
-        )
-        return carry
-
-    lax.fori_loop(1, N_CTX, greet_ctx, 0)
-    lax.fori_loop(1, N_TP, greet_tp, 0)
+    def turn(row):
+        return jnp.broadcast_to(row, (BLOCK, BLOCK)).T
+
+    ids = jnp.broadcast_to(pack_ref[0:1, :], (BLOCK, BLOCK))
+    ids_t = ids.T
+    sub = lax.broadcasted_iota(jnp.int32, (BLOCK, BLOCK), 0)
+    lan = lax.broadcasted_iota(jnp.int32, (BLOCK, BLOCK), 1)
+    before = jnp.where((ids == ids_t) & (sub < lan), 1.0, 0.0)
+    slot_row = pack_ref[0:1, :] * CAP + jnp.sum(before, axis=0, keepdims=True)
+    slot_ids = lax.broadcasted_iota(jnp.int32, (EXPERTS * CAP, BLOCK), 0).astype(jnp.float32)
+    placing = jnp.where(slot_ids == slot_row, 1.0, 0.0).astype(jnp.bfloat16)
+    placed = mm(placing, grad_ref[...])
+    for e in range(EXPERTS):
+        slots_out[e] = placed[e * CAP : (e + 1) * CAP].astype(jnp.bfloat16)
+    slot_col = turn(slot_row)[:, 0:1]
+    number = lax.broadcasted_iota(jnp.int32, (8, N_Y * N_Z * CAP_PAD), 1).astype(jnp.float32)
+    device_row = jnp.floor((number + 0.5) / (N_Z * CAP_PAD))
+    within = number - device_row * (N_Z * CAP_PAD)
+    device = jnp.floor((within + 0.5) / CAP)
+    column = (
+        jnp.floor((device_row * N_Z + device + 0.5) / GROUP) * CAP + within - device * CAP
+    )
+    column = jnp.where(within < CHUNK, column, -1.0)
+    pick[...] = jnp.where(column[0:1, :] == slot_col, 1.0, 0.0).astype(jnp.bfloat16)
+    score = turn(pack_ref[1:2, :])[:, 0:1]
+    gain_val = jnp.concatenate([pack_ref[2 + h : 3 + h, :] for h in range(GROUP_Q)], axis=1)
+
+    gate = gate_ref[...].astype(jnp.float32).T
+    up = up_ref[...].astype(jnp.float32).T
+    act, slope = silu_parts(gate)
+    gu[tp, :, 0:FF_DEV] = (up * slope).astype(jnp.bfloat16)
+    gu[tp, :, FF_DEV : 2 * FF_DEV] = act.astype(jnp.bfloat16)
+    prod_buf[...] = act * up
+    spot = lax.broadcasted_iota(jnp.int32, (CHUNK, BLOCK), 0).astype(jnp.float32)
+    spot = spot - CAP * jnp.floor((spot + 0.5) / CAP)
+    spot_is = jnp.where(
+        spot == lax.broadcasted_iota(jnp.int32, (CHUNK, BLOCK), 1).astype(jnp.float32), 1.0, 0.0
+    )
+    own_sub = lax.broadcasted_iota(jnp.int32, (N_Z, CHUNK), 0) * CAP
+    own_lan = lax.broadcasted_iota(jnp.int32, (N_Z, CHUNK), 1)
+    owner_is = jnp.where((own_lan >= own_sub) & (own_lan < own_sub + CAP), 1.0, 0.0)
+    owner_is = owner_is.astype(jnp.bfloat16)
+    for h in range(GROUP_Q):
+        heads = slice(h * BLOCK, (h + 1) * BLOCK)
+        q5[y, heads, :] = q_ref[:, heads]
+    kv_out[0] = key_ref[...]
+    kv_out[1] = value_ref[...]
     hidden_val = hidden_ref[...].astype(jnp.float32)
     square[...] = jnp.broadcast_to(
         jnp.sum(hidden_val * hidden_val, axis=1, keepdims=True), square.shape
     )
     pl.semaphore_wait(barrier, N_CTX - 1 + N_TP - 1)
 
+    def exchange(buf, x_s, x_r, f_s, f_r, s_s, s_r):
+        def send_near(ch):
+            rows = chunk_rows(ch)
+            for i, dx in enumerate(near):
+                remote(
+                    buf.at[tp, rows], buf.at[tp, rows], x_s.at[i, ch], x_r.at[i, ch],
+                    me, 2 * chip(dx) + k,
+                ).start()
+            share(tp, 3, ch).start()
+
+        def source(i):
+            return 2 * chip(N_X - near[i]) + k
+
+        def share(t, i, ch):
+            rows = chunk_rows(ch)
+            return remote(
+                buf.at[t, rows], buf.at[t, rows], s_s.at[i, ch], s_r.at[i, ch], me, sibling
+            )
+
+        def half(i, ch):
+            start = rows_by_chunk[ch] * CHUNK + i * (CHUNK // 2)
+            return pl.ds(pl.multiple_of(start, CHUNK // 2), CHUNK // 2)
+
+        def pass_on(i, ch):
+            rows = half(i, ch)
+            t = source(i)
+            return remote(
+                buf.at[t, rows], buf.at[t, rows], f_s.at[i, ch], f_r.at[i, ch],
+                me, 2 * chip(near[i]) + k,
+            )
+
+        def get_near(ch):
+            rows = chunk_rows(ch)
+            for i in range(2):
+                t = source(i)
+                remote(
+                    buf.at[t, rows], buf.at[t, rows], x_s.at[i, ch], x_r.at[i, ch], me, t
+                ).wait_recv()
+                pass_on(i, ch).start()
+                share(t, i, ch).start()
+
+        opposite = 2 * chip(2) + k
+
+        def get_far(ch):
+            for i in range(2):
+                rows = half(i, ch)
+                remote(
+                    buf.at[opposite, rows], buf.at[opposite, rows], f_s.at[i, ch], f_r.at[i, ch],
+                    me, opposite,
+                ).wait_recv()
+            share(opposite, 2, ch).start()
+
+        def shared(i):
+            return (source(0), source(1), opposite, tp)[i] + 1 - 2 * k
+
+        def get_shared(i, ch):
+            share(shared(i), i, ch).wait_recv()
+
+        def drain(ch):
+            rows = chunk_rows(ch)
+            for i in range(2):
+                remote(
+                    buf.at[tp, rows], buf.at[tp, rows], x_s.at[i, ch], x_r.at[i, ch],
+                    me, 2 * chip(near[i]) + k,
+                ).wait_send()
+                pass_on(i, ch).wait_send()
+            for i in range(4):
+                share(tp, i, ch).wait_send()
+
+        return send_near, get_near, get_far, get_shared, drain, source, opposite, shared
+
+    def chunk_rows(ch):
+        return pl.ds(pl.multiple_of(rows_by_chunk[ch] * CHUNK, CHUNK), CHUNK)
+
+    def pair_first(p):
+        return 2 * (y // 2) if p == 0 else 2 - 2 * (y // 2)
+
+    def pair_rows(p):
+        return pl.ds(pl.multiple_of(pair_first(p) * CHUNK, PAIR_ROWS), PAIR_ROWS)
+
+    gu_x = exchange(gu, gx_send, gx_recv, gf_send, gf_recv, gs_send, gs_recv)
+    hid_x = exchange(hid, ax_send, ax_recv, af_send, af_recv, as_send, as_recv)
+    source, opposite, shared = hid_x[5:]
+
     def dispatch(j):
         return remote(
-            slots_ref.at[j // GROUP], recv_d.at[me], d_send.at[j], d_recv.at[me], j, tp
-        )
-
-    for dy in ROW_ORDER:
-        row = (y - dy + N_Y) % N_Y
-
-        def send_step(dz, carry, row=row):
+            slots_out.at[j // GROUP], recv_d.at[me], d_send.at[j], d_recv.at[me], j, tp
+        )
+
+    def dispatch_row(ch):
+        row = rows_by_chunk[ch]
+
+        def send_step(dz, carry):
             dispatch(row * N_Z + (z + dz) % N_Z).start()
             return carry
 
-        lax.fori_loop(1 if dy == 0 else 0, N_Z, send_step, 0)
-    recv_d[me] = slots_ref[me // GROUP]
+        lax.fori_loop(1 if ch == 0 else 0, N_Z, send_step, 0)
+
+    recv_d[me] = slots_out[me // GROUP]
 
     def q_copy(i, owner):
         ctx = ((y + i) % N_Y) * N_Z + z
         return remote(q5.at[owner], q5.at[owner], q_send.at[i], q_recv.at[owner], ctx, tp)
-
-    for h in range(GROUP_Q):
-        heads = slice(h * BLOCK, (h + 1) * BLOCK)
-        q5[y, heads, :] = q_ref[:, heads]
-    for i in range(1, N_Y):
-        q_copy(i, y).start()
 
     def turn_queries():
         for i in range(1, N_Y):
@@ -510,19 +621,46 @@
                 heads = slice(h * BLOCK, (h + 1) * BLOCK)
                 qt_ref[r, :, heads] = q5[r, heads, :].astype(jnp.float32).T.astype(jnp.bfloat16)
 
-    def chunk_rows(ch):
-        start = ((y + ROW_ORDER[ch]) % N_Y) * CHUNK
-        return pl.ds(pl.multiple_of(start, CHUNK), CHUNK)
+    user_row = (y - z // 2 + N_Y) % N_Y
+
+    def kv_copy(i):
+        return remote(
+            kv_out, kv.at[y, z % 2], k_send.at[i], k_recv.at[y, z % 2], user_row * N_Z + i, tp
+        )
+
+    def send_keys():
+        for i in range(N_Z):
+
+            @pl.when(user_row * N_Z + i != me)
+            def _():
+                kv_copy(i).start()
+
+        @pl.when(user_row == y)
+        def _():
+            kv[y, z % 2] = kv_out[...]
+
+    def get_keys():
+        for r in range(N_Y):
+            for h in range(2):
+                peer = r * N_Z + 2 * ((r - y + N_Y) % N_Y) + h
+
+                @pl.when(peer != me)
+                def _():
+                    remote(
+                        kv_out, kv.at[r, h], k_send.at[0], k_recv.at[r, h], peer, tp
+                    ).wait_recv()
+
+        kv_ref[...] = kv[...]
 
     def arrive(ch):
-        first = ((y + ROW_ORDER[ch]) % N_Y) * N_Z
+        first = rows_by_chunk[ch] * N_Z
         for i in range(N_Z):
             j = first + i
 
             @pl.when(j != me)
             def _():
                 remote(
-                    slots_ref.at[0], recv_d.at[j], d_send.at[j], d_recv.at[j], j, tp
+                    slots_out.at[0], recv_d.at[j], d_send.at[j], d_recv.at[j], j, tp
                 ).wait_recv()
 
             flat[i * CAP : (i + 1) * CAP, :] = recv_d[j].astype(jnp.float32)
@@ -567,107 +705,133 @@
             x_out[i, rows, :] = joined(i, ch).astype(jnp.bfloat16)
             x_copy(i, ch).start()
 
-    def prepare():
-        gate = gate_ref[...].astype(jnp.float32).T
-        up = up_ref[...].astype(jnp.float32).T
-        act, slope = silu_parts(gate)
-        act_buf[...] = act
-        slope_buf[...] = up * slope
-        prod_buf[...] = act * up
-
-    def ag_out(i, ch):
-        rows = chunk_rows(ch)
-        return remote(
-            ag.at[tp, rows], ag.at[tp, rows], ax_send.at[i, ch], ax_recv.at[i, ch],
-            me, 2 * chip(far[i]) + k,
-        )
-
-    def ag_chip(i, ch):
-        return 2 * chip(N_X - far[i]) + k
-
-    def ag_in(i, ch):
-        rows = chunk_rows(ch)
-        t = ag_chip(i, ch)
-        return remote(
-            ag.at[t, rows], ag.at[t, rows], ax_send.at[i, ch], ax_recv.at[i, ch], me, t
-        )
-
-    def ag_share(t, i, ch):
-        rows = chunk_rows(ch)
-        return remote(
-            ag.at[t, rows], ag.at[t, rows], as_send.at[i, ch], as_recv.at[i, ch], me, sibling
-        )
+    def rt_copy(j, ch):
+        return remote(rt_out.at[ch], rt_in.at[me], r_send.at[j], r_recv.at[me], j, tp)
 
     def stage3(ch):
         rows = chunk_rows(ch)
-        hid = joined(3, ch)
+        total = joined(3, ch)
         for i in range(3):
             x_copy(i, ch).wait_recv()
-            hid = hid + x_in[i, rows, :].astype(jnp.float32)
-        ag[tp, rows, 0:FF_DEV] = (hid * slope_buf[rows, :]).astype(jnp.bfloat16)
-        ag[tp, rows, FF_DEV : 2 * FF_DEV] = (hid * act_buf[rows, :]).astype(jnp.bfloat16)
-        for i in range(3):
-            ag_out(i, ch).start()
-        ag_share(tp, 3, ch).start()
-        term = jnp.sum(hid * prod_buf[rows, :], axis=1, keepdims=True)
-        prod_buf[rows, 0:HD] = jnp.broadcast_to(term, (CHUNK, HD))
-
-    def product(t, rows):
+            total = total + x_in[i, rows, :].astype(jnp.float32)
+        hid[tp, rows, :] = total.astype(jnp.bfloat16)
+        hid_x[0](ch)
+        term = jnp.sum(total * prod_buf[rows, :], axis=1, keepdims=True)
+        rt_out[ch] = mm(owner_is, (term * spot_is).astype(jnp.bfloat16))
+        for i in range(N_Z):
+            j = rows_by_chunk[ch] * N_Z + i
+
+            @pl.when(j != me)
+            def _():
+                rt_copy(j, ch).start()
+
+        if ch == 0:
+            rt_in[me] = rt_out[0]
+
+    def product(t, p):
+        rows = pair_rows(p)
         cols = pl.ds(pl.multiple_of(t * FF_DEV, FF_DEV), FF_DEV)
-        return dot_nt(ag[t, rows, 0:FF_DEV], wg[:, cols]) + dot_nt(
-            ag[t, rows, FF_DEV : 2 * FF_DEV], wu[:, cols]
-        )
+        val = hid[t, rows, :].astype(jnp.float32)
+        grad_gate = (val * gu[t, rows, 0:FF_DEV].astype(jnp.float32)).astype(jnp.bfloat16)
+        grad_up = (val * gu[t, rows, FF_DEV : 2 * FF_DEV].astype(jnp.float32)).astype(jnp.bfloat16)
+        return dot_nt(grad_gate, wg[:, cols]) + dot_nt(grad_up, wu[:, cols])
 
     def back_copy(j):
         return remote(back.at[j], ret.at[me], b_send.at[j], b_recv.at[me], j, tp)
 
-    def stage4(ch):
-        rows = chunk_rows(ch)
-        acc[:, FEAT : FEAT + HD] = prod_buf[rows, 0:HD]
-        acc[:, 0:FEAT] = product(tp, rows)
-        for i in (1, 2, 0):
-            ag_in(i, ch).wait_recv()
-            ag_share(ag_chip(i, ch), i, ch).start()
-            acc[:, 0:FEAT] += product(ag_chip(i, ch), rows)
-        for i in (3, 1, 2, 0):
-            t = sibling if i == 3 else ag_chip(i, ch) + 1 - 2 * k
-            ag_share(t, i, ch).wait_recv()
-            acc[:, 0:FEAT] += product(t, rows)
-        first = ((y + ROW_ORDER[ch]) % N_Y) * N_Z
-        for i in range(N_Z):
-            j = first + i
-            back[j] = acc[i * CAP : (i + 1) * CAP, :].astype(jnp.bfloat16)
+    def near_products(p):
+        acc[p] = product(tp, p)
+        for i in range(2):
+            acc[p] += product(source(i), p)
+
+    def far_products(p):
+        acc[p] += product(opposite, p)
+        for i in (3, 0, 1, 2):
+            for ch in (2 * p, 2 * p + 1):
+                hid_x[3](i, ch)
+            acc[p] += product(shared(i), p)
+
+    def give_back(p):
+        for i in range(2 * N_Z):
+            j = pair_first(p) * N_Z + i
+            back[j] = acc[p, i * CAP : (i + 1) * CAP, :].astype(jnp.bfloat16)
 
             @pl.when(j != me)
             def _():
                 back_copy(j).start()
 
+    for ch in range(2):
+        dispatch_row(ch)
+    for ch in range(N_Y):
+        gu_x[0](ch)
+    for ch in range(2, N_Y):
+        dispatch_row(ch)
     w_copies[0].wait()
     arrive(0)
     stage1(0)
+    gu_x[1](0)
     arrive(1)
     stage1(1)
     stage2(0)
+    gu_x[1](1)
     arrive(2)
     stage1(2)
     stage2(1)
+    gu_x[1](2)
     arrive(3)
+    for i in range(1, N_Y):
+        q_copy(i, y).start()
+    send_keys()
     stage1(3)
     stage2(2)
+    gu_x[1](3)
     stage2(3)
-    prepare()
-    turn_queries()
-    w_copies[1].wait()
-    w_copies[2].wait()
+    for ch in range(N_Y):
+        gu_x[2](ch)
     for ch in range(N_Y):
         stage3(ch)
     for ch in range(N_Y):
-        stage4(ch)
+        for i in range(4):
+            gu_x[3](i, ch)
+    w_copies[1].wait()
+    w_copies[2].wait()
+    hid_x[1](0)
+    hid_x[1](1)
+    near_products(0)
+    hid_x[2](0)
+    hid_x[2](1)
+    hid_x[1](2)
+    hid_x[1](3)
+    far_products(0)
+    give_back(0)
+    near_products(1)
+    hid_x[2](2)
+    hid_x[2](3)
+    far_products(1)
+    give_back(1)
     ret[me] = back[me]
-
+    turn_queries()
+    get_keys()
+
+    for j in range(N_CTX):
+
+        @pl.when(j != me)
+        def _():
+            remote(rt_out.at[0], rt_in.at[j], r_send.at[j], r_recv.at[j], j, tp).wait_recv()
+
+        terms[j : j + 1, :] = rt_in[j, pl.ds(z, 1), :]
+    expert_col = turn(pack_ref[0:1, :])[:, 0:1]
+    rank_col = slot_col - CAP * expert_col
+    member = lax.broadcasted_iota(jnp.int32, (BLOCK, N_CTX), 1)
+    member = jnp.floor((member.astype(jnp.float32) + 0.5) / GROUP)
+    member_is = jnp.where(member == expert_col, 1.0, 0.0).astype(jnp.bfloat16)
+    token_terms = mm(member_is, terms[...].astype(jnp.bfloat16))
+    router_tok = jnp.sum(
+        jnp.where(lan.astype(jnp.float32) == rank_col, token_terms, 0.0), axis=1, keepdims=True
+    )
     picked[...] = jnp.zeros_like(picked)
     for ch in range(N_Y):
-        first = ((y - ROW_ORDER[ch] + N_Y) % N_Y) * N_Z
+        first = rows_by_chunk[ch] * N_Z
         for i in range(N_Z):
             j = first + i
 
@@ -675,17 +839,15 @@
             def _():
                 remote(back.at[j], ret.at[j], b_send.at[j], b_recv.at[j], j, tp).wait_recv()
 
-            acc[i * CAP : (i + 1) * CAP, :] = ret[j].astype(jnp.float32)
+            flat[i * CAP : (i + 1) * CAP, :] = ret[j].astype(jnp.float32)
         cols = pl.ds(pl.multiple_of(first * CAP_PAD, N_Z * CAP_PAD), N_Z * CAP_PAD)
-        picked[...] += mm(pick_ref[:, cols][:, 0:CHUNK], acc[...].astype(jnp.bfloat16))
-
-    norm_grad = picked[:, 0:FEAT] * score_ref[...]
+        picked[...] += mm(pick[:, cols][:, 0:CHUNK], flat[...].astype(jnp.bfloat16))
+
+    norm_grad = picked[...] * score
     hidden_now = hidden_ref[...].astype(jnp.float32)
-    gain_val = gain_ref[...].astype(jnp.float32)
     cross = jnp.sum(hidden_now * gain_val * norm_grad, axis=1, keepdims=True)
-    lane = lax.broadcasted_iota(jnp.int32, (BLOCK, HD), 1)
     packed = jnp.where(
-        lane == 0, picked[:, FEAT : FEAT + HD], jnp.where(lane == 1, square[...], cross)
+        lan == 0, router_tok, jnp.where(lan == 1, square[...], cross)
     )
     stats[tp] = packed.T[0:8, :]
 
@@ -719,14 +881,13 @@
     dh_ref[...] = d_hidden
     full[tp] = d_hidden
 
+    def full_chip(i):
+        return 2 * chip(N_X - far[i]) + k
+
     def full_out(i):
         return remote(
             full.at[tp], full.at[tp], fx_send.at[i], fx_recv.at[i], me, 2 * chip(far[i]) + k
         )
-
-    def full_in(i):
-        t = ag_chip(i, 0)
-        return remote(full.at[t], full.at[t], fx_send.at[i], fx_recv.at[i], me, t)
 
     def full_share(t, i):
         return remote(full.at[t], full.at[t], fs_send.at[i], fs_recv.at[i], me, sibling)
@@ -735,10 +896,11 @@
         full_out(i).start()
     full_share(tp, 3).start()
     for i in (1, 2, 0):
-        full_in(i).wait_recv()
-        full_share(ag_chip(i, 0), i).start()
+        t = full_chip(i)
+        remote(full.at[t], full.at[t], fx_send.at[i], fx_recv.at[i], me, t).wait_recv()
+        full_share(t, i).start()
     for i in (3, 1, 2, 0):
-        t = sibling if i == 3 else ag_chip(i, 0) + 1 - 2 * k
+        t = sibling if i == 3 else full_chip(i) + 1 - 2 * k
         full_share(t, i).wait_recv()
     full_ref[...] = full[...]
 
@@ -746,6 +908,7 @@
         j = (me + i) % N_CTX
         dispatch(j).wait_send()
         back_copy(j).wait_send()
+        rt_copy(j, 0).wait_send()
         return carry
 
     def drain_tp(i, carry):
@@ -757,24 +920,29 @@
     for ch in range(N_Y):
         for i in range(4):
             sib_copy(i, ch).wait_send()
-            ag_share(tp, i, ch).wait_send()
         for i in range(3):
             x_copy(i, ch).wait_send()
-            ag_out(i, ch).wait_send()
+        gu_x[4](ch)
+        hid_x[4](ch)
     for i in range(1, N_Y):
         q_copy(i, y).wait_send()
+    for i in range(N_Z):
+
+        @pl.when(user_row * N_Z + i != me)
+        def _():
+            kv_copy(i).wait_send()
+
     for i in range(3):
         full_out(i).wait_send()
     for i in range(4):
         full_share(tp, i).wait_send()
 
 
-def expert_block(slots, pick, score, hidden, gain, grad, queries, down, gate, up, wg, wu):
+def expert_block(pack, hidden, grad, queries, keys, values, down, gate, up, wg, wu):
     bf, f32 = jnp.bfloat16, jnp.float32
     vmem = pl.BlockSpec(memory_space=pltpu.VMEM)
     hbm = pl.BlockSpec(memory_space=pl.ANY)
     dma = pltpu.SemaphoreType.DMA
-    wide = FEAT + HD
     return pl.pallas_call(
         expert_kernel,
         name="expert_block",
@@ -784,13 +952,15 @@
             jax.ShapeDtypeStruct((N_TP, BLOCK, FEAT), bf),
             jax.ShapeDtypeStruct((N_Y, ROWS_Q, HD), bf),
             jax.ShapeDtypeStruct((N_Y, HD, ROWS_Q), bf),
+            jax.ShapeDtypeStruct((N_Y, 2, 2, BLOCK, HD), bf),
         ],
-        in_specs=[vmem] * 7 + [hbm, vmem, vmem, hbm, hbm],
-        out_specs=[vmem] * 5,
+        in_specs=[vmem] * 6 + [hbm, vmem, vmem, hbm, hbm],
+        out_specs=[vmem] * 6,
         scratch_shapes=[
             pltpu.VMEM((FF_GRP, FEAT), bf),
             pltpu.VMEM((FEAT, FF_GRP), bf),
             pltpu.VMEM((FEAT, FF_GRP), bf),
+            pltpu.VMEM((EXPERTS, CAP, FEAT), bf),
             pltpu.VMEM((N_CTX, CAP, FEAT), bf),
             pltpu.VMEM((CHUNK, FEAT), f32),
             pltpu.VMEM((SLOTS, FEAT), bf),
@@ -800,28 +970,39 @@
             pltpu.VMEM((3, SLOTS, FF_DEV), bf),
             pltpu.VMEM((3, SLOTS, FF_DEV), bf),
             pltpu.VMEM((SLOTS, FF_DEV), f32),
-            pltpu.VMEM((SLOTS, FF_DEV), f32),
-            pltpu.VMEM((SLOTS, FF_DEV), f32),
             pltpu.VMEM((N_TP, SLOTS, 2 * FF_DEV), bf),
-            pltpu.VMEM((CHUNK, wide), f32),
-            pltpu.VMEM((N_CTX, CAP, wide), bf),
-            pltpu.VMEM((N_CTX, CAP, wide), bf),
-            pltpu.VMEM((BLOCK, wide), f32),
+            pltpu.VMEM((N_TP, SLOTS, FF_DEV), bf),
+            pltpu.VMEM((2, PAIR_ROWS, FEAT), f32),
+            pltpu.VMEM((N_CTX, CAP, FEAT), bf),
+            pltpu.VMEM((N_CTX, CAP, FEAT), bf),
+            pltpu.VMEM((N_Y, N_Z, BLOCK), f32),
+            pltpu.VMEM((N_CTX, N_Z, BLOCK), f32),
+            pltpu.VMEM((N_CTX, BLOCK), f32),
+            pltpu.VMEM((BLOCK, N_Y * N_Z * CAP_PAD), bf),
+            pltpu.VMEM((BLOCK, FEAT), f32),
             pltpu.VMEM((N_TP, 8, BLOCK), f32),
             pltpu.VMEM((BLOCK, HD), f32),
             pltpu.VMEM((N_TP, BLOCK, FEAT), bf),
             pltpu.VMEM((N_Y, ROWS_Q, HD), bf),
+            pltpu.VMEM((2, BLOCK, HD), bf),
+            pltpu.VMEM((N_Y, 2, 2, BLOCK, HD), bf),
             dma((3,)),
             dma((N_CTX,)), dma((N_CTX,)),
             dma((4, N_Y)), dma((4, N_Y)),
             dma((3, N_Y)), dma((3, N_Y)),
-            dma((3, N_Y)), dma((3, N_Y)),
+            dma((2, N_Y)), dma((2, N_Y)),
+            dma((2, N_Y)), dma((2, N_Y)),
+            dma((4, N_Y)), dma((4, N_Y)),
+            dma((2, N_Y)), dma((2, N_Y)),
+            dma((2, N_Y)), dma((2, N_Y)),
             dma((4, N_Y)), dma((4, N_Y)),
             dma((N_CTX,)), dma((N_CTX,)),
             dma((N_TP,)), dma((N_TP,)),
             dma((3,)), dma((3,)),
             dma((4,)), dma((4,)),
             dma((N_Y,)), dma((N_Y,)),
+            dma((N_Z,)), dma((N_Y, 2)),
+            dma((N_CTX,)), dma((N_CTX,)),
         ],
         cost_estimate=pl.CostEstimate(
             flops=60_000_000_000, bytes_accessed=200_000_000, transcendentals=3_000_000
@@ -829,7 +1010,7 @@
         compiler_params=pltpu.CompilerParams(
             collective_id=3, has_side_effects=True, vmem_limit_bytes=56 * 2**20
         ),
-    )(slots, pick, score, hidden, gain, grad, queries, down, gate, up, wg, wu)
+    )(pack, hidden, grad, queries, keys, values, down, gate, up, wg, wu)
 
 
 def body(
@@ -848,38 +1029,23 @@
     keys,
     values,
 ):
-    tok_rows = out_grad.shape[0]
-    pad = W_ROWS - tok_rows
-    shared_part = jnp.concatenate(
-        [w_out.T, jnp.pad(keys, ((0, pad), (0, 0))), jnp.pad(values, ((0, pad), (0, 0)))], axis=1
+    gathered = lax.all_gather(w_out.T, "ctx", axis=0, tiled=True)
+    pack = jnp.concatenate(
+        [
+            expert_ids.reshape(1, BLOCK).astype(jnp.float32),
+            router_score.astype(jnp.float32).reshape(1, BLOCK),
+            norm_gain.astype(jnp.float32).reshape(GROUP_Q, BLOCK),
+            jnp.zeros((1, BLOCK), jnp.float32),
+        ],
+        axis=0,
     )
-    gathered = lax.all_gather(shared_part, "ctx", axis=0, tiled=True)
-
-    chosen = expert_ids
-    chosen_row = chosen.reshape(1, tok_rows)
-    earlier = (
-        jnp.arange(tok_rows, dtype=jnp.int32)[None, :] < jnp.arange(tok_rows, dtype=jnp.int32)[:, None]
-    )
-    ranked = jnp.sum(((chosen == chosen_row) & earlier).astype(jnp.int32), axis=1)
-    chosen = chosen[:, 0]
-    slot_index = chosen * CAP + ranked
-    placing = (
-        jnp.arange(EXPERTS * CAP, dtype=jnp.int32)[:, None] == slot_index[None, :]
-    ).astype(jnp.bfloat16)
-    grad_slots = mm(placing, out_grad).astype(jnp.bfloat16).reshape(EXPERTS, CAP, FEAT)
-    column = jnp.arange(N_Y * N_Z * CAP_PAD, dtype=jnp.int32)
-    within = column % (N_Z * CAP_PAD)
-    member = column // (N_Z * CAP_PAD) * N_Z + within // CAP
-    column_slot = jnp.where(within < CHUNK, member // GROUP * CAP + within % CAP, -1)
-    pick = (slot_index[:, None] == column_slot[None, :]).astype(jnp.bfloat16)
-    d_hidden, stats, full_grad, q5, qt = expert_block(
-        grad_slots,
-        pick,
-        router_score.astype(jnp.float32)[:, None],
+    d_hidden, stats, full_grad, q5, qt, kv = expert_block(
+        pack,
         hidden_in,
-        norm_gain[None, :],
         out_grad,
         queries,
+        keys,
+        values,
         w_down[0],
         gate_saved[0],
         up_saved[0],
@@ -887,7 +1053,10 @@
         w_up[0],
     )
     router_grad = stats[0]
-    query_grad, key_grad, value_grad = attention(full_grad, q5, qt, gathered)
+    grads = attention(full_grad, q5, qt, kv, gathered)
+    query_grad = grads[:, 0:ROWS_Q]
+    key_grad = grads[:, ROWS_Q : ROWS_Q + HD]
+    value_grad = grads[:, ROWS_Q + HD :]
     return (
         d_hidden,
         router_grad,

time: 204 us -> 191 us (0.936)
  Pallas kernels: 172 us -> 165 us
  local copies, waits for them, and re-layouts: 8.21 us -> 4.93 us
  other arithmetic: 5.41 us -> 2.66 us
    unnamed x6 -> x3, local copies, waits for them, and re-layouts: 5.02 us -> 0.67 us
    pallas_call x1, Pallas kernels: 127 us -> 123 us  [expert_block(): pl.pallas_call(expert_kernel, name='expert_block', out_shape=[jax.ShapeDt...]
    slice x0 -> x2, local copies, waits for them, and re-layouts: none -> 3 us  [the longest x1 1.6 us: body(): query_grad = grads[:, 0:ROWS_Q]]
    pallas_call x1, Pallas kernels: 44.5 us -> 42.1 us  [attention(): pl.pallas_call(attention_kernel, name='attention_grads', out_shape=jax.Sh...]
  transfers between devices with their start and end apart: 1 -> 1, of which waited for: 0 -> 0; matrix products, arithmetic and copies ran while one was open for 4% -> 2% of each run, Pallas kernels for 63% -> 66%
where the time goes in v4:
time: 191 us; the launch traced here: 188 us
  Pallas kernels  165 us (86%)
  between operations  14 us (7%)
  local copies, waits for them, and re-layouts  4.93 us (3%)
  other arithmetic  2.66 us (1%)
    pallas_call x1, Pallas kernels, expert_block(): pl.pallas_call(expert_kernel, name='expert_block', out_shape=[jax.ShapeDt...  123 us
    pallas_call x1, Pallas kernels, attention(): pl.pallas_call(attention_kernel, name='attention_grads', out_shape=jax.Sh...  42.1 us
  transfers between devices with their start and end apart: 1, of which 0 were waited for; matrix products, arithmetic and copies ran while one was open for 2% of the time, Pallas kernels for 66%

profile of v4, /device:TPU:88, one launch (start us, length us, event | category | flops | bytes accessed | tf_op | source)
XLA Modules:
  0.0 187.7 jit_solution(15638130947471348208)
XLA Ops:
  7.2 0.0 all-gather.2.cloned.1.call-start
  7.2 0.7 all-gather.2.cloned.1.call-update
  7.9 0.1 pad.3.clone
  8.0 0.7 bitcast_convert_fusion.1
  8.6 0.7 convert_bitcast_fusion
  9.3 0.7 bitcast_convert_fusion
  10.0 0.7 maximum_maximum_fusion.pack_ref
  10.6 123.2 %expert_block.1 = (bf16[128,640]{1,0:T(8,128)(2,1)}, f32[8,128]{1,0:T(8,128)}, bf16[8,128,640]{2,1,0:T(8,128)(2,1)}, bf16[4,640,128]{2,1,0:T(8,128)(2,1)}, bf16[...) custom-call(f32[8,128]{1,0:T(8,128)} %maximum_maximum_fusion.pack_ref, bf16[128,640]{1,0:T(8,128)(2,1)} %hidden_ref.1, ...), custom_call_target="tpu_custom_call" | custom-call | flops 60000002048 | bytes 200000000 | tf_op jit(solution)/shard_map/expert_block/pallas_call | solution.py:946
  133.8 1.2 slice_bitcast_fusion
  135.0 0.0 all-gather.2.cloned.1.call-done.gathered_ref
  135.0 0.0 copy-start
  135.0 42.1 %attention_grads.1 = bf16[128,896]{1,0:T(8,128)(2,1)} custom-call(bf16[8,128,640]{2,1,0:T(8,128)(2,1)} %get-tuple-element.13.full_ref, bf16[4,640,128]{2,1,0:T(8,128)(2,1)} %get-tuple-element.14.q5_ref, bf16[4,128,640]{2,1,0:T(8,128)(2,1)} %get-tuple-element.15.qt_ref, bf16[4,2,2,128,128]{4,3,2,1,0:T(8,128)(2,1)} %get-tuple-element.16.kv_ref, ...), custom_call_target="tpu_custom_call" | custom-call | flops 6000000000 | bytes 12000000 | tf_op jit(solution)/shard_map/attention_grads/pallas_call | solution.py:353
  177.2 1.6 slice.13
  178.8 1.4 fusion
  180.2 0.0 copy-done
  180.2 0.7 copy.20
Async XLA Ops:
  7.2 127.9 %all-gather.2.cloned.1.call-start = ((), (), s32[]{:S(2)}) async-start(), calls=%async_computation | async-start | bytes 6758400 | tf_op jit(solution)/shard_map/all_gather | solution.py:1032
  135.0 45.2 %copy-start = (bf16[128,640]{1,0:T(8,128)(2,1)S(1)}, bf16[128,640]{1,0:T(8,128)(2,1)}, u32[]{:S(2)}) copy-start(bf16[128,640]{1,0:T(8,128)(2,1)} %get-tuple-element.24) | copy-start | bytes 491524
Sparse Core Ops, SparseCore 0:
  10.6 116.1 all-gather.1

commit v5 on v4

--- a/solution.py
+++ b/solution.py
@@ -16,6 +16,7 @@
 PAIR = 2 * BLOCK
 ROWS_Q = GROUP_Q * BLOCK
 N_Y, N_Z, N_X, N_TP = 4, 8, 4, 8
+W_ROWS = D // N_CTX
 GROUP = N_CTX // EXPERTS
 CAP = 24
 CAP_PAD = 32
@@ -403,14 +404,14 @@
 
 def expert_kernel(
     pack_ref, hidden_ref, grad_ref, q_ref, key_ref, value_ref,
-    down_ref, gate_ref, up_ref, wg_ref, wu_ref,
-    dh_ref, stat_ref, full_ref, q5_ref, qt_ref, kv_ref,
+    down_ref, gate_ref, up_ref, wg_ref, wu_ref, wt_ref,
+    dh_ref, stat_ref, full_ref, q5_ref, qt_ref, kv_ref, all_ref,
     down, wg, wu, slots_out, recv_d, flat, slots, own, sib_out, sib_in, x_out, x_in,
-    prod_buf, gu, hid, acc, back, ret, rt_out, rt_in, terms, pick, picked, stats, square, full, q5, kv_out, kv,
-    w_sem, d_send, d_recv, s_send, s_recv, x_send, x_recv, gx_send, gx_recv,
-    gf_send, gf_recv, gs_send, gs_recv, ax_send, ax_recv, af_send, af_recv,
+    prod_buf, slope_buf, act_buf, gu, acc, back, ret, rt_out, rt_in, terms, pick, picked, stats, square, full, q5, kv_out, kv,
+    w_sem, d_send, d_recv, s_send, s_recv, x_send, x_recv, ax_send, ax_recv, af_send, af_recv,
     as_send, as_recv, b_send, b_recv, t_send, t_recv, fx_send, fx_recv, fs_send, fs_recv,
     q_send, q_recv, k_send, k_recv, r_send, r_recv,
+    wz_send, wz_recv, wy_send, wy_recv, wf_send, wf_recv, wo_sem,
 ):
     me = lax.axis_index("ctx")
     tp = lax.axis_index("tp")
@@ -469,6 +470,359 @@
     placed = mm(placing, grad_ref[...])
     for e in range(EXPERTS):
         slots_out[e] = placed[e * CAP : (e + 1) * CAP].astype(jnp.bfloat16)
+    for h in range(GROUP_Q):
+        heads = slice(h * BLOCK, (h + 1) * BLOCK)
+        q5[y, heads, :] = q_ref[:, heads]
+    kv_out[0] = key_ref[...]
+    kv_out[1] = value_ref[...]
+    pl.semaphore_wait(barrier, N_CTX - 1 + N_TP - 1)
+
+    def exchange(buf, x_s, x_r, f_s, f_r, s_s, s_r):
+        def send_near(ch):
+            rows = chunk_rows(ch)
+            for i, dx in enumerate(near):
+                remote(
+                    buf.at[tp, rows], buf.at[tp, rows], x_s.at[i, ch], x_r.at[i, ch],
+                    me, 2 * chip(dx) + k,
+                ).start()
+            share(tp, 3, ch).start()
+
+        def source(i):
+            return 2 * chip(N_X - near[i]) + k
+
+        def share(t, i, ch):
+            rows = chunk_rows(ch)
+            return remote(
+                buf.at[t, rows], buf.at[t, rows], s_s.at[i, ch], s_r.at[i, ch], me, sibling
+            )
+
+        def half(i, ch):
+            start = rows_by_chunk[ch] * CHUNK + i * (CHUNK // 2)
+            return pl.ds(pl.multiple_of(start, CHUNK // 2), CHUNK // 2)
+
+        def pass_on(i, ch):
+            rows = half(i, ch)
+            t = source(i)
+            return remote(
+                buf.at[t, rows], buf.at[t, rows], f_s.at[i, ch], f_r.at[i, ch],
+                me, 2 * chip(near[i]) + k,
+            )
+
+        def get_near(ch):
+            rows = chunk_rows(ch)
+            for i in range(2):
+                t = source(i)
+                remote(
+                    buf.at[t, rows], buf.at[t, rows], x_s.at[i, ch], x_r.at[i, ch], me, t
+                ).wait_recv()
+                pass_on(i, ch).start()
+                share(t, i, ch).start()
+
+        opposite = 2 * chip(2) + k
+
+        def get_far(ch):
+            for i in range(2):
+                rows = half(i, ch)
+                remote(
+                    buf.at[opposite, rows], buf.at[opposite, rows], f_s.at[i, ch], f_r.at[i, ch],
+                    me, opposite,
+                ).wait_recv()
+            share(opposite, 2, ch).start()
+
+        def shared(i):
+            return (source(0), source(1), opposite, tp)[i] + 1 - 2 * k
+
+        def get_shared(i, ch):
+            share(shared(i), i, ch).wait_recv()
+
+        def drain(ch):
+            rows = chunk_rows(ch)
+            for i in range(2):
+                remote(
+                    buf.at[tp, rows], buf.at[tp, rows], x_s.at[i, ch], x_r.at[i, ch],
+                    me, 2 * chip(near[i]) + k,
+                ).wait_send()
+                pass_on(i, ch).wait_send()
+            for i in range(4):
+                share(tp, i, ch).wait_send()
+
+        return send_near, get_near, get_far, get_shared, drain, source, opposite, shared
+
+    def w_rows(ctx, part=None):
+        if part is None:
+            return pl.ds(pl.multiple_of(ctx * W_ROWS, W_ROWS), W_ROWS)
+        half = W_ROWS // 2
+        return pl.ds(pl.multiple_of(ctx * W_ROWS + part * half, half), half)
+
+    def w_to(dst_rows, src, send, recv, ctx):
+        return remote(src, all_ref.at[dst_rows], send, recv, ctx, tp)
+
+    def turn_z(i, n):
+        return (z + (n if i == 0 else N_Z - n)) % N_Z
+
+    def wz(i, n):
+        block = y * N_Z + turn_z(i, N_Z - n + 1)
+        rows = w_rows(block, i if n == N_Z // 2 else None)
+        src = wt_ref if n == 1 else all_ref.at[rows]
+        return w_to(rows, src, wz_send.at[i, n - 1], wz_recv.at[i, n - 1], y * N_Z + turn_z(i, 1))
+
+    def wz_wait(i, n):
+        rows = w_rows(y * N_Z + turn_z(i, N_Z - n), i if n == N_Z // 2 else None)
+        w_to(
+            rows, all_ref.at[rows], wz_send.at[i, n - 1], wz_recv.at[i, n - 1],
+            y * N_Z + turn_z(1 - i, 1),
+        ).wait_recv()
+
+    row_order = (0, 7, 1, 6, 2, 5, 3, 4)
+
+    def next_row(i, n=1):
+        return (y + (n if i == 0 else N_Y - n)) % N_Y
+
+    def wy(i, o):
+        rows = w_rows(y * N_Z + (z + row_order[o]) % N_Z)
+        src = wt_ref if o == 0 else all_ref.at[rows]
+        return w_to(rows, src, wy_send.at[i, o], wy_recv.at[i, o], next_row(i) * N_Z + z)
+
+    def wf(i, o):
+        rows = w_rows(next_row(1 - i) * N_Z + (z + row_order[o]) % N_Z, i)
+        return w_to(
+            rows, all_ref.at[rows], wf_send.at[i, o], wf_recv.at[i, o], next_row(i) * N_Z + z
+        )
+
+    w_own = pltpu.make_async_copy(wt_ref, all_ref.at[w_rows(me)], wo_sem)
+
+    def ring_first():
+        w_own.start()
+        for i in range(2):
+            wz(i, 1).start()
+            wy(i, 0).start()
+
+    def ring_step(n):
+        for i in range(2):
+            wz_wait(i, n)
+        if n < N_Z // 2:
+            for i in range(2):
+                wz(i, n + 1).start()
+        for o in (2 * n - 1, 2 * n) if n < N_Z // 2 else (N_Z - 1,):
+            for i in range(2):
+                wy(i, o).start()
+
+    def row_step(o):
+        for i in range(2):
+            rows = w_rows(next_row(1 - i) * N_Z + (z + row_order[o]) % N_Z)
+            w_to(
+                rows, all_ref.at[rows], wy_send.at[i, o], wy_recv.at[i, o],
+                next_row(1 - i) * N_Z + z,
+            ).wait_recv()
+            wf(i, o).start()
+
+    def ring_last():
+        w_own.wait()
+        for o in range(N_Z):
+            for i in range(2):
+                rows = w_rows(next_row(i, 2) * N_Z + (z + row_order[o]) % N_Z, i)
+                w_to(
+                    rows, all_ref.at[rows], wf_send.at[i, o], wf_recv.at[i, o],
+                    next_row(1 - i) * N_Z + z,
+                ).wait_recv()
+
+    def ring_drain():
+        for i in range(2):
+            for n in range(1, N_Z // 2 + 1):
+                wz(i, n).wait_send()
+            for o in range(N_Z):
+                wy(i, o).wait_send()
+                wf(i, o).wait_send()
+
+    def chunk_rows(ch):
+        return pl.ds(pl.multiple_of(rows_by_chunk[ch] * CHUNK, CHUNK), CHUNK)
+
+    def pair_first(p):
+        return 2 * (y // 2) if p == 0 else 2 - 2 * (y // 2)
+
+    def pair_rows(p):
+        return pl.ds(pl.multiple_of(pair_first(p) * CHUNK, PAIR_ROWS), PAIR_ROWS)
+
+    hid_x = exchange(gu, ax_send, ax_recv, af_send, af_recv, as_send, as_recv)
+    source, opposite, shared = hid_x[5:]
+
+    def dispatch(j):
+        return remote(
+            slots_out.at[j // GROUP], recv_d.at[me], d_send.at[j], d_recv.at[me], j, tp
+        )
+
+    def dispatch_row(ch):
+        row = rows_by_chunk[ch]
+
+        def send_step(dz, carry):
+            dispatch(row * N_Z + (z + dz) % N_Z).start()
+            return carry
+
+        lax.fori_loop(1 if ch == 0 else 0, N_Z, send_step, 0)
+
+    recv_d[me] = slots_out[me // GROUP]
+
+    def q_copy(i, owner):
+        ctx = ((y + i) % N_Y) * N_Z + z
+        return remote(q5.at[owner], q5.at[owner], q_send.at[i], q_recv.at[owner], ctx, tp)
+
+    def turn_queries():
+        for i in range(1, N_Y):
+            q_copy(i, (y + i) % N_Y).wait_recv()
+        q5_ref[...] = q5[...]
+        for r in range(N_Y):
+            for h in range(GROUP_Q):
+                heads = slice(h * BLOCK, (h + 1) * BLOCK)
+                qt_ref[r, :, heads] = q5[r, heads, :].astype(jnp.float32).T.astype(jnp.bfloat16)
+
+    user_row = (y - z // 2 + N_Y) % N_Y
+
+    def kv_copy(i):
+        return remote(
+            kv_out, kv.at[y, z % 2], k_send.at[i], k_recv.at[y, z % 2], user_row * N_Z + i, tp
+        )
+
+    def send_keys():
+        for i in range(N_Z):
+
+            @pl.when(user_row * N_Z + i != me)
+            def _():
+                kv_copy(i).start()
+
+        @pl.when(user_row == y)
+        def _():
+            kv[y, z % 2] = kv_out[...]
+
+    def get_keys():
+        for r in range(N_Y):
+            for h in range(2):
+                peer = r * N_Z + 2 * ((r - y + N_Y) % N_Y) + h
+
+                @pl.when(peer != me)
+                def _():
+                    remote(
+                        kv_out, kv.at[r, h], k_send.at[0], k_recv.at[r, h], peer, tp
+                    ).wait_recv()
+
+        kv_ref[...] = kv[...]
+
+    def arrive(ch):
+        first = rows_by_chunk[ch] * N_Z
+        for i in range(N_Z):
+            j = first + i
+
+            @pl.when(j != me)
+            def _():
+                remote(
+                    slots_out.at[0], recv_d.at[j], d_send.at[j], d_recv.at[j], j, tp
+                ).wait_recv()
+
+            flat[i * CAP : (i + 1) * CAP, :] = recv_d[j].astype(jnp.float32)
+        slots[chunk_rows(ch), :] = flat[...].astype(jnp.bfloat16)
+
+    def sib_copy(i, ch):
+        rows = chunk_rows(ch)
+        return remote(
+            sib_out.at[i, rows], sib_in.at[i, rows], s_send.at[i, ch], s_recv.at[i, ch],
+            me, sibling,
+        )
+
+    def x_copy(i, ch):
+        rows = chunk_rows(ch)
+        return remote(
+            x_out.at[i, rows], x_in.at[i, rows], x_send.at[i, ch], x_recv.at[i, ch],
+            me, 2 * chip(far[i]) + k,
+        )
+
+    def stage1(ch):
+        rows = chunk_rows(ch)
+        part = slots[rows, :]
+        for i, dx in enumerate(far + (0,)):
+            base = 2 * chip(dx)
+
+            def block(t):
+                start = pl.multiple_of(t * FF_DEV, FF_DEV)
+                return dot_nt(part, down[pl.ds(start, FF_DEV), :]).astype(jnp.bfloat16)
+
+            sib_out[i, rows, :] = block(base + 1 - k)
+            sib_copy(i, ch).start()
+            own[i, rows, :] = block(base + k)
+
+    def joined(i, ch):
+        rows = chunk_rows(ch)
+        sib_copy(i, ch).wait_recv()
+        return own[i, rows, :].astype(jnp.float32) + sib_in[i, rows, :].astype(jnp.float32)
+
+    def stage2(ch):
+        rows = chunk_rows(ch)
+        for i in range(3):
+            x_out[i, rows, :] = joined(i, ch).astype(jnp.bfloat16)
+            x_copy(i, ch).start()
+
+    def rt_copy(j, ch):
+        return remote(rt_out.at[ch], rt_in.at[me], r_send.at[j], r_recv.at[me], j, tp)
+
+    def stage3(ch):
+        rows = chunk_rows(ch)
+        total = joined(3, ch)
+        for i in range(3):
+            x_copy(i, ch).wait_recv()
+            total = total + x_in[i, rows, :].astype(jnp.float32)
+        gu[tp, rows, 0:FF_DEV] = (total * slope_buf[rows, :]).astype(jnp.bfloat16)
+        gu[tp, rows, FF_DEV : 2 * FF_DEV] = (total * act_buf[rows, :]).astype(jnp.bfloat16)
+        hid_x[0](ch)
+        term = jnp.sum(total * prod_buf[rows, :], axis=1, keepdims=True)
+        rt_out[ch] = mm(owner_is, (term * spot_is).astype(jnp.bfloat16))
+        for i in range(N_Z):
+            j = rows_by_chunk[ch] * N_Z + i
+
+            @pl.when(j != me)
+            def _():
+                rt_copy(j, ch).start()
+
+        if ch == 0:
+            rt_in[me] = rt_out[0]
+
+    def product(t, p):
+        rows = pair_rows(p)
+        cols = pl.ds(pl.multiple_of(t * FF_DEV, FF_DEV), FF_DEV)
+        return dot_nt(gu[t, rows, 0:FF_DEV], wg[:, cols]) + dot_nt(
+            gu[t, rows, FF_DEV : 2 * FF_DEV], wu[:, cols]
+        )
+
+    def back_copy(j):
+        return remote(back.at[j], ret.at[me], b_send.at[j], b_recv.at[me], j, tp)
+
+    def near_products(p):
+        acc[p] = product(tp, p)
+        for i in range(2):
+            acc[p] += product(source(i), p)
+
+    def far_products(p):
+        acc[p] += product(opposite, p)
+        for i in (3, 0, 1, 2):
+            for ch in (2 * p, 2 * p + 1):
+                hid_x[3](i, ch)
+            acc[p] += product(shared(i), p)
+
+    def give_back(p):
+        for i in range(2 * N_Z):
+            j = pair_first(p) * N_Z + i
+            back[j] = acc[p, i * CAP : (i + 1) * CAP, :].astype(jnp.bfloat16)
+
+            @pl.when(j != me)
+            def _():
+                back_copy(j).start()
+
+    for ch in range(N_Y):
+        dispatch_row(ch)
+    gate = gate_ref[...].astype(jnp.float32).T
+    up = up_ref[...].astype(jnp.float32).T
+    act, slope = silu_parts(gate)
+    slope_buf[...] = up * slope
+    act_buf[...] = act
+    prod_buf[...] = act * up
+    ring_first()
     slot_col = turn(slot_row)[:, 0:1]
     number = lax.broadcasted_iota(jnp.int32, (8, N_Y * N_Z * CAP_PAD), 1).astype(jnp.float32)
     device_row = jnp.floor((number + 0.5) / (N_Z * CAP_PAD))
@@ -482,12 +836,6 @@
     score = turn(pack_ref[1:2, :])[:, 0:1]
     gain_val = jnp.concatenate([pack_ref[2 + h : 3 + h, :] for h in range(GROUP_Q)], axis=1)
 
-    gate = gate_ref[...].astype(jnp.float32).T
-    up = up_ref[...].astype(jnp.float32).T
-    act, slope = silu_parts(gate)
-    gu[tp, :, 0:FF_DEV] = (up * slope).astype(jnp.bfloat16)
-    gu[tp, :, FF_DEV : 2 * FF_DEV] = act.astype(jnp.bfloat16)
-    prod_buf[...] = act * up
     spot = lax.broadcasted_iota(jnp.int32, (CHUNK, BLOCK), 0).astype(jnp.float32)
     spot = spot - CAP * jnp.floor((spot + 0.5) / CAP)
     spot_is = jnp.where(
@@ -497,320 +845,60 @@
     own_lan = lax.broadcasted_iota(jnp.int32, (N_Z, CHUNK), 1)
     owner_is = jnp.where((own_lan >= own_sub) & (own_lan < own_sub + CAP), 1.0, 0.0)
     owner_is = owner_is.astype(jnp.bfloat16)
-    for h in range(GROUP_Q):
-        heads = slice(h * BLOCK, (h + 1) * BLOCK)
-        q5[y, heads, :] = q_ref[:, heads]
-    kv_out[0] = key_ref[...]
-    kv_out[1] = value_ref[...]
     hidden_val = hidden_ref[...].astype(jnp.float32)
     square[...] = jnp.broadcast_to(
         jnp.sum(hidden_val * hidden_val, axis=1, keepdims=True), square.shape
     )
-    pl.semaphore_wait(barrier, N_CTX - 1 + N_TP - 1)
-
-    def exchange(buf, x_s, x_r, f_s, f_r, s_s, s_r):
-        def send_near(ch):
-            rows = chunk_rows(ch)
-            for i, dx in enumerate(near):
-                remote(
-                    buf.at[tp, rows], buf.at[tp, rows], x_s.at[i, ch], x_r.at[i, ch],
-                    me, 2 * chip(dx) + k,
-                ).start()
-            share(tp, 3, ch).start()
-
-        def source(i):
-            return 2 * chip(N_X - near[i]) + k
-
-        def share(t, i, ch):
-            rows = chunk_rows(ch)
-            return remote(
-                buf.at[t, rows], buf.at[t, rows], s_s.at[i, ch], s_r.at[i, ch], me, sibling
-            )
-
-        def half(i, ch):
-            start = rows_by_chunk[ch] * CHUNK + i * (CHUNK // 2)
-            return pl.ds(pl.multiple_of(start, CHUNK // 2), CHUNK // 2)
-
-        def pass_on(i, ch):
-            rows = half(i, ch)
-            t = source(i)
-            return remote(
-                buf.at[t, rows], buf.at[t, rows], f_s.at[i, ch], f_r.at[i, ch],
-                me, 2 * chip(near[i]) + k,
-            )
-
-        def get_near(ch):
-            rows = chunk_rows(ch)
-            for i in range(2):
-                t = source(i)
-                remote(
-                    buf.at[t, rows], buf.at[t, rows], x_s.at[i, ch], x_r.at[i, ch], me, t
-                ).wait_recv()
-                pass_on(i, ch).start()
-                share(t, i, ch).start()
-
-        opposite = 2 * chip(2) + k
-
-        def get_far(ch):
-            for i in range(2):
-                rows = half(i, ch)
-                remote(
-                    buf.at[opposite, rows], buf.at[opposite, rows], f_s.at[i, ch], f_r.at[i, ch],
-                    me, opposite,
-                ).wait_recv()
-            share(opposite, 2, ch).start()
-
-        def shared(i):
-            return (source(0), source(1), opposite, tp)[i] + 1 - 2 * k
-
-        def get_shared(i, ch):
-            share(shared(i), i, ch).wait_recv()
-
-        def drain(ch):
-            rows = chunk_rows(ch)
-            for i in range(2):
-                remote(
-                    buf.at[tp, rows], buf.at[tp, rows], x_s.at[i, ch], x_r.at[i, ch],
-                    me, 2 * chip(near[i]) + k,
-                ).wait_send()
-                pass_on(i, ch).wait_send()
-            for i in range(4):
-                share(tp, i, ch).wait_send()
-
-        return send_near, get_near, get_far, get_shared, drain, source, opposite, shared
-
-    def chunk_rows(ch):
-        return pl.ds(pl.multiple_of(rows_by_chunk[ch] * CHUNK, CHUNK), CHUNK)
-
-    def pair_first(p):
-        return 2 * (y // 2) if p == 0 else 2 - 2 * (y // 2)
-
-    def pair_rows(p):
-        return pl.ds(pl.multiple_of(pair_first(p) * CHUNK, PAIR_ROWS), PAIR_ROWS)
-
-    gu_x = exchange(gu, gx_send, gx_recv, gf_send, gf_recv, gs_send, gs_recv)
-    hid_x = exchange(hid, ax_send, ax_recv, af_send, af_recv, as_send, as_recv)
-    source, opposite, shared = hid_x[5:]
-
-    def dispatch(j):
-        return remote(
-            slots_out.at[j // GROUP], recv_d.at[me], d_send.at[j], d_recv.at[me], j, tp
-        )
-
-    def dispatch_row(ch):
-        row = rows_by_chunk[ch]
-
-        def send_step(dz, carry):
-            dispatch(row * N_Z + (z + dz) % N_Z).start()
-            return carry
-
-        lax.fori_loop(1 if ch == 0 else 0, N_Z, send_step, 0)
-
-    recv_d[me] = slots_out[me // GROUP]
-
-    def q_copy(i, owner):
-        ctx = ((y + i) % N_Y) * N_Z + z
-        return remote(q5.at[owner], q5.at[owner], q_send.at[i], q_recv.at[owner], ctx, tp)
-
-    def turn_queries():
-        for i in range(1, N_Y):
-            q_copy(i, (y + i) % N_Y).wait_recv()
-        q5_ref[...] = q5[...]
-        for r in range(N_Y):
-            for h in range(GROUP_Q):
-                heads = slice(h * BLOCK, (h + 1) * BLOCK)
-                qt_ref[r, :, heads] = q5[r, heads, :].astype(jnp.float32).T.astype(jnp.bfloat16)
-
-    user_row = (y - z // 2 + N_Y) % N_Y
-
-    def kv_copy(i):
-        return remote(
-            kv_out, kv.at[y, z % 2], k_send.at[i], k_recv.at[y, z % 2], user_row * N_Z + i, tp
-        )
-
-    def send_keys():
-        for i in range(N_Z):
-
-            @pl.when(user_row * N_Z + i != me)
-            def _():
-                kv_copy(i).start()
-
-        @pl.when(user_row == y)
-        def _():
-            kv[y, z % 2] = kv_out[...]
-
-    def get_keys():
-        for r in range(N_Y):
-            for h in range(2):
-                peer = r * N_Z + 2 * ((r - y + N_Y) % N_Y) + h
-
-                @pl.when(peer != me)
-                def _():
-                    remote(
-                        kv_out, kv.at[r, h], k_send.at[0], k_recv.at[r, h], peer, tp
-                    ).wait_recv()
-
-        kv_ref[...] = kv[...]
-
-    def arrive(ch):
-        first = rows_by_chunk[ch] * N_Z
-        for i in range(N_Z):
-            j = first + i
-
-            @pl.when(j != me)
-            def _():
-                remote(
-                    slots_out.at[0], recv_d.at[j], d_send.at[j], d_recv.at[j], j, tp
-                ).wait_recv()
-
-            flat[i * CAP : (i + 1) * CAP, :] = recv_d[j].astype(jnp.float32)
-        slots[chunk_rows(ch), :] = flat[...].astype(jnp.bfloat16)
-
-    def sib_copy(i, ch):
-        rows = chunk_rows(ch)
-        return remote(
-            sib_out.at[i, rows], sib_in.at[i, rows], s_send.at[i, ch], s_recv.at[i, ch],
-            me, sibling,
-        )
-
-    def x_copy(i, ch):
-        rows = chunk_rows(ch)
-        return remote(
-            x_out.at[i, rows], x_in.at[i, rows], x_send.at[i, ch], x_recv.at[i, ch],
-            me, 2 * chip(far[i]) + k,
-        )
-
-    def stage1(ch):
-        rows = chunk_rows(ch)
-        part = slots[rows, :]
-        for i, dx in enumerate(far + (0,)):
-            base = 2 * chip(dx)
-
-            def block(t):
-                start = pl.multiple_of(t * FF_DEV, FF_DEV)
-                return dot_nt(part, down[pl.ds(start, FF_DEV), :]).astype(jnp.bfloat16)
-
-            sib_out[i, rows, :] = block(base + 1 - k)
-            sib_copy(i, ch).start()
-            own[i, rows, :] = block(base + k)
-
-    def joined(i, ch):
-        rows = chunk_rows(ch)
-        sib_copy(i, ch).wait_recv()
-        return own[i, rows, :].astype(jnp.float32) + sib_in[i, rows, :].astype(jnp.float32)
-
-    def stage2(ch):
-        rows = chunk_rows(ch)
-        for i in range(3):
-            x_out[i, rows, :] = joined(i, ch).astype(jnp.bfloat16)
-            x_copy(i, ch).start()
-
-    def rt_copy(j, ch):
-        return remote(rt_out.at[ch], rt_in.at[me], r_send.at[j], r_recv.at[me], j, tp)
-
-    def stage3(ch):
-        rows = chunk_rows(ch)
-        total = joined(3, ch)
-        for i in range(3):
-            x_copy(i, ch).wait_recv()
-            total = total + x_in[i, rows, :].astype(jnp.float32)
-        hid[tp, rows, :] = total.astype(jnp.bfloat16)
-        hid_x[0](ch)
-        term = jnp.sum(total * prod_buf[rows, :], axis=1, keepdims=True)
-        rt_out[ch] = mm(owner_is, (term * spot_is).astype(jnp.bfloat16))
-        for i in range(N_Z):
-            j = rows_by_chunk[ch] * N_Z + i
-
-            @pl.when(j != me)
-            def _():
-                rt_copy(j, ch).start()
-
-        if ch == 0:
-            rt_in[me] = rt_out[0]
-
-    def product(t, p):
-        rows = pair_rows(p)
-        cols = pl.ds(pl.multiple_of(t * FF_DEV, FF_DEV), FF_DEV)
-        val = hid[t, rows, :].astype(jnp.float32)
-        grad_gate = (val * gu[t, rows, 0:FF_DEV].astype(jnp.float32)).astype(jnp.bfloat16)
-        grad_up = (val * gu[t, rows, FF_DEV : 2 * FF_DEV].astype(jnp.float32)).astype(jnp.bfloat16)
-        return dot_nt(grad_gate, wg[:, cols]) + dot_nt(grad_up, wu[:, cols])
-
-    def back_copy(j):
-        return remote(back.at[j], ret.at[me], b_send.at[j], b_recv.at[me], j, tp)
-
-    def near_products(p):
-        acc[p] = product(tp, p)
-        for i in range(2):
-            acc[p] += product(source(i), p)
-
-    def far_products(p):
-        acc[p] += product(opposite, p)
-        for i in (3, 0, 1, 2):
-            for ch in (2 * p, 2 * p + 1):
-                hid_x[3](i, ch)
-            acc[p] += product(shared(i), p)
-
-    def give_back(p):
-        for i in range(2 * N_Z):
-            j = pair_first(p) * N_Z + i
-            back[j] = acc[p, i * CAP : (i + 1) * CAP, :].astype(jnp.bfloat16)
-
-            @pl.when(j != me)
-            def _():
-                back_copy(j).start()
-
-    for ch in range(2):
-        dispatch_row(ch)
-    for ch in range(N_Y):
-        gu_x[0](ch)
-    for ch in range(2, N_Y):
-        dispatch_row(ch)
     w_copies[0].wait()
     arrive(0)
     stage1(0)
-    gu_x[1](0)
     arrive(1)
     stage1(1)
     stage2(0)
-    gu_x[1](1)
     arrive(2)
     stage1(2)
     stage2(1)
-    gu_x[1](2)
     arrive(3)
+    stage1(3)
+    stage2(2)
+    stage2(3)
+    send_keys()
     for i in range(1, N_Y):
         q_copy(i, y).start()
-    send_keys()
-    stage1(3)
-    stage2(2)
-    gu_x[1](3)
-    stage2(3)
-    for ch in range(N_Y):
-        gu_x[2](ch)
-    for ch in range(N_Y):
-        stage3(ch)
-    for ch in range(N_Y):
-        for i in range(4):
-            gu_x[3](i, ch)
+    ring_step(1)
+    row_step(0)
+    stage3(0)
+    ring_step(2)
+    stage3(1)
+    row_step(1)
+    row_step(2)
+    stage3(2)
+    stage3(3)
+    ring_step(3)
+    turn_queries()
     w_copies[1].wait()
     w_copies[2].wait()
     hid_x[1](0)
     hid_x[1](1)
     near_products(0)
+    hid_x[1](2)
+    hid_x[1](3)
     hid_x[2](0)
     hid_x[2](1)
-    hid_x[1](2)
-    hid_x[1](3)
+    ring_step(4)
     far_products(0)
     give_back(0)
     near_products(1)
+    row_step(3)
     hid_x[2](2)
     hid_x[2](3)
     far_products(1)
     give_back(1)
+    row_step(4)
+    row_step(5)
+    row_step(6)
     ret[me] = back[me]
-    turn_queries()
+    row_step(7)
     get_keys()
 
     for j in range(N_CTX):
@@ -903,7 +991,9 @@
         t = sibling if i == 3 else full_chip(i) + 1 - 2 * k
         full_share(t, i).wait_recv()
     full_ref[...] = full[...]
-
+    ring_last()
+
+    ring_drain()
     def drain_ctx(i, carry):
         j = (me + i) % N_CTX
         dispatch(j).wait_send()
@@ -922,7 +1012,6 @@
             sib_copy(i, ch).wait_send()
         for i in range(3):
             x_copy(i, ch).wait_send()
-        gu_x[4](ch)
         hid_x[4](ch)
     for i in range(1, N_Y):
         q_copy(i, y).wait_send()
@@ -938,7 +1027,7 @@
         full_share(tp, i).wait_send()
 
 
-def expert_block(pack, hidden, grad, queries, keys, values, down, gate, up, wg, wu):
+def expert_block(pack, hidden, grad, queries, keys, values, down, gate, up, wg, wu, w_out_t):
     bf, f32 = jnp.bfloat16, jnp.float32
     vmem = pl.BlockSpec(memory_space=pltpu.VMEM)
     hbm = pl.BlockSpec(memory_space=pl.ANY)
@@ -953,9 +1042,10 @@
             jax.ShapeDtypeStruct((N_Y, ROWS_Q, HD), bf),
             jax.ShapeDtypeStruct((N_Y, HD, ROWS_Q), bf),
             jax.ShapeDtypeStruct((N_Y, 2, 2, BLOCK, HD), bf),
+            jax.ShapeDtypeStruct((D, ROWS_Q), bf),
         ],
-        in_specs=[vmem] * 6 + [hbm, vmem, vmem, hbm, hbm],
-        out_specs=[vmem] * 6,
+        in_specs=[vmem] * 6 + [hbm, vmem, vmem, hbm, hbm, hbm],
+        out_specs=[vmem] * 6 + [hbm],
         scratch_shapes=[
             pltpu.VMEM((FF_GRP, FEAT), bf),
             pltpu.VMEM((FEAT, FF_GRP), bf),
@@ -970,8 +1060,9 @@
             pltpu.VMEM((3, SLOTS, FF_DEV), bf),
             pltpu.VMEM((3, SLOTS, FF_DEV), bf),
             pltpu.VMEM((SLOTS, FF_DEV), f32),
+            pltpu.VMEM((SLOTS, FF_DEV), f32),
+            pltpu.VMEM((SLOTS, FF_DEV), f32),
             pltpu.VMEM((N_TP, SLOTS, 2 * FF_DEV), bf),
-            pltpu.VMEM((N_TP, SLOTS, FF_DEV), bf),
             pltpu.VMEM((2, PAIR_ROWS, FEAT), f32),
             pltpu.VMEM((N_CTX, CAP, FEAT), bf),
             pltpu.VMEM((N_CTX, CAP, FEAT), bf),
@@ -993,9 +1084,6 @@
             dma((2, N_Y)), dma((2, N_Y)),
             dma((2, N_Y)), dma((2, N_Y)),
             dma((4, N_Y)), dma((4, N_Y)),
-            dma((2, N_Y)), dma((2, N_Y)),
-            dma((2, N_Y)), dma((2, N_Y)),
-            dma((4, N_Y)), dma((4, N_Y)),
             dma((N_CTX,)), dma((N_CTX,)),
             dma((N_TP,)), dma((N_TP,)),
             dma((3,)), dma((3,)),
@@ -1003,6 +1091,10 @@
             dma((N_Y,)), dma((N_Y,)),
             dma((N_Z,)), dma((N_Y, 2)),
             dma((N_CTX,)), dma((N_CTX,)),
+            dma((2, N_Z // 2)), dma((2, N_Z // 2)),
+            dma((2, N_Z)), dma((2, N_Z)),
+            dma((2, N_Z)), dma((2, N_Z)),
+            dma,
         ],
         cost_estimate=pl.CostEstimate(
             flops=60_000_000_000, bytes_accessed=200_000_000, transcendentals=3_000_000
@@ -1010,7 +1102,7 @@
         compiler_params=pltpu.CompilerParams(
             collective_id=3, has_side_effects=True, vmem_limit_bytes=56 * 2**20
         ),
-    )(pack, hidden, grad, queries, keys, values, down, gate, up, wg, wu)
+    )(pack, hidden, grad, queries, keys, values, down, gate, up, wg, wu, w_out_t)
 
 
 def body(
@@ -1029,7 +1121,6 @@
     keys,
     values,
 ):
-    gathered = lax.all_gather(w_out.T, "ctx", axis=0, tiled=True)
     pack = jnp.concatenate(
         [
             expert_ids.reshape(1, BLOCK).astype(jnp.float32),
@@ -1039,7 +1130,7 @@
         ],
         axis=0,
     )
-    d_hidden, stats, full_grad, q5, qt, kv = expert_block(
+    d_hidden, stats, full_grad, q5, qt, kv, gathered = expert_block(
         pack,
         hidden_in,
         out_grad,
@@ -1051,6 +1142,7 @@
         up_saved[0],
         w_gate[0],
         w_up[0],
+        w_out.T,
     )
     router_grad = stats[0]
     grads = attention(full_grad, q5, qt, kv, gathered)

time: 191 us -> 179 us (0.937)
  between operations: 14 us -> 0.65 us
  Pallas kernels: 165 us -> 168 us
    pallas_call x1, Pallas kernels: 123 us -> 127 us  [expert_block(): pl.pallas_call(expert_kernel, name='expert_block', out_shape=[jax.ShapeDt...]
  transfers between devices with their start and end apart: 1 -> 0, of which waited for: 0 -> 0; matrix products, arithmetic and copies ran while one was open for 2% -> 0% of each run, Pallas kernels for 66% -> 0%
where the time goes in v5:
time: 179 us; the launch traced here: 176 us
  Pallas kernels  168 us (94%)
  local copies, waits for them, and re-layouts  4.93 us (3%)
  other arithmetic  2.66 us (1%)
    pallas_call x1, Pallas kernels, expert_block(): pl.pallas_call(expert_kernel, name='expert_block', out_shape=[jax.ShapeDt...  127 us
    pallas_call x1, Pallas kernels, attention(): pl.pallas_call(attention_kernel, name='attention_grads', out_shape=jax.Sh...  41.4 us

profile of v5, /device:TPU:88, one launch (start us, length us, event | category | flops | bytes accessed | tf_op | source)
XLA Modules:
  0.0 176.5 jit_solution(14424897057862934414)
XLA Ops:
  0.6 0.7 bitcast_convert_fusion.1
  1.3 0.7 convert_bitcast_fusion
  1.9 0.1 pad.3.clone
  2.0 0.7 bitcast_convert_fusion
  2.7 0.7 maximum_maximum_fusion.pack_ref
  3.4 126.8 %expert_block.1 = (bf16[128,640]{1,0:T(8,128)(2,1)}, f32[8,128]{1,0:T(8,128)}, bf16[8,128,640]{2,1,0:T(8,128)(2,1)}, bf16[4,640,128]{2,1,0:T(8,128)(2,1)}, bf16[...) custom-call(f32[8,128]{1,0:T(8,128)} %maximum_maximum_fusion.pack_ref, ...), custom_call_target="tpu_custom_call" | custom-call | flops 60000002048 | bytes 200000000 | tf_op jit(solution)/shard_map/expert_block/pallas_call | solution.py:1035
  130.2 1.2 slice_bitcast_fusion
  131.4 0.0 copy-start
  131.4 41.4 %attention_grads.1 = bf16[128,896]{1,0:T(8,128)(2,1)} custom-call(bf16[8,128,640]{2,1,0:T(8,128)(2,1)} %get-tuple-element.14.full_ref, bf16[4,640,128]{2,1,0:T(8,128)(2,1)} %get-tuple-element.15.q5_ref, bf16[4,128,640]{2,1,0:T(8,128)(2,1)} %get-tuple-element.16.qt_ref, bf16[4,2,2,128,128]{4,3,2,1,0:T(8,128)(2,1)} %get-tuple-element.17.kv_ref, ...), custom_call_target="tpu_custom_call" | custom-call | flops 6000000000 | bytes 12000000 | tf_op jit(solution)/shard_map/attention_grads/pallas_call | solution.py:354
  172.8 1.4 fusion
  174.2 1.6 slice.13
  175.8 0.0 copy-done
  175.8 0.7 copy.20
Async XLA Ops:
  131.4 44.5 %copy-start = (bf16[128,640]{1,0:T(8,128)(2,1)S(1)}, bf16[128,640]{1,0:T(8,128)(2,1)}, u32[]{:S(2)}) copy-start(bf16[128,640]{1,0:T(8,128)(2,1)} %get-tuple-element.26) | copy-start | bytes 491524
